TPU v7x, 512 devices: a whole 4x4x16 slice. The times are simulated.
512 devices in a mesh: tm: 8 (over y_lo, x), rows: 64 (over z, y_hi, core).
Axes of the slice: x: 4, y: 4 (y_hi: 2, y_lo: 2; y = y_hi * 2 + y_lo), z: 16, core: 2. Of those that a mesh axis runs over, the one named last changes fastest.
Arguments:
- frames_in: bfloat16 [16, 128, 512, 128], P('tm', 'rows'), may hold values from -6 to 6
- temporal_weight: bfloat16 [3, 3, 3, 128, 128], replicated, may hold values from -0.109375 to 0.109375
- first_weight: bfloat16 [3, 3, 128, 128], replicated, may hold values from -0.1875 to 0.1875
- second_weight: bfloat16 [3, 3, 128, 128], replicated, may hold values from -0.1875 to 0.1875
Outputs:
- encoded: bfloat16 [8, 128, 512, 128], P(None, 'rows', 'tm')
All inputs are finite; a program needn't handle non-finite values.
Results may differ from a plain program's by a relative error of at most 0.0052.
Values may be sent and summed in bfloat16 or wider, within the bound.
No kernel may reach another device: no remote copies, remote signals or barrier semaphores. Data moves between devices by JAX's collectives and lax.ppermute only.
A program may use at most 64 MiB of HBM per device.

v0:
```python
import jax
import jax.numpy as jnp
from jax import lax
from jax.sharding import PartitionSpec as P


def extended_2(shard, sides, width):
    for axis, dim in sides:
        peers, length = (lax.axis_size(axis), shard.shape[dim])
        up = [(i, (i + 1) % peers) for i in range(peers - 1)]
        down = [(j, i) for i, j in up]
        last = lax.slice_in_dim(shard, length - width, length, axis=dim)
        initial = lax.slice_in_dim(shard, 0, width, axis=dim)
        before = lax.ppermute(last, axis, up)
        after = lax.ppermute(initial, axis, down)
        shard = jnp.concatenate([before, shard, after], axis=dim)
    return shard


def from_behind(value, axis, steps):
    count = lax.axis_size(axis)
    initial, last = (max(0, -steps), min(count, count - steps))
    return lax.ppermute(value, axis, [(source, source + steps) for source in range(initial, last)])


def temporal_taps(padded, weight, out_frames, row_count, col_count):
    chans = padded.shape[-1]
    summed = jnp.zeros((out_frames, row_count, col_count, weight.shape[-1]), jnp.float32)
    for tap_frame in range(3):
        for tap_row in range(3):
            for tap_col in range(3):
                sliced = lax.slice(
                    padded,
                    (tap_frame, tap_row, tap_col, 0),
                    (
                        tap_frame + 2 * out_frames - 1,
                        tap_row + row_count,
                        tap_col + col_count,
                        chans,
                    ),
                    (2, 1, 1, 1),
                )
                summed = summed + jnp.einsum(
                    "trwc,cd->trwd",
                    sliced,
                    weight[tap_frame, tap_row, tap_col],
                    preferred_element_type=jnp.float32,
                )
    return summed


def plane_conv(padded, weight, row_count, col_count):
    summed = jnp.zeros((padded.shape[0], row_count, col_count, weight.shape[-1]), jnp.float32)
    for tap_row in range(3):
        for tap_col in range(3):
            sliced = padded[:, tap_row : tap_row + row_count, tap_col : tap_col + col_count]
            summed = summed + jnp.einsum(
                "trwc,cd->trwd",
                sliced,
                weight[tap_row, tap_col],
                preferred_element_type=jnp.float32,
            )
    return summed


def rim_once(field):
    return extended_2(field, (("tm", 2), ("rows", 1)), 1)


def per_device(frames_in, temporal_weight, first_weight, second_weight):
    frame_count, row_count, col_count, chans = frames_in.shape
    out_frames = frame_count // 2
    prior_frame = from_behind(frames_in[frame_count - 1 :], "tm", 1)
    extended = jnp.concatenate([prior_frame, frames_in], axis=0)
    rimmed = extended_2(extended, (("rows", 1),), 1)
    padded = jnp.pad(rimmed, ((0, 0), (0, 0), (1, 1), (0, 0)))
    summed = temporal_taps(padded, temporal_weight, out_frames, row_count, col_count)
    temporal = summed.astype(jnp.bfloat16)
    columns = lax.all_to_all(temporal, "tm", split_axis=2, concat_axis=0, tiled=True)
    col_local = columns.shape[2]
    first_rims = rim_once(columns)
    hidden = jax.nn.silu(plane_conv(first_rims, first_weight, row_count, col_local)).astype(
        jnp.bfloat16
    )
    second_rims = rim_once(hidden)
    mixed_out = plane_conv(second_rims, second_weight, row_count, col_local)
    return (columns.astype(jnp.float32) + mixed_out).astype(jnp.bfloat16)


def solution(mesh):
    placed = (P("tm", "rows", None, None), P(), P(), P())
    return jax.shard_map(
        per_device,
        mesh=mesh,
        in_specs=placed,
        out_specs=P(None, "rows", "tm", None),
        check_vma=False,
    )
```

profile of v0, /device:TPU:247, one launch (start us, length us, event | category | flops | bytes accessed | tf_op | source)
XLA Modules:
  0.0 96.8 jit_solution(7616087878525762403)
XLA Ops:
  0.0 1.0 %slice.356 = bf16[1,2,512,128]{3,2,1,0:T(8,128)(2,1)S(1)} slice(bf16[2,2,512,128]{3,2,1,0:T(8,128)(2,1)} %param.4), slice={[1:2], [0:2], [0:512], [0:128]} | slice | bytes 524288 | tf_op jit(solution)/shard_map/slice | solution.py:73
  1.0 2.8 %collective-permute-start = (bf16[1,2,512,128]{3,2,1,0:T(8,128)(2,1)S(1)}, bf16[1,2,512,128]{3,2,1,0:T(8,128)(2,1)S(1)}, u32[]{:S(2)}, u32[]{:S(2)}) collective-permute-start(bf16[1,2,512,128]{3,2,1,0:T(8,128)(2,1)S(1)} %slice.356), channel_id=1, source_target_pairs={{0,64},{64,128},{128,192},{192,256},{256,320},{320,384},{384,448},... | collective-permute-start | bytes 786440 | tf_op jit(solution)/shard_map/ppermute | solution.py:23
  3.9 1.2 %fusion.97 = f32[2,512,128]{2,1,0:T(8,128)S(1)} fusion(bf16[3,3,3,128,128]{4,3,2,1,0:T(8,128)(2,1)} %param.5, bf16[2,2,512,128]{3,2,1,0:T(8,128)(2,1)} %param.4), kind=kOutput, calls=%fused_computation.139 | convolution fusion | flops 33554432 | bytes 819200 | tf_op jit(solution)/shard_map/trwc,cd->trwd/dot_general | solution.py:43
  5.1 5.1 %collective-permute-done = bf16[1,2,512,128]{3,2,1,0:T(8,128)(2,1)S(1)} collective-permute-done((bf16[1,2,512,128]{3,2,1,0:T(8,128)(2,1)S(1)}, bf16[1,2,512,128]{3,2,1,0:T(8,128)(2,1)S(1)}, u32[]{:S(2)}, u32[]{:S(2)}) %collective-permute-start) | collective-permute-done | bytes 262176 | tf_op jit(solution)/shard_map/ppermute | solution.py:23
  10.3 6.0 %collective-permute-start.1 = (bf16[3,1,512,128]{3,2,1,0:T(8,128)(2,1)S(1)}, bf16[3,1,512,128]{3,2,1,0:T(8,128)(2,1)S(1)}, u32[]{:S(2)}, u32[]{:S(2)}) collective-permute-start(bf16[3,1,512,128]{3,2,1,0:T(8,128)(2,1)S(1)} %get-tuple-element.5), channel_id=1, source_target_pairs={{0,1},{1,2},{2,3},{3,4},{4,5},{5,6},{6,7},{7,8},{8,9},{9,10},{10,1... | collective-permute-start | bytes 1179656 | tf_op jit(solution)/shard_map/ppermute | solution.py:14
  16.3 1.9 %collective-permute-start.2 = (bf16[3,1,512,128]{3,2,1,0:T(8,128)(2,1)S(1)}, bf16[3,1,512,128]{3,2,1,0:T(8,128)(2,1)S(1)}, u32[]{:S(2)}, u32[]{:S(2)}) collective-permute-start(bf16[3,1,512,128]{3,2,1,0:T(8,128)(2,1)S(1)} %get-tuple-element.6), channel_id=1, source_target_pairs={{1,0},{2,1},{3,2},{4,3},{5,4},{6,5},{7,6},{8,7},{9,8},{10,9},{11,1... | collective-permute-start | bytes 1179656 | tf_op jit(solution)/shard_map/ppermute | solution.py:15
  18.6 2.3 %collective-permute-done.1 = bf16[3,1,512,128]{3,2,1,0:T(8,128)(2,1)S(1)} collective-permute-done((bf16[3,1,512,128]{3,2,1,0:T(8,128)(2,1)S(1)}, bf16[3,1,512,128]{3,2,1,0:T(8,128)(2,1)S(1)}, u32[]{:S(2)}, u32[]{:S(2)}) %collective-permute-start.1) | collective-permute-done | bytes 393248 | tf_op jit(solution)/shard_map/ppermute | solution.py:14
  21.0 8.0 %collective-permute-done.2 = bf16[3,1,512,128]{3,2,1,0:T(8,128)(2,1)S(1)} collective-permute-done((bf16[3,1,512,128]{3,2,1,0:T(8,128)(2,1)S(1)}, bf16[3,1,512,128]{3,2,1,0:T(8,128)(2,1)S(1)}, u32[]{:S(2)}, u32[]{:S(2)}) %collective-permute-start.2) | collective-permute-done | bytes 393248 | tf_op jit(solution)/shard_map/ppermute | solution.py:15
  29.0 0.4 fusion.5
  33.9 0.6 fusion.13
  35.3 9.9 %all_to_all.18 = bf16[1,2,512,128]{3,1,0,2:T(2,128)(2,1)S(1)} all-to-all(bf16[1,2,512,128]{3,1,0,2:T(2,128)(2,1)S(1)} %copy.7), channel_id=1, replica_groups=mesh['tm'=8,'rows'=64] {'tm'}, dimensions={2} | all-to-all | bytes 524288 | tf_op jit(solution)/shard_map/all_to_all | solution.py:79
  45.3 3.8 %collective-permute-start.3 = (bf16[8,2,1,128]{3,2,1,0:T(2,128)(2,1)S(1)}, bf16[8,2,1,128]{3,2,1,0:T(2,128)(2,1)S(1)}, u32[]{:S(2)}, u32[]{:S(2)}) collective-permute-start(bf16[8,2,1,128]{3,2,1,0:T(2,128)(2,1)S(1)} %get-tuple-element.17), channel_id=1, source_target_pairs={{0,64},{64,128},{128,192},{192,256},{256,320},{320,384},{384,448},... | collective-permute-start | bytes 12296 | tf_op jit(solution)/shard_map/ppermute | solution.py:14
  49.1 1.9 %collective-permute-start.4 = (bf16[8,2,1,128]{3,2,1,0:T(2,128)(2,1)S(1)}, bf16[8,2,1,128]{3,2,1,0:T(2,128)(2,1)S(1)}, u32[]{:S(2)}, u32[]{:S(2)}) collective-permute-start(bf16[8,2,1,128]{3,2,1,0:T(2,128)(2,1)S(1)} %get-tuple-element.18), channel_id=1, source_target_pairs={{64,0},{128,64},{192,128},{256,192},{320,256},{384,320},{448,384},... | collective-permute-start | bytes 12296 | tf_op jit(solution)/shard_map/ppermute | solution.py:15
  51.2 4.4 %collective-permute-done.4 = bf16[8,2,1,128]{3,2,1,0:T(2,128)(2,1)S(1)} collective-permute-done((bf16[8,2,1,128]{3,2,1,0:T(2,128)(2,1)S(1)}, bf16[8,2,1,128]{3,2,1,0:T(2,128)(2,1)S(1)}, u32[]{:S(2)}, u32[]{:S(2)}) %collective-permute-start.4) | collective-permute-done | bytes 4128 | tf_op jit(solution)/shard_map/ppermute | solution.py:15
  55.8 4.9 %collective-permute-start.5 = (bf16[8,1,66,128]{3,2,1,0:T(8,128)(2,1)S(1)}, bf16[8,1,66,128]{3,2,1,0:T(8,128)(2,1)S(1)}, u32[]{:S(2)}, u32[]{:S(2)}) collective-permute-start(bf16[8,1,66,128]{3,2,1,0:T(8,128)(2,1)S(1)} %get-tuple-element.9), channel_id=1, source_target_pairs={{0,1},{1,2},{2,3},{3,4},{4,5},{5,6},{6,7},{7,8},{8,9},{9,10},{10,1... | collective-permute-start | bytes 405512 | tf_op jit(solution)/shard_map/ppermute | solution.py:14
  60.7 1.9 %collective-permute-start.6 = (bf16[8,1,66,128]{3,2,1,0:T(8,128)(2,1)S(1)}, bf16[8,1,66,128]{3,2,1,0:T(8,128)(2,1)S(1)}, u32[]{:S(2)}, u32[]{:S(2)}) collective-permute-start(bf16[8,1,66,128]{3,2,1,0:T(8,128)(2,1)S(1)} %get-tuple-element.10), channel_id=1, source_target_pairs={{1,0},{2,1},{3,2},{4,3},{5,4},{6,5},{7,6},{8,7},{9,8},{10,9},{11,1... | collective-permute-start | bytes 405512 | tf_op jit(solution)/shard_map/ppermute | solution.py:15
  62.9 7.9 %collective-permute-done.6 = bf16[8,1,66,128]{3,2,1,0:T(8,128)(2,1)S(1)} collective-permute-done((bf16[8,1,66,128]{3,2,1,0:T(8,128)(2,1)S(1)}, bf16[8,1,66,128]{3,2,1,0:T(8,128)(2,1)S(1)}, u32[]{:S(2)}, u32[]{:S(2)}) %collective-permute-start.6) | collective-permute-done | bytes 135200 | tf_op jit(solution)/shard_map/ppermute | solution.py:15
  72.7 2.0 %collective-permute-start.7 = (bf16[8,2,1,128]{3,2,1,0:T(2,128)(2,1)S(1)}, bf16[8,2,1,128]{3,2,1,0:T(2,128)(2,1)S(1)}, u32[]{:S(2)}, u32[]{:S(2)}) collective-permute-start(bf16[8,2,1,128]{3,2,1,0:T(2,128)(2,1)S(1)} %get-tuple-element.15), channel_id=1, source_target_pairs={{0,64},{64,128},{128,192},{192,256},{256,320},{320,384},{384,448},... | collective-permute-start | bytes 12296 | tf_op jit(solution)/shard_map/ppermute | solution.py:14
  74.7 3.3 %collective-permute-start.8 = (bf16[8,2,1,128]{3,2,1,0:T(2,128)(2,1)S(1)}, bf16[8,2,1,128]{3,2,1,0:T(2,128)(2,1)S(1)}, u32[]{:S(2)}, u32[]{:S(2)}) collective-permute-start(bf16[8,2,1,128]{3,2,1,0:T(2,128)(2,1)S(1)} %get-tuple-element.16), channel_id=1, source_target_pairs={{64,0},{128,64},{192,128},{256,192},{320,256},{384,320},{448,384},... | collective-permute-start | bytes 12296 | tf_op jit(solution)/shard_map/ppermute | solution.py:15
  78.2 3.1 %collective-permute-done.8 = bf16[8,2,1,128]{3,2,1,0:T(2,128)(2,1)S(1)} collective-permute-done((bf16[8,2,1,128]{3,2,1,0:T(2,128)(2,1)S(1)}, bf16[8,2,1,128]{3,2,1,0:T(2,128)(2,1)S(1)}, u32[]{:S(2)}, u32[]{:S(2)}) %collective-permute-start.8) | collective-permute-done | bytes 4128 | tf_op jit(solution)/shard_map/ppermute | solution.py:15
  81.4 2.8 %collective-permute-start.9 = (bf16[8,1,66,128]{3,2,1,0:T(8,128)(2,1)S(1)}, bf16[8,1,66,128]{3,2,1,0:T(8,128)(2,1)S(1)}, u32[]{:S(2)}, u32[]{:S(2)}) collective-permute-start(bf16[8,1,66,128]{3,2,1,0:T(8,128)(2,1)S(1)} %get-tuple-element.7), channel_id=1, source_target_pairs={{0,1},{1,2},{2,3},{3,4},{4,5},{5,6},{6,7},{7,8},{8,9},{9,10},{10,1... | collective-permute-start | bytes 405512 | tf_op jit(solution)/shard_map/ppermute | solution.py:14
  84.2 1.9 %collective-permute-start.10 = (bf16[8,1,66,128]{3,2,1,0:T(8,128)(2,1)S(1)}, bf16[8,1,66,128]{3,2,1,0:T(8,128)(2,1)S(1)}, u32[]{:S(2)}, u32[]{:S(2)}) collective-permute-start(bf16[8,1,66,128]{3,2,1,0:T(8,128)(2,1)S(1)} %get-tuple-element.8), channel_id=1, source_target_pairs={{1,0},{2,1},{3,2},{4,3},{5,4},{6,5},{7,6},{8,7},{9,8},{10,9},{11,1... | collective-permute-start | bytes 405512 | tf_op jit(solution)/shard_map/ppermute | solution.py:15
  86.4 7.9 %collective-permute-done.10 = bf16[8,1,66,128]{3,2,1,0:T(8,128)(2,1)S(1)} collective-permute-done((bf16[8,1,66,128]{3,2,1,0:T(8,128)(2,1)S(1)}, bf16[8,1,66,128]{3,2,1,0:T(8,128)(2,1)S(1)}, u32[]{:S(2)}, u32[]{:S(2)}) %collective-permute-start.10) | collective-permute-done | bytes 135200 | tf_op jit(solution)/shard_map/ppermute | solution.py:15
  95.8 1.0 %fusion.31 = bf16[8,2,64,128]{3,2,1,0:T(8,128)(2,1)} fusion(f32[8,2,64,128]{3,2,1,0:T(8,128)S(1)} %fusion.33, f32[8,2,64,128]{3,2,1,0:T(8,128)S(1)} %fusion.35, f32[8,2,64,128]{3,2,1,0:T(8,128)S(1)} %fusion.37, f32[8,2,64,128]{3,2,1,0:T(8,128)S(1)} %fusion.25, bf16[8,2,1,128]{3,2,1,0:T(2,128)(2,1)S(1)} %collective-permute-done.8, ...), kind=kOutput, calls=%fused_computation.39 | convolution fusion | flops 34996224 | bytes 2924544 | tf_op jit(solution)/shard_map/trwc,cd->trwd/dot_general | solution.py:57
  (67 shorter events, 10.2 us)
Async XLA Ops:
  0.0 10.1 %copy-start = (bf16[2,2,512,128]{3,2,1,0:T(8,128)(2,1)S(1)}, bf16[2,2,512,128]{3,2,1,0:T(8,128)(2,1)}, u32[]{:S(2)}) copy-start(bf16[2,2,512,128]{3,2,1,0:T(8,128)(2,1)} %param.4) | copy-start | bytes 1572868
  1.0 9.1 %collective-permute-start = (bf16[1,2,512,128]{3,2,1,0:T(8,128)(2,1)S(1)}, bf16[1,2,512,128]{3,2,1,0:T(8,128)(2,1)S(1)}, u32[]{:S(2)}, u32[]{:S(2)}) collective-permute-start(bf16[1,2,512,128]{3,2,1,0:T(8,128)(2,1)S(1)} %slice.356), channel_id=1, source_target_pairs={{0,64},{64,128},{128,192},{192,256},{256,320},{320,384},{384,448},... | collective-permute-start | bytes 786440 | tf_op jit(solution)/shard_map/ppermute | solution.py:23
  5.0 13.1 %copy-start.1 = (bf16[3,3,3,128,128]{4,3,2,1,0:T(8,128)(2,1)S(1)}, bf16[3,3,3,128,128]{4,3,2,1,0:T(8,128)(2,1)}, u32[]{:S(2)}) copy-start(bf16[3,3,3,128,128]{4,3,2,1,0:T(8,128)(2,1)} %param.5) | copy-start | bytes 2654212
  10.3 10.7 %collective-permute-start.1 = (bf16[3,1,512,128]{3,2,1,0:T(8,128)(2,1)S(1)}, bf16[3,1,512,128]{3,2,1,0:T(8,128)(2,1)S(1)}, u32[]{:S(2)}, u32[]{:S(2)}) collective-permute-start(bf16[3,1,512,128]{3,2,1,0:T(8,128)(2,1)S(1)} %get-tuple-element.5), channel_id=1, source_target_pairs={{0,1},{1,2},{2,3},{3,4},{4,5},{5,6},{6,7},{7,8},{8,9},{9,10},{10,1... | collective-permute-start | bytes 1179656 | tf_op jit(solution)/shard_map/ppermute | solution.py:14
  16.3 12.7 %collective-permute-start.2 = (bf16[3,1,512,128]{3,2,1,0:T(8,128)(2,1)S(1)}, bf16[3,1,512,128]{3,2,1,0:T(8,128)(2,1)S(1)}, u32[]{:S(2)}, u32[]{:S(2)}) collective-permute-start(bf16[3,1,512,128]{3,2,1,0:T(8,128)(2,1)S(1)} %get-tuple-element.6), channel_id=1, source_target_pairs={{1,0},{2,1},{3,2},{4,3},{5,4},{6,5},{7,6},{8,7},{9,8},{10,9},{11,1... | collective-permute-start | bytes 1179656 | tf_op jit(solution)/shard_map/ppermute | solution.py:15
  34.8 16.2 %copy-start.3 = (bf16[3,3,128,128]{3,2,1,0:T(8,128)(2,1)S(1)}, bf16[3,3,128,128]{3,2,1,0:T(8,128)(2,1)}, u32[]{:S(2)}) copy-start(bf16[3,3,128,128]{3,2,1,0:T(8,128)(2,1)} %param.6) | copy-start | bytes 884740
  45.3 5.9 %collective-permute-start.3 = (bf16[8,2,1,128]{3,2,1,0:T(2,128)(2,1)S(1)}, bf16[8,2,1,128]{3,2,1,0:T(2,128)(2,1)S(1)}, u32[]{:S(2)}, u32[]{:S(2)}) collective-permute-start(bf16[8,2,1,128]{3,2,1,0:T(2,128)(2,1)S(1)} %get-tuple-element.17), channel_id=1, source_target_pairs={{0,64},{64,128},{128,192},{192,256},{256,320},{320,384},{384,448},... | collective-permute-start | bytes 12296 | tf_op jit(solution)/shard_map/ppermute | solution.py:14
  49.1 6.6 %collective-permute-start.4 = (bf16[8,2,1,128]{3,2,1,0:T(2,128)(2,1)S(1)}, bf16[8,2,1,128]{3,2,1,0:T(2,128)(2,1)S(1)}, u32[]{:S(2)}, u32[]{:S(2)}) collective-permute-start(bf16[8,2,1,128]{3,2,1,0:T(2,128)(2,1)S(1)} %get-tuple-element.18), channel_id=1, source_target_pairs={{64,0},{128,64},{192,128},{256,192},{320,256},{384,320},{448,384},... | collective-permute-start | bytes 12296 | tf_op jit(solution)/shard_map/ppermute | solution.py:15
  55.8 7.1 %collective-permute-start.5 = (bf16[8,1,66,128]{3,2,1,0:T(8,128)(2,1)S(1)}, bf16[8,1,66,128]{3,2,1,0:T(8,128)(2,1)S(1)}, u32[]{:S(2)}, u32[]{:S(2)}) collective-permute-start(bf16[8,1,66,128]{3,2,1,0:T(8,128)(2,1)S(1)} %get-tuple-element.9), channel_id=1, source_target_pairs={{0,1},{1,2},{2,3},{3,4},{4,5},{5,6},{6,7},{7,8},{8,9},{9,10},{10,1... | collective-permute-start | bytes 405512 | tf_op jit(solution)/shard_map/ppermute | solution.py:14
  60.7 10.1 %collective-permute-start.6 = (bf16[8,1,66,128]{3,2,1,0:T(8,128)(2,1)S(1)}, bf16[8,1,66,128]{3,2,1,0:T(8,128)(2,1)S(1)}, u32[]{:S(2)}, u32[]{:S(2)}) collective-permute-start(bf16[8,1,66,128]{3,2,1,0:T(8,128)(2,1)S(1)} %get-tuple-element.10), channel_id=1, source_target_pairs={{1,0},{2,1},{3,2},{4,3},{5,4},{6,5},{7,6},{8,7},{9,8},{10,9},{11,1... | collective-permute-start | bytes 405512 | tf_op jit(solution)/shard_map/ppermute | solution.py:15
  72.3 5.7 %copy-start.2 = (bf16[3,3,128,128]{3,2,1,0:T(8,128)(2,1)S(1)}, bf16[3,3,128,128]{3,2,1,0:T(8,128)(2,1)}, u32[]{:S(2)}) copy-start(bf16[3,3,128,128]{3,2,1,0:T(8,128)(2,1)} %param.7) | copy-start | bytes 884740
  72.7 5.5 %collective-permute-start.7 = (bf16[8,2,1,128]{3,2,1,0:T(2,128)(2,1)S(1)}, bf16[8,2,1,128]{3,2,1,0:T(2,128)(2,1)S(1)}, u32[]{:S(2)}, u32[]{:S(2)}) collective-permute-start(bf16[8,2,1,128]{3,2,1,0:T(2,128)(2,1)S(1)} %get-tuple-element.15), channel_id=1, source_target_pairs={{0,64},{64,128},{128,192},{192,256},{256,320},{320,384},{384,448},... | collective-permute-start | bytes 12296 | tf_op jit(solution)/shard_map/ppermute | solution.py:14
  74.7 6.6 %collective-permute-start.8 = (bf16[8,2,1,128]{3,2,1,0:T(2,128)(2,1)S(1)}, bf16[8,2,1,128]{3,2,1,0:T(2,128)(2,1)S(1)}, u32[]{:S(2)}, u32[]{:S(2)}) collective-permute-start(bf16[8,2,1,128]{3,2,1,0:T(2,128)(2,1)S(1)} %get-tuple-element.16), channel_id=1, source_target_pairs={{64,0},{128,64},{192,128},{256,192},{320,256},{384,320},{448,384},... | collective-permute-start | bytes 12296 | tf_op jit(solution)/shard_map/ppermute | solution.py:15
  81.4 5.0 %collective-permute-start.9 = (bf16[8,1,66,128]{3,2,1,0:T(8,128)(2,1)S(1)}, bf16[8,1,66,128]{3,2,1,0:T(8,128)(2,1)S(1)}, u32[]{:S(2)}, u32[]{:S(2)}) collective-permute-start(bf16[8,1,66,128]{3,2,1,0:T(8,128)(2,1)S(1)} %get-tuple-element.7), channel_id=1, source_target_pairs={{0,1},{1,2},{2,3},{3,4},{4,5},{5,6},{6,7},{7,8},{8,9},{9,10},{10,1... | collective-permute-start | bytes 405512 | tf_op jit(solution)/shard_map/ppermute | solution.py:14
  84.2 10.1 %collective-permute-start.10 = (bf16[8,1,66,128]{3,2,1,0:T(8,128)(2,1)S(1)}, bf16[8,1,66,128]{3,2,1,0:T(8,128)(2,1)S(1)}, u32[]{:S(2)}, u32[]{:S(2)}) collective-permute-start(bf16[8,1,66,128]{3,2,1,0:T(8,128)(2,1)S(1)} %get-tuple-element.8), channel_id=1, source_target_pairs={{1,0},{2,1},{3,2},{4,3},{5,4},{6,5},{7,6},{8,7},{9,8},{10,9},{11,1... | collective-permute-start | bytes 405512 | tf_op jit(solution)/shard_map/ppermute | solution.py:15
where the time goes:
time: 97.2 us; the launch traced here: 96.8 us
  waiting for transfers between devices  38.7 us (40%)
  starting transfers between devices  33.3 us (34%)
  matrix products  11.8 us (12%)
  blocking collectives  9.91 us (10%)
  local copies, waits for them, and re-layouts  1.6 us (2%)
    ppermute x5, waiting for transfers between devices, extended_2(): after = lax.ppermute(initial, axis, down)  31.3 us
    ppermute x5, starting transfers between devices, extended_2(): before = lax.ppermute(last, axis, up)  19.4 us
    ppermute x5, starting transfers between devices, extended_2(): after = lax.ppermute(initial, axis, down)  11 us
    all_to_all x1, blocking collectives, per_device(): lax.all_to_all(temporal, 'tm', split_axis=2, concat_axis=0, tiled=True)  9.91 us
    dot_general x27, matrix products, temporal_taps(): jnp.einsum('trwc,cd->trwd', sliced, weight[tap_frame, tap_row, tap_col],...  7.07 us
    ppermute x1, waiting for transfers between devices, from_behind(): lax.ppermute(value, axis, [(source, source + steps) for source in range(i...  5.06 us
    dot_general x18, matrix products, plane_conv(): jnp.einsum('trwc,cd->trwd', sliced, weight[tap_row, tap_col], preferred_e...  4.73 us
    ppermute x1, starting transfers between devices, from_behind(): lax.ppermute(value, axis, [(source, source + steps) for source in range(i...  2.83 us
  transfers between devices with their start and end apart: 11, of which 7 were waited for; matrix products, arithmetic and copies ran while one was open for 2% of the time, Pallas kernels for 0%

commit v1 on v0

v1 whole, which is shorter than its diff:
```python
import functools

import jax
import jax.numpy as jnp
from jax import lax
from jax.experimental import pallas as pl
from jax.experimental.pallas import tpu as pltpu
from jax.sharding import PartitionSpec as P

SLABS = 4
HALO = 4


def windows(frames, count, width):
    frame_count, row_count, col_count, chans = frames.shape
    padded = jnp.pad(frames, ((0, 0), (0, 0), (HALO, width - HALO), (0, 0)))
    body = padded[:, :, :col_count].reshape(frame_count, row_count, count, width, chans)
    tail = padded[:, :, width:].reshape(frame_count, row_count, count, width, chans)
    joined = jnp.concatenate([body, tail[:, :, :, : 2 * HALO]], axis=3)
    return jnp.transpose(joined, (2, 0, 1, 3, 4))


def conv_kernel(place, own, swap_a, swap_b, w_temporal, w_first, w_second, out, xs, ts, hs, wt, w1, w2):
    frames, rows, span, chans = own.shape[0], 8, own.shape[4], own.shape[5]
    pitch = frames * span
    even, first_col, first_row = place[0], place[1], place[2]
    last_col, last_row = place[3], place[4]

    for a in range(3):
        for b in range(3):
            for c in range(3):
                k = (a * 3 + b) * chans
                wt[k : k + chans, c * chans : (c + 1) * chans] = w_temporal[a, b, c]
    for b in range(3):
        for c in range(3):
            w1[b * chans : (b + 1) * chans, c * chans : (c + 1) * chans] = w_first[b, c]
            w2[b * chans : (b + 1) * chans, c * chans : (c + 1) * chans] = w_second[b, c]

    def put(row, pick):
        for t in range(0, frames, 2):
            at = row * pitch + t * span
            for a, f in ((1, 0), (2, 1)):
                pair = jnp.concatenate([pick(t, f), pick(t + 1, f)], axis=0)
                xs[a, at : at + 2 * span] = pair.astype(jnp.bfloat16)
            before = pick(t - 1, 1) if t else jnp.zeros((span, chans), jnp.float32)
            pair = jnp.concatenate([before, pick(t, 1)], axis=0)
            xs[0, at : at + 2 * span] = pair.astype(jnp.bfloat16)

    for row in range(rows):
        put(row + 3, lambda m, f: own[m, row // 2, f, row % 2].astype(jnp.float32))
    for row in range(3):
        def above(m, f):
            return jnp.where(even == 1, swap_b[m, f, row], swap_a[m, f, row]).astype(jnp.float32)

        def below(m, f):
            return jnp.where(even == 1, swap_a[m, f, row], swap_b[m, f, row]).astype(jnp.float32)

        put(row, above)
        put(row + 3 + rows, below)

    def taps(sum3):
        left, mid, right = sum3[:, :chans], sum3[:, chans : 2 * chans], sum3[:, 2 * chans :]
        return mid + pltpu.roll(left, 1, 0) + pltpu.roll(right, sum3.shape[0] - 1, 0)

    def inside(value, row):
        shape = (value.shape[0] // pitch, frames, span, chans)
        col = lax.broadcasted_iota(jnp.int32, shape, 2) + first_col
        r = lax.broadcasted_iota(jnp.int32, shape, 0) + (first_row + row)
        keep = (col >= 0) & (col < last_col) & (r >= 0) & (r < last_row)
        return jnp.where(keep, value.reshape(shape), 0.0).reshape(value.shape)

    step = 2
    block = step * pitch

    @pl.loop(0, (rows + 4) // step)
    def _(i):
        base = pl.multiple_of(i * block, block)
        lhs = jnp.concatenate(
            [xs[a, pl.ds(base + b * pitch, block)] for a in range(3) for b in range(3)], axis=1
        )
        sums = taps(jnp.dot(lhs, wt[...], preferred_element_type=jnp.float32))
        ts[pl.ds(base, block)] = inside(sums, i * step - 2).astype(jnp.bfloat16)

    @pl.loop(0, (rows + 2) // step)
    def _(i):
        base = pl.multiple_of(i * block, block)
        lhs = jnp.concatenate([ts[pl.ds(base + b * pitch, block)] for b in range(3)], axis=1)
        sums = taps(jnp.dot(lhs, w1[...], preferred_element_type=jnp.float32))
        active = sums / (1.0 + jnp.exp(-sums))
        hs[pl.ds(base, block)] = inside(active, i * step - 1).astype(jnp.bfloat16)

    @pl.loop(0, rows // step)
    def _(i):
        base = pl.multiple_of(i * block, block)
        lhs = jnp.concatenate([hs[pl.ds(base + b * pitch, block)] for b in range(3)], axis=1)
        sums = taps(jnp.dot(lhs, w2[...], preferred_element_type=jnp.float32))
        sums = sums + ts[pl.ds(base + 2 * pitch, block)].astype(jnp.float32)
        sums = sums.reshape(step, frames, span, chans)[:, :, HALO : span - HALO]
        for r in range(step):
            out[i, :, r] = sums[r].astype(jnp.bfloat16)


def per_device(frames_in, temporal_weight, first_weight, second_weight):
    tm, slabs = lax.axis_size("tm"), lax.axis_size("rows")
    planes = slabs // SLABS
    frame_count, row_count, col_count, chans = frames_in.shape
    windows_count = tm * SLABS
    width = col_count // windows_count
    span = width + 2 * HALO
    plane_rows = SLABS * row_count
    column, slab = lax.axis_index("tm"), lax.axis_index("rows")
    plane = slab // SLABS

    members = [[m * slabs + z * SLABS + j for m in range(tm) for j in range(SLABS)] for z in range(planes)]
    own = lax.all_to_all(
        windows(frames_in, windows_count, width),
        ("tm", "rows"),
        split_axis=0,
        concat_axis=0,
        tiled=True,
        axis_index_groups=members,
    ).reshape(tm, SLABS, frame_count, row_count, span, chans)

    bottom = jnp.concatenate([own[:, 2, :, 1:], own[:, 3]], axis=2)
    top = jnp.concatenate([own[:, 0], own[:, 1, :, :1]], axis=2)
    even = plane % 2 == 0

    def swap(parity):
        pairs = []
        for z in range(parity, planes - 1, 2):
            for j in range(SLABS):
                low, high = z * SLABS + j, (z + 1) * SLABS + j
                pairs += [(low, high), (high, low)]
        return pairs

    swap_a = lax.ppermute(jnp.where(even, bottom, top), "rows", swap(0))
    swap_b = lax.ppermute(jnp.where(even, top, bottom), "rows", swap(1))

    place = jnp.stack(
        [
            even.astype(jnp.int32),
            (column * SLABS + slab % SLABS) * width - HALO,
            plane * plane_rows,
            jnp.int32(col_count),
            jnp.int32(slabs * row_count),
        ]
    ).astype(jnp.int32)
    pitch = tm * span
    vmem = pl.BlockSpec(memory_space=pltpu.VMEM)
    encoded = pl.pallas_call(
        conv_kernel,
        out_shape=jax.ShapeDtypeStruct((SLABS, tm, row_count, width, chans), jnp.bfloat16),
        in_specs=[pl.BlockSpec(memory_space=pltpu.SMEM)] + [vmem] * 6,
        out_specs=vmem,
        scratch_shapes=[
            pltpu.VMEM((3, (plane_rows + 6) * pitch, chans), jnp.bfloat16),
            pltpu.VMEM(((plane_rows + 4) * pitch, chans), jnp.bfloat16),
            pltpu.VMEM(((plane_rows + 2) * pitch, chans), jnp.bfloat16),
            pltpu.VMEM((9 * chans, 3 * chans), jnp.bfloat16),
            pltpu.VMEM((3 * chans, 3 * chans), jnp.bfloat16),
            pltpu.VMEM((3 * chans, 3 * chans), jnp.bfloat16),
        ],
        compiler_params=pltpu.CompilerParams(vmem_limit_bytes=32 * 1024 * 1024),
        name="convs",
    )(place, own, swap_a, swap_b, temporal_weight, first_weight, second_weight)

    groups = [[z * SLABS + j for j in range(SLABS)] for z in range(planes)]
    encoded = lax.all_to_all(
        encoded, "rows", split_axis=0, concat_axis=0, tiled=True, axis_index_groups=groups
    )
    return jnp.transpose(encoded, (1, 2, 0, 3, 4)).reshape(tm, row_count, SLABS * width, chans)


def solution(mesh):
    placed = (P("tm", "rows", None, None), P(), P(), P())
    return jax.shard_map(
        per_device,
        mesh=mesh,
        in_specs=placed,
        out_specs=P(None, "rows", "tm", None),
        check_vma=False,
    )
```

time: 97.2 us -> 60 us (0.62)
  the two profiles are of different devices: /device:TPU:247 before, /device:TPU:64 now
where the time goes in v1:
time: 60 us; the launch traced here: 59.7 us
  waiting for transfers between devices  21.4 us (36%)
  starting transfers between devices  16.3 us (27%)
  blocking collectives  9.93 us (17%)
  Pallas kernels  8.33 us (14%)
  local copies, waits for them, and re-layouts  3.43 us (6%)
    all_to_all x1, waiting for transfers between devices, per_device(): lax.all_to_all(windows(frames_in, windows_count, width), ('tm', 'rows'),...  14.6 us
    all_to_all x1, blocking collectives, per_device(): lax.all_to_all(encoded, 'rows', split_axis=0, concat_axis=0, tiled=True,...  9.93 us
    pallas_call x1, Pallas kernels, per_device(): pl.pallas_call(conv_kernel, out_shape=jax.ShapeDtypeStruct((SLABS, tm, ro...  8.33 us
    all_to_all x1, starting transfers between devices, per_device(): lax.all_to_all(windows(frames_in, windows_count, width), ('tm', 'rows'),...  7.32 us
    ppermute x1, starting transfers between devices, per_device(): swap_a = lax.ppermute(jnp.where(even, bottom, top), 'rows', swap(0))  6.85 us
    ppermute x1, waiting for transfers between devices, per_device(): swap_a = lax.ppermute(jnp.where(even, bottom, top), 'rows', swap(0))  4.95 us
    ppermute x1, starting transfers between devices, per_device(): swap_b = lax.ppermute(jnp.where(even, top, bottom), 'rows', swap(1))  2.15 us
    ppermute x1, waiting for transfers between devices, per_device(): swap_b = lax.ppermute(jnp.where(even, top, bottom), 'rows', swap(1))  1.83 us
  transfers between devices with their start and end apart: 3, of which 3 were waited for; matrix products, arithmetic and copies ran while one was open for 0% of the time, Pallas kernels for 0%

profile of v1, /device:TPU:64, one launch (start us, length us, event | category | flops | bytes accessed | tf_op | source)
XLA Modules:
  0.0 59.7 jit_solution(9965077322216240413)
XLA Ops:
  0.0 1.5 %pad_slice_fusion.1 = (bf16[2,2,512,128]{3,2,1,0:T(8,128)(2,1)S(1)}, bf16[2,2,512,128]{3,2,1,0:T(8,128)(2,1)S(1)}) fusion(bf16[2,2,512,128]{3,2,1,0:T(8,128)(2,1)} %param.4), kind=kLoop, calls=%fused_computation.2 | loop fusion | bytes 1572864 | tf_op jit(solution)/shard_map/slice | solution.py:17
  1.6 0.1 maximum_bitcast_fusion
  1.7 1.0 %copy.20 = bf16[32,2,2,24,128]{4,3,2,1,0:T(8,128)(2,1)} copy(bf16[32,2,2,24,128]{4,3,0,2,1:T(8,128)(2,1)S(1)} %maximum_bitcast_fusion) | data formatting | bytes 1572864 | tf_op jit(solution)/shard_map/transpose | solution.py:20
  2.7 7.3 %all-to-all-start = ((bf16[32,2,2,24,128]{4,3,2,1,0:T(8,128)(2,1)}), bf16[32,2,2,24,128]{4,3,2,1,0:T(8,128)(2,1)S(1)}, u32[]{:S(2)}, u32[]{:S(2)}) async-start(bf16[32,2,2,24,128]{4,3,2,1,0:T(8,128)(2,1)} %copy.20), calls=%async_computation | async-start | bytes 1572864 | tf_op jit(solution)/shard_map/all_to_all | solution.py:115
  10.1 14.6 %all-to-all-done = bf16[32,2,2,24,128]{4,3,2,1,0:T(8,128)(2,1)S(1)} async-done(((bf16[32,2,2,24,128]{4,3,2,1,0:T(8,128)(2,1)}), bf16[32,2,2,24,128]{4,3,2,1,0:T(8,128)(2,1)S(1)}, u32[]{:S(2)}, u32[]{:S(2)}) %all-to-all-start) | async-done | bytes 786464 | tf_op jit(solution)/shard_map/all_to_all | solution.py:115
  24.7 0.0 copy-start
  24.7 0.0 copy-start.1
  24.7 0.0 copy-start.2
  24.8 0.1 broadcast_select_fusion
  24.8 2.1 %collective-permute-start.1 = (bf16[8,2,3,24,128]{4,3,2,1,0:T(8,128)(2,1)S(1)}, bf16[8,2,3,24,128]{4,3,2,1,0:T(8,128)(2,1)S(1)}, u32[]{:S(2)}, u32[]{:S(2)}) collective-permute-start(bf16[8,2,3,24,128]{4,3,2,1,0:T(8,128)(2,1)S(1)} %get-tuple-element.9), channel_id=1, source_target_pairs={{4,8},{8,4},{5,9},{9,5},{6,10},{10,6},{7,11},{11,7},{12,16},{16,12... | collective-permute-start | bytes 884744 | tf_op jit(solution)/shard_map/ppermute | solution.py:137
  27.0 6.8 %collective-permute-start = (bf16[8,2,3,24,128]{4,3,2,1,0:T(8,128)(2,1)S(1)}, bf16[8,2,3,24,128]{4,3,2,1,0:T(8,128)(2,1)S(1)}, u32[]{:S(2)}, u32[]{:S(2)}) collective-permute-start(bf16[8,2,3,24,128]{4,3,2,1,0:T(8,128)(2,1)S(1)} %get-tuple-element.10), channel_id=1, source_target_pairs={{0,4},{4,0},{1,5},{5,1},{2,6},{6,2},{3,7},{7,3},{8,12},{12,8},{9,1... | collective-permute-start | bytes 884744 | tf_op jit(solution)/shard_map/ppermute | solution.py:136
  33.9 0.1 stack.19.place
  33.9 1.8 %collective-permute-done.1.swap_b = bf16[8,2,3,24,128]{4,3,2,1,0:T(8,128)(2,1)S(1)} collective-permute-done((bf16[8,2,3,24,128]{4,3,2,1,0:T(8,128)(2,1)S(1)}, bf16[8,2,3,24,128]{4,3,2,1,0:T(8,128)(2,1)S(1)}, u32[]{:S(2)}, u32[]{:S(2)}) %collective-permute-start.1) | collective-permute-done | bytes 294944 | tf_op jit(solution)/shard_map/ppermute | solution.py:137
  35.8 4.9 %collective-permute-done.swap_a = bf16[8,2,3,24,128]{4,3,2,1,0:T(8,128)(2,1)S(1)} collective-permute-done((bf16[8,2,3,24,128]{4,3,2,1,0:T(8,128)(2,1)S(1)}, bf16[8,2,3,24,128]{4,3,2,1,0:T(8,128)(2,1)S(1)}, u32[]{:S(2)}, u32[]{:S(2)}) %collective-permute-start) | collective-permute-done | bytes 294944 | tf_op jit(solution)/shard_map/ppermute | solution.py:136
  40.7 0.0 copy-done
  40.7 0.0 copy-done.1
  40.7 0.0 copy-done.2
  40.7 8.3 %convs.1 = bf16[4,8,2,16,128]{4,3,2,1,0:T(8,128)(2,1)S(1)} custom-call(s32[5]{0:T(128)S(1)} %stack.19.place, bf16[8,4,2,2,24,128]{5,4,3,2,1,0:T(8,128)(2,1)S(1)} %bitcast.28, bf16[8,2,3,24,128]{4,3,2,1,0:T(8,128)(2,1)S(1)} %collective-permute-done.swap_a, bf16[8,2,3,24,128]{4,3,2,1,0:T(8,128)(2,1)S(1)} %collective-permute-done.1.swap_b, ...), custom_call_target="tpu_custom_call" | custom-call | tf_op jit(solution)/shard_map/convs/pallas_call | solution.py:150
  49.1 9.9 %all_to_all.10 = bf16[4,8,2,16,128]{4,3,2,1,0:T(8,128)(2,1)S(1)} all-to-all(bf16[4,8,2,16,128]{4,3,2,1,0:T(8,128)(2,1)S(1)} %convs.1), channel_id=1, replica_groups={{0,1,2,3},{4,5,6,7},{8,9,10,11},{12,13,14,15},{16,17,18,19},{20,21,22,2..., dimensions={0} | all-to-all | bytes 524288 | tf_op jit(solution)/shard_map/all_to_all | solution.py:168
  59.0 0.7 %copy.25 = bf16[8,2,4,16,128]{4,3,2,1,0:T(8,128)(2,1)} copy(bf16[8,2,4,16,128]{4,3,1,0,2:T(8,128)(2,1)S(1)} %bitcast.31) | data formatting | bytes 524288 | tf_op jit(solution)/shard_map/transpose | solution.py:171
  (3 shorter events, 0.1 us)
Async XLA Ops:
  2.7 21.9 %all-to-all-start = ((bf16[32,2,2,24,128]{4,3,2,1,0:T(8,128)(2,1)}), bf16[32,2,2,24,128]{4,3,2,1,0:T(8,128)(2,1)S(1)}, u32[]{:S(2)}, u32[]{:S(2)}) async-start(bf16[32,2,2,24,128]{4,3,2,1,0:T(8,128)(2,1)} %copy.20), calls=%async_computation | async-start | bytes 1572864 | tf_op jit(solution)/shard_map/all_to_all | solution.py:115
  24.7 16.1 %copy-start = (bf16[3,3,3,128,128]{4,3,2,1,0:T(8,128)(2,1)S(1)}, bf16[3,3,3,128,128]{4,3,2,1,0:T(8,128)(2,1)}, u32[]{:S(2)}) copy-start(bf16[3,3,3,128,128]{4,3,2,1,0:T(8,128)(2,1)} %w_temporal.1) | copy-start | bytes 2654212
  24.7 16.0 %copy-start.1 = (bf16[3,3,128,128]{3,2,1,0:T(8,128)(2,1)S(1)}, bf16[3,3,128,128]{3,2,1,0:T(8,128)(2,1)}, u32[]{:S(2)}) copy-start(bf16[3,3,128,128]{3,2,1,0:T(8,128)(2,1)} %w_first.1) | copy-start | bytes 884740
  24.7 16.0 %copy-start.2 = (bf16[3,3,128,128]{3,2,1,0:T(8,128)(2,1)S(1)}, bf16[3,3,128,128]{3,2,1,0:T(8,128)(2,1)}, u32[]{:S(2)}) copy-start(bf16[3,3,128,128]{3,2,1,0:T(8,128)(2,1)} %w_second.1) | copy-start | bytes 884740
  24.8 11.0 %collective-permute-start.1 = (bf16[8,2,3,24,128]{4,3,2,1,0:T(8,128)(2,1)S(1)}, bf16[8,2,3,24,128]{4,3,2,1,0:T(8,128)(2,1)S(1)}, u32[]{:S(2)}, u32[]{:S(2)}) collective-permute-start(bf16[8,2,3,24,128]{4,3,2,1,0:T(8,128)(2,1)S(1)} %get-tuple-element.9), channel_id=1, source_target_pairs={{4,8},{8,4},{5,9},{9,5},{6,10},{10,6},{7,11},{11,7},{12,16},{16,12... | collective-permute-start | bytes 884744 | tf_op jit(solution)/shard_map/ppermute | solution.py:137
  27.0 13.7 %collective-permute-start = (bf16[8,2,3,24,128]{4,3,2,1,0:T(8,128)(2,1)S(1)}, bf16[8,2,3,24,128]{4,3,2,1,0:T(8,128)(2,1)S(1)}, u32[]{:S(2)}, u32[]{:S(2)}) collective-permute-start(bf16[8,2,3,24,128]{4,3,2,1,0:T(8,128)(2,1)S(1)} %get-tuple-element.10), channel_id=1, source_target_pairs={{0,4},{4,0},{1,5},{5,1},{2,6},{6,2},{3,7},{7,3},{8,12},{12,8},{9,1... | collective-permute-start | bytes 884744 | tf_op jit(solution)/shard_map/ppermute | solution.py:136

commit v2 on v1

v2 whole, which is shorter than its diff:
```python
import jax
import jax.numpy as jnp
from jax import lax
from jax.experimental import pallas as pl
from jax.experimental.pallas import tpu as pltpu
from jax.sharding import PartitionSpec as P

SLABS = 4
HALO = 4
VMEM_BYTES = 32 * 1024 * 1024


def windows_kernel(frames, out):
    count, span = out.shape[0], out.shape[3]
    width = span - 2 * HALO
    for f in range(out.shape[1]):
        for r in range(out.shape[2]):
            row = frames[f, r].astype(jnp.float32)
            edge = jnp.zeros((HALO, row.shape[1]), jnp.float32)
            row = jnp.concatenate([edge, row, edge], axis=0)
            for k in range(count):
                out[k, f, r] = row[k * width : k * width + span].astype(jnp.bfloat16)


def column_taps(sums):
    chans = sums.shape[1] // 3
    left, mid, right = sums[:, :chans], sums[:, chans : 2 * chans], sums[:, 2 * chans :]
    return mid + pltpu.roll(left, 1, 0) + pltpu.roll(right, sums.shape[0] - 1, 0)


def inside(place, value, row, frames, span):
    first_col, first_row, last_col, last_row = place[1], place[2], place[3], place[4]
    shape = (value.shape[0] // (frames * span), frames, span, value.shape[1])
    col = lax.broadcasted_iota(jnp.int32, shape, 2) + first_col
    r = lax.broadcasted_iota(jnp.int32, shape, 0) + (first_row + row)
    keep = (col >= 0) & (col < last_col) & (r >= 0) & (r < last_row)
    return jnp.where(keep, value.reshape(shape), 0.0).reshape(value.shape)


def temporal_kernel(place, own, weight, ts, edges, send_a, send_b, xs, wt):
    frames, span, chans = own.shape[0], own.shape[4], own.shape[5]
    rows = own.shape[1] * own.shape[3]
    pitch = frames * span

    for a in range(3):
        for b in range(3):
            for c in range(3):
                k = (a * 3 + b) * chans
                wt[k : k + chans, c * chans : (c + 1) * chans] = weight[a, b, c]

    for row in range(rows):
        def pick(m, f):
            return own[m, row // 2, f, row % 2].astype(jnp.float32)

        for t in range(0, frames, 2):
            at = (row + 1) * pitch + t * span
            for a, f in ((1, 0), (2, 1)):
                pair = jnp.concatenate([pick(t, f), pick(t + 1, f)], axis=0)
                xs[a, at : at + 2 * span] = pair.astype(jnp.bfloat16)
            before = pick(t - 1, 1) if t else jnp.zeros((span, chans), jnp.float32)
            pair = jnp.concatenate([before, pick(t, 1)], axis=0)
            xs[0, at : at + 2 * span] = pair.astype(jnp.bfloat16)
    for a in range(3):
        for row in (0, rows + 1):
            xs[a, row * pitch : (row + 1) * pitch] = jnp.zeros((pitch, chans), jnp.bfloat16)

    step = rows // 2
    block = step * pitch
    for i in range(2):
        base = i * block
        lhs = jnp.concatenate(
            [xs[a, base + b * pitch : base + b * pitch + block] for a in range(3) for b in range(3)],
            axis=1,
        )
        sums = column_taps(jnp.dot(lhs, wt[...], preferred_element_type=jnp.float32))
        ts[base : base + block] = inside(place, sums, i * step, frames, span).astype(jnp.bfloat16)
        edges[i] = sums[:pitch] if i == 0 else sums[block - pitch :]

    for i, row, b in ((2, 1, 2), (3, rows, 0)):
        lhs = jnp.concatenate([xs[a, row * pitch : (row + 1) * pitch] for a in range(3)], axis=1)
        rhs = jnp.concatenate(
            [wt[(a * 3 + b) * chans : (a * 3 + b + 1) * chans] for a in range(3)], axis=0
        )
        edges[i] = column_taps(jnp.dot(lhs, rhs, preferred_element_type=jnp.float32))

    even = place[0] == 1
    up = (ts[(rows - 2) * pitch : (rows - 1) * pitch], edges[1].astype(jnp.bfloat16), edges[3].astype(jnp.bfloat16))
    down = (ts[pitch : 2 * pitch], edges[0].astype(jnp.bfloat16), edges[2].astype(jnp.bfloat16))
    for i in range(3):
        send_a[i] = jnp.where(even, up[i], down[i])
        send_b[i] = jnp.where(even, down[i], up[i])


def spatial_kernel(frames, place, ts, edges, swap_a, swap_b, w_first, w_second, out, tall, hs, w1, w2):
    rows = out.shape[0] * out.shape[2]
    chans = out.shape[4]
    pitch = ts.shape[0] // rows
    span = pitch // frames

    for b in range(3):
        for c in range(3):
            w1[b * chans : (b + 1) * chans, c * chans : (c + 1) * chans] = w_first[b, c]
            w2[b * chans : (b + 1) * chans, c * chans : (c + 1) * chans] = w_second[b, c]

    even = place[0] == 1

    def above(i):
        return jnp.where(even, swap_b[i], swap_a[i]).astype(jnp.float32)

    def below(i):
        return jnp.where(even, swap_a[i], swap_b[i]).astype(jnp.float32)

    def fill(row, value):
        at = (row + 2) * pitch
        tall[at : at + pitch] = inside(place, value, row, frames, span).astype(jnp.bfloat16)

    fill(-2, above(0))
    fill(-1, above(1) + edges[2])
    fill(0, above(2) + edges[0])
    tall[3 * pitch : (rows + 1) * pitch] = ts[pitch : (rows - 1) * pitch]
    fill(rows - 1, below(2) + edges[1])
    fill(rows, below(1) + edges[3])
    fill(rows + 1, below(0))

    step = rows // 2 + 1
    block = step * pitch
    for i in range(2):
        base = i * block
        lhs = jnp.concatenate([tall[base + b * pitch : base + b * pitch + block] for b in range(3)], axis=1)
        sums = column_taps(jnp.dot(lhs, w1[...], preferred_element_type=jnp.float32))
        active = sums / (1.0 + jnp.exp(-sums))
        hs[base : base + block] = inside(place, active, i * step - 1, frames, span).astype(jnp.bfloat16)

    step = rows // 2
    block = step * pitch
    for i in range(2):
        base = i * block
        lhs = jnp.concatenate([hs[base + b * pitch : base + b * pitch + block] for b in range(3)], axis=1)
        sums = column_taps(jnp.dot(lhs, w2[...], preferred_element_type=jnp.float32))
        sums = sums + tall[base + 2 * pitch : base + 2 * pitch + block].astype(jnp.float32)
        sums = sums.reshape(step // 2, 2, frames, span, chans)[:, :, :, HALO : span - HALO]
        for j in range(step // 2):
            for r in range(2):
                out[i * (step // 2) + j, :, r] = sums[j, r].astype(jnp.bfloat16)


def per_device(frames_in, temporal_weight, first_weight, second_weight):
    tm, slabs = lax.axis_size("tm"), lax.axis_size("rows")
    planes = slabs // SLABS
    frame_count, row_count, col_count, chans = frames_in.shape
    count = tm * SLABS
    width = col_count // count
    span = width + 2 * HALO
    plane_rows = SLABS * row_count
    pitch = tm * span
    column, slab = lax.axis_index("tm"), lax.axis_index("rows")
    plane = slab // SLABS
    place = jnp.stack(
        [
            (plane % 2 == 0).astype(jnp.int32),
            (column * SLABS + slab % SLABS) * width - HALO,
            plane * plane_rows,
            jnp.int32(col_count),
            jnp.int32(slabs * row_count),
        ]
    ).astype(jnp.int32)
    frames_in, place = lax.optimization_barrier((frames_in, place))
    vmem, smem = pl.BlockSpec(memory_space=pltpu.VMEM), pl.BlockSpec(memory_space=pltpu.SMEM)
    params = pltpu.CompilerParams(vmem_limit_bytes=VMEM_BYTES)

    cut = pl.pallas_call(
        windows_kernel,
        out_shape=jax.ShapeDtypeStruct((count, frame_count, row_count, span, chans), jnp.bfloat16),
        in_specs=[vmem],
        out_specs=vmem,
        compiler_params=params,
        name="windows",
    )(frames_in)
    members = [[m * slabs + z * SLABS + j for m in range(tm) for j in range(SLABS)] for z in range(planes)]
    own = lax.all_to_all(
        cut, ("tm", "rows"), split_axis=0, concat_axis=0, tiled=True, axis_index_groups=members
    ).reshape(tm, SLABS, frame_count, row_count, span, chans)

    line = (pitch, chans)
    ts, edges, send_a, send_b = pl.pallas_call(
        temporal_kernel,
        out_shape=[
            jax.ShapeDtypeStruct((plane_rows * pitch, chans), jnp.bfloat16),
            jax.ShapeDtypeStruct((4, *line), jnp.float32),
            jax.ShapeDtypeStruct((3, *line), jnp.bfloat16),
            jax.ShapeDtypeStruct((3, *line), jnp.bfloat16),
        ],
        in_specs=[smem, vmem, vmem],
        out_specs=[vmem] * 4,
        scratch_shapes=[
            pltpu.VMEM((3, (plane_rows + 2) * pitch, chans), jnp.bfloat16),
            pltpu.VMEM((9 * chans, 3 * chans), jnp.bfloat16),
        ],
        compiler_params=params,
        name="temporal",
    )(place, own, temporal_weight)

    def swap(parity):
        pairs = []
        for z in range(parity, planes - 1, 2):
            for j in range(SLABS):
                low, high = z * SLABS + j, (z + 1) * SLABS + j
                pairs += [(low, high), (high, low)]
        return pairs

    swap_a = lax.ppermute(send_a, "rows", swap(0))
    swap_b = lax.ppermute(send_b, "rows", swap(1))

    encoded = pl.pallas_call(
        lambda *refs: spatial_kernel(tm, *refs),
        out_shape=jax.ShapeDtypeStruct((SLABS, tm, row_count, width, chans), jnp.bfloat16),
        in_specs=[smem] + [vmem] * 6,
        out_specs=vmem,
        scratch_shapes=[
            pltpu.VMEM(((plane_rows + 4) * pitch, chans), jnp.bfloat16),
            pltpu.VMEM(((plane_rows + 2) * pitch, chans), jnp.bfloat16),
            pltpu.VMEM((3 * chans, 3 * chans), jnp.bfloat16),
            pltpu.VMEM((3 * chans, 3 * chans), jnp.bfloat16),
        ],
        compiler_params=params,
        name="spatial",
    )(place, ts, edges, swap_a, swap_b, first_weight, second_weight)

    groups = [[z * SLABS + j for j in range(SLABS)] for z in range(planes)]
    encoded = lax.all_to_all(
        encoded, "rows", split_axis=0, concat_axis=0, tiled=True, axis_index_groups=groups
    )
    return jnp.transpose(encoded, (1, 2, 0, 3, 4)).reshape(tm, row_count, SLABS * width, chans)


def solution(mesh):
    placed = (P("tm", "rows", None, None), P(), P(), P())
    return jax.shard_map(
        per_device,
        mesh=mesh,
        in_specs=placed,
        out_specs=P(None, "rows", "tm", None),
        check_vma=False,
    )
```

time: 60 us -> 52.3 us (0.87)
  the two profiles are of different devices: /device:TPU:64 before, /device:TPU:96 now
where the time goes in v2:
time: 52.3 us; the launch traced here: 52.1 us
  blocking collectives  31.8 us (61%)
  starting transfers between devices  8.86 us (17%)
  Pallas kernels  5.76 us (11%)
  waiting for transfers between devices  3.72 us (7%)
  local copies, waits for them, and re-layouts  1.87 us (4%)
    all_to_all x1, blocking collectives, per_device(): lax.all_to_all(cut, ('tm', 'rows'), split_axis=0, concat_axis=0, tiled=Tr...  21.9 us
    all_to_all x1, blocking collectives, per_device(): lax.all_to_all(encoded, 'rows', split_axis=0, concat_axis=0, tiled=True,...  9.93 us
    ppermute x1, starting transfers between devices, per_device(): swap_b = lax.ppermute(send_b, 'rows', swap(1))  6.85 us
    ppermute x1, waiting for transfers between devices, per_device(): swap_b = lax.ppermute(send_b, 'rows', swap(1))  3.72 us
    pallas_call x1, Pallas kernels, per_device(): pl.pallas_call(temporal_kernel, out_shape=[jax.ShapeDtypeStruct((plane_ro...  3.07 us
    pallas_call x1, Pallas kernels, per_device(): pl.pallas_call(lambda *refs: spatial_kernel(tm, *refs), out_shape=jax.Sha...  2.55 us
    ppermute x1, starting transfers between devices, per_device(): swap_a = lax.ppermute(send_a, 'rows', swap(0))  2.02 us
    unnamed x8, local copies, waits for them, and re-layouts  1.06 us
  transfers between devices with their start and end apart: 2, of which 1 were waited for; matrix products, arithmetic and copies ran while one was open for 0% of the time, Pallas kernels for 0%

profile of v2, /device:TPU:96, one launch (start us, length us, event | category | flops | bytes accessed | tf_op | source)
XLA Modules:
  0.0 52.1 jit_solution(4883768958411296962)
XLA Ops:
  0.0 0.1 stack.19.place.refs_0_
  0.1 0.0 copy-start.1
  0.1 1.0 %copy-done.1 = bf16[2,2,512,128]{3,2,1,0:T(8,128)(2,1)S(1)} copy-done((bf16[2,2,512,128]{3,2,1,0:T(8,128)(2,1)S(1)}, bf16[2,2,512,128]{3,2,1,0:T(8,128)(2,1)}, u32[]{:S(2)}) %copy-start.1) | copy-done | bytes 524312
  1.1 0.1 windows.1
  1.3 0.0 copy-start
  1.3 21.9 %all_to_all.10 = bf16[32,2,2,24,128]{4,3,2,1,0:T(8,128)(2,1)S(1)} all-to-all(bf16[32,2,2,24,128]{4,3,2,1,0:T(8,128)(2,1)S(1)} %windows.1), channel_id=1, replica_groups={{0,1,2,3,64,65,66,67,128,129,130,131,192,193,194,195,256,257,258,259,32..., dimensions={0} | all-to-all | bytes 1572864 | tf_op jit(solution)/shard_map/all_to_all | solution.py:180
  23.1 0.0 copy-done
  23.2 0.0 copy-start.2
  23.2 0.0 copy-start.3
  23.2 3.1 %temporal.1 = (bf16[1536,128]{1,0:T(8,128)(2,1)S(1)}, f32[4,192,128]{2,1,0:T(8,128)S(1)}, bf16[3,192,128]{2,1,0:T(8,128)(2,1)S(1)}, bf16[3,192,128]{2,1,0:T(8,128)(2,1)S(1)}) custom-call(s32[5]{0:T(128)S(1)} %stack.19.place.refs_0_, bf16[8,4,2,2,24,128]{5,4,3,2,1,0:T(8,128)(2,1)S(1)} %bitcast.6, bf16[3,3,3,128,128]{4,3,2,1,0:T(8,128)(2,1)S(1)} %copy-done), custom_call_target="tpu_custom_call" | custom-call | tf_op jit(solution)/shard_map/temporal/pallas_call | solution.py:185
  26.2 2.0 %collective-permute-start = (bf16[3,192,128]{2,1,0:T(8,128)(2,1)S(1)}, bf16[3,192,128]{2,1,0:T(8,128)(2,1)S(1)}, u32[]{:S(2)}, u32[]{:S(2)}) collective-permute-start(bf16[3,192,128]{2,1,0:T(8,128)(2,1)S(1)} %get-tuple-element.15), channel_id=1, source_target_pairs={{0,4},{4,0},{1,5},{5,1},{2,6},{6,2},{3,7},{7,3},{8,12},{12,8},{9,1... | collective-permute-start | bytes 442376 | tf_op jit(solution)/shard_map/ppermute | solution.py:211
  28.3 6.8 %collective-permute-start.1 = (bf16[3,192,128]{2,1,0:T(8,128)(2,1)S(1)}, bf16[3,192,128]{2,1,0:T(8,128)(2,1)S(1)}, u32[]{:S(2)}, u32[]{:S(2)}) collective-permute-start(bf16[3,192,128]{2,1,0:T(8,128)(2,1)S(1)} %get-tuple-element.16), channel_id=1, source_target_pairs={{4,8},{8,4},{5,9},{9,5},{6,10},{10,6},{7,11},{11,7},{12,16},{16,12... | collective-permute-start | bytes 442376 | tf_op jit(solution)/shard_map/ppermute | solution.py:212
  35.1 0.0 collective-permute-done.refs_3_
  35.1 3.7 %collective-permute-done.1.refs_4_ = bf16[3,192,128]{2,1,0:T(8,128)(2,1)S(1)} collective-permute-done((bf16[3,192,128]{2,1,0:T(8,128)(2,1)S(1)}, bf16[3,192,128]{2,1,0:T(8,128)(2,1)S(1)}, u32[]{:S(2)}, u32[]{:S(2)}) %collective-permute-start.1) | collective-permute-done | bytes 147488 | tf_op jit(solution)/shard_map/ppermute | solution.py:212
  38.8 0.0 copy-done.2
  38.9 0.0 copy-done.3
  38.9 2.5 %spatial.1 = bf16[4,8,2,16,128]{4,3,2,1,0:T(8,128)(2,1)S(1)} custom-call(s32[5]{0:T(128)S(1)} %stack.19.place.refs_0_, bf16[1536,128]{1,0:T(8,128)(2,1)S(1)} %get-tuple-element.13.refs_1_, f32[4,192,128]{2,1,0:T(8,128)S(1)} %get-tuple-element.14.refs_2_, bf16[3,192,128]{2,1,0:T(8,128)(2,1)S(1)} %collective-permute-done.refs_3_, ...), custom_call_target="tpu_custom_call" | custom-call | tf_op jit(solution)/shard_map/spatial/pallas_call | solution.py:214
  41.4 9.9 %all_to_all.11 = bf16[4,8,2,16,128]{4,3,2,1,0:T(8,128)(2,1)S(1)} all-to-all(bf16[4,8,2,16,128]{4,3,2,1,0:T(8,128)(2,1)S(1)} %spatial.1), channel_id=1, replica_groups={{0,1,2,3},{4,5,6,7},{8,9,10,11},{12,13,14,15},{16,17,18,19},{20,21,22,2..., dimensions={0} | all-to-all | bytes 524288 | tf_op jit(solution)/shard_map/all_to_all | solution.py:230
  51.3 0.7 %copy.5 = bf16[8,2,4,16,128]{4,3,2,1,0:T(8,128)(2,1)} copy(bf16[8,2,4,16,128]{4,3,1,0,2:T(8,128)(2,1)S(1)} %bitcast.7) | data formatting | bytes 524288 | tf_op jit(solution)/shard_map/transpose | solution.py:233
Async XLA Ops:
  0.1 1.0 %copy-start.1 = (bf16[2,2,512,128]{3,2,1,0:T(8,128)(2,1)S(1)}, bf16[2,2,512,128]{3,2,1,0:T(8,128)(2,1)}, u32[]{:S(2)}) copy-start(bf16[2,2,512,128]{3,2,1,0:T(8,128)(2,1)} %frames) | copy-start | bytes 1572868
  1.3 21.9 %copy-start = (bf16[3,3,3,128,128]{4,3,2,1,0:T(8,128)(2,1)S(1)}, bf16[3,3,3,128,128]{4,3,2,1,0:T(8,128)(2,1)}, u32[]{:S(2)}) copy-start(bf16[3,3,3,128,128]{4,3,2,1,0:T(8,128)(2,1)} %weight.1) | copy-start | bytes 2654212
  23.2 15.7 %copy-start.2 = (bf16[3,3,128,128]{3,2,1,0:T(8,128)(2,1)S(1)}, bf16[3,3,128,128]{3,2,1,0:T(8,128)(2,1)}, u32[]{:S(2)}) copy-start(bf16[3,3,128,128]{3,2,1,0:T(8,128)(2,1)} %refs_5_.1) | copy-start | bytes 884740
  23.2 15.7 %copy-start.3 = (bf16[3,3,128,128]{3,2,1,0:T(8,128)(2,1)S(1)}, bf16[3,3,128,128]{3,2,1,0:T(8,128)(2,1)}, u32[]{:S(2)}) copy-start(bf16[3,3,128,128]{3,2,1,0:T(8,128)(2,1)} %refs_6_.1) | copy-start | bytes 884740
  26.2 8.9 %collective-permute-start = (bf16[3,192,128]{2,1,0:T(8,128)(2,1)S(1)}, bf16[3,192,128]{2,1,0:T(8,128)(2,1)S(1)}, u32[]{:S(2)}, u32[]{:S(2)}) collective-permute-start(bf16[3,192,128]{2,1,0:T(8,128)(2,1)S(1)} %get-tuple-element.15), channel_id=1, source_target_pairs={{0,4},{4,0},{1,5},{5,1},{2,6},{6,2},{3,7},{7,3},{8,12},{12,8},{9,1... | collective-permute-start | bytes 442376 | tf_op jit(solution)/shard_map/ppermute | solution.py:211
  28.3 10.6 %collective-permute-start.1 = (bf16[3,192,128]{2,1,0:T(8,128)(2,1)S(1)}, bf16[3,192,128]{2,1,0:T(8,128)(2,1)S(1)}, u32[]{:S(2)}, u32[]{:S(2)}) collective-permute-start(bf16[3,192,128]{2,1,0:T(8,128)(2,1)S(1)} %get-tuple-element.16), channel_id=1, source_target_pairs={{4,8},{8,4},{5,9},{9,5},{6,10},{10,6},{7,11},{11,7},{12,16},{16,12... | collective-permute-start | bytes 442376 | tf_op jit(solution)/shard_map/ppermute | solution.py:212

commit v3 on v2

v3 whole, which is shorter than its diff:
```python
import jax
import jax.numpy as jnp
from jax import lax
from jax.experimental import pallas as pl
from jax.experimental.pallas import tpu as pltpu
from jax.sharding import PartitionSpec as P

SLABS = 4
HALO = 4
VMEM_BYTES = 32 * 1024 * 1024


def windows_kernel(frames, out):
    count, span = out.shape[0], out.shape[3]
    width = span - 2 * HALO
    for f in range(out.shape[1]):
        for r in range(out.shape[2]):
            row = frames[f, r].astype(jnp.float32)
            edge = jnp.zeros((HALO, row.shape[1]), jnp.float32)
            row = jnp.concatenate([edge, row, edge], axis=0)
            for k in range(count):
                out[k, f, r] = row[k * width : k * width + span].astype(jnp.bfloat16)


def column_taps(sums):
    chans = sums.shape[1] // 3
    left, mid, right = sums[:, :chans], sums[:, chans : 2 * chans], sums[:, 2 * chans :]
    return mid + pltpu.roll(left, 1, 0) + pltpu.roll(right, sums.shape[0] - 1, 0)


def inside(place, value, row, frames, span):
    first_col, first_row, last_col, last_row = place[1], place[2], place[3], place[4]
    count, chans = value.shape[0] // (frames * span), value.shape[1]
    col = lax.broadcasted_iota(jnp.int32, (span, chans), 0) + first_col
    keep = (col >= 0) & (col < last_col)
    value = jnp.where(keep[None], value.reshape(count * frames, span, chans), 0.0)
    value = value.reshape(count, frames * span, chans)
    kept = []
    for i in range(count):
        r = first_row + row + i
        shown = jnp.where((r >= 0) & (r < last_row), 1.0, 0.0) if row + i < 0 or row + i >= 8 else None
        kept.append(value[i] if shown is None else value[i] * shown)
    return jnp.concatenate(kept, axis=0)


def temporal_weight_to(wt, weight):
    chans = weight.shape[3]
    for a in range(3):
        for b in range(3):
            for c in range(3):
                k = (b * 3 + a) * chans
                wt[k : k + chans, c * chans : (c + 1) * chans] = weight[a, b, c]


def plane_weight_to(wt, weight):
    chans = weight.shape[2]
    for b in range(3):
        for c in range(3):
            wt[b * chans : (b + 1) * chans, c * chans : (c + 1) * chans] = weight[b, c]


def frames_to(xs, at, own, row):
    frames, span, chans = own.shape[0], own.shape[4], own.shape[5]

    def pick(m, f):
        return own[m, row // 2, f, row % 2].astype(jnp.float32)

    for t in range(0, frames, 2):
        here = at + t * span
        for a, f in ((1, 0), (2, 1)):
            pair = jnp.concatenate([pick(t, f), pick(t + 1, f)], axis=0)
            xs[a, here : here + 2 * span] = pair.astype(jnp.bfloat16)
        before = pick(t - 1, 1) if t else jnp.zeros((span, chans), jnp.float32)
        pair = jnp.concatenate([before, pick(t, 1)], axis=0)
        xs[0, here : here + 2 * span] = pair.astype(jnp.bfloat16)


def rows_of(ref, first, count, pitch):
    return ref[first * pitch : (first + count) * pitch]


def row_taps(ref, first, count, pitch):
    return jnp.concatenate([rows_of(ref, first + b, count, pitch) for b in range(3)], axis=1)


def edge_kernel(place, own, weight, t_edge, edges, send_a, send_b, xs, wt):
    frames, span, chans = own.shape[0], own.shape[4], own.shape[5]
    rows = own.shape[1] * own.shape[3]
    pitch = frames * span
    temporal_weight_to(wt, weight)

    for i in range(3):
        frames_to(xs, i * pitch, own, i)
        frames_to(xs, (3 + i) * pitch, own, rows - 3 + i)

    def taps_of(i):
        return jnp.concatenate([xs[a, i * pitch : (i + 1) * pitch] for a in range(3)], axis=1)

    def dot(lhs, rhs):
        return column_taps(jnp.dot(lhs, rhs, preferred_element_type=jnp.float32))

    deep = 3 * chans
    x = [taps_of(i) for i in range(6)]
    low = dot(
        jnp.concatenate([jnp.concatenate(x[0:2], axis=1), jnp.concatenate(x[1:3], axis=1)], axis=0),
        wt[deep:],
    )
    high = dot(
        jnp.concatenate([jnp.concatenate(x[3:5], axis=1), jnp.concatenate(x[4:6], axis=1)], axis=0),
        wt[: 2 * deep],
    )
    outer = jnp.dot(
        jnp.concatenate([x[0], x[5]], axis=0),
        jnp.concatenate([wt[:deep], wt[2 * deep :]], axis=1),
        preferred_element_type=jnp.float32,
    )
    upper, lower = column_taps(outer[:, :deep]), column_taps(outer[:, deep:])
    first, last = low[:pitch], high[pitch:]
    before, after = lower[:pitch], upper[pitch:]
    edges[0], edges[1], edges[2], edges[3] = first, last, before, after
    near = inside(place, low[pitch:] + upper[:pitch], 1, frames, span).astype(jnp.bfloat16)
    far = inside(place, high[:pitch] + lower[pitch:], rows - 2, frames, span).astype(jnp.bfloat16)
    t_edge[0], t_edge[1] = near, far

    even = place[0] == 1
    up = (far, last.astype(jnp.bfloat16), after.astype(jnp.bfloat16))
    down = (near, first.astype(jnp.bfloat16), before.astype(jnp.bfloat16))
    for i in range(3):
        send_a[i] = jnp.where(even, up[i], down[i])
        send_b[i] = jnp.where(even, down[i], up[i])


def crop(value, frames, span):
    shape = (value.shape[0] // (frames * span), frames, span, value.shape[1])
    return value.reshape(shape)[:, :, HALO : span - HALO].astype(jnp.bfloat16)


def inner_kernel(place, own, weight, t_edge, w_first, w_second, t_mid, h_mid, o_mid, xs, tall, wt, w1, w2):
    frames, span = own.shape[0], own.shape[4]
    rows = own.shape[1] * own.shape[3]
    pitch = frames * span
    temporal_weight_to(wt, weight)
    plane_weight_to(w1, w_first)
    plane_weight_to(w2, w_second)
    for row in range(1, rows - 1):
        frames_to(xs, (row - 1) * pitch, own, row)
    lhs = jnp.concatenate(
        [xs[a, b * pitch : (b + rows - 4) * pitch] for b in range(3) for a in range(3)], axis=1
    )
    sums = column_taps(jnp.dot(lhs, wt[...], preferred_element_type=jnp.float32))
    middle = inside(place, sums, 2, frames, span).astype(jnp.bfloat16)
    t_mid[...] = middle
    tall[:pitch] = t_edge[0]
    tall[pitch : (rows - 3) * pitch] = middle
    tall[(rows - 3) * pitch :] = t_edge[1]

    sums = column_taps(
        jnp.dot(row_taps(tall, 0, rows - 4, pitch), w1[...], preferred_element_type=jnp.float32)
    )
    active = sums * (0.5 * jnp.tanh(0.5 * sums) + 0.5)
    h_mid[...] = inside(place, active, 2, frames, span).astype(jnp.bfloat16)

    sums = column_taps(
        jnp.dot(row_taps(h_mid, 0, rows - 6, pitch), w2[...], preferred_element_type=jnp.float32)
    )
    sums = sums + rows_of(t_mid, 1, rows - 6, pitch).astype(jnp.float32)
    o_mid[...] = crop(sums, frames, span)


def outer_kernel(
    frames, place, t_edge, edges, t_mid, h_mid, o_mid, swap_a, swap_b, w_first, w_second,
    out, tall, hs, w1, w2,
):
    rows = out.shape[0] * out.shape[2]
    pitch = t_edge.shape[1]
    span = pitch // frames
    plane_weight_to(w1, w_first)
    plane_weight_to(w2, w_second)

    even = place[0] == 1

    def above(i):
        return jnp.where(even, swap_b[i], swap_a[i]).astype(jnp.float32)

    def below(i):
        return jnp.where(even, swap_a[i], swap_b[i]).astype(jnp.float32)

    def fill(at, row, value):
        value = inside(place, value, row, frames, span)
        tall[at * pitch : (at + 1) * pitch] = value.astype(jnp.bfloat16)

    fill(0, -2, above(0))
    fill(1, -1, above(1) + edges[2])
    fill(2, 0, above(2) + edges[0])
    tall[3 * pitch : 4 * pitch] = t_edge[0]
    tall[4 * pitch : 5 * pitch] = rows_of(t_mid, 0, 1, pitch)
    tall[5 * pitch : 6 * pitch] = rows_of(t_mid, rows - 5, 1, pitch)
    tall[6 * pitch : 7 * pitch] = t_edge[1]
    fill(7, rows - 1, below(2) + edges[1])
    fill(8, rows, below(1) + edges[3])
    fill(9, rows + 1, below(0))

    lhs = jnp.concatenate([row_taps(tall, s, 3, pitch) for s in (0, 5)], axis=0)
    sums = column_taps(jnp.dot(lhs, w1[...], preferred_element_type=jnp.float32))
    active = sums * (0.5 * jnp.tanh(0.5 * sums) + 0.5)
    half = 3 * pitch
    hs[:half] = inside(place, active[:half], -1, frames, span).astype(jnp.bfloat16)
    hs[half : 5 * pitch] = rows_of(h_mid, 0, 2, pitch)
    hs[5 * pitch : 7 * pitch] = rows_of(h_mid, rows - 6, 2, pitch)
    hs[7 * pitch :] = inside(place, active[half:], rows - 2, frames, span).astype(jnp.bfloat16)

    lhs = jnp.concatenate([row_taps(hs, s, 3, pitch) for s in (0, 5)], axis=0)
    sums = column_taps(jnp.dot(lhs, w2[...], preferred_element_type=jnp.float32))
    skip = jnp.concatenate([rows_of(tall, s, 3, pitch) for s in (2, 5)], axis=0)
    done = crop(sums + skip.astype(jnp.float32), frames, span)
    for i in range(3):
        out[i // 2, :, i % 2] = done[i]
        row = rows - 3 + i
        out[row // 2, :, row % 2] = done[3 + i]
    for row in range(3, rows - 3):
        out[row // 2, :, row % 2] = o_mid[row - 3]


def per_device(frames_in, temporal_weight, first_weight, second_weight):
    tm, slabs = lax.axis_size("tm"), lax.axis_size("rows")
    planes = slabs // SLABS
    frame_count, row_count, col_count, chans = frames_in.shape
    count = tm * SLABS
    width = col_count // count
    span = width + 2 * HALO
    plane_rows = SLABS * row_count
    pitch = tm * span
    column, slab = lax.axis_index("tm"), lax.axis_index("rows")
    plane = slab // SLABS
    place = jnp.stack(
        [
            (plane % 2 == 0).astype(jnp.int32),
            (column * SLABS + slab % SLABS) * width - HALO,
            plane * plane_rows,
            jnp.int32(col_count),
            jnp.int32(slabs * row_count),
        ]
    ).astype(jnp.int32)
    frames_in, place = lax.optimization_barrier((frames_in, place))
    vmem, smem = pl.BlockSpec(memory_space=pltpu.VMEM), pl.BlockSpec(memory_space=pltpu.SMEM)
    params = pltpu.CompilerParams(vmem_limit_bytes=VMEM_BYTES)

    def brain(*shape):
        return jax.ShapeDtypeStruct(shape, jnp.bfloat16)

    def held(*shape):
        return pltpu.VMEM(shape, jnp.bfloat16)

    cut = pl.pallas_call(
        windows_kernel,
        out_shape=brain(count, frame_count, row_count, span, chans),
        in_specs=[vmem],
        out_specs=vmem,
        compiler_params=params,
        name="windows",
    )(frames_in)
    members = [[m * slabs + z * SLABS + j for m in range(tm) for j in range(SLABS)] for z in range(planes)]
    own = lax.all_to_all(
        cut, ("tm", "rows"), split_axis=0, concat_axis=0, tiled=True, axis_index_groups=members
    ).reshape(tm, SLABS, frame_count, row_count, span, chans)

    t_edge, edges, send_a, send_b = pl.pallas_call(
        edge_kernel,
        out_shape=[
            brain(2, pitch, chans),
            jax.ShapeDtypeStruct((4, pitch, chans), jnp.float32),
            brain(3, pitch, chans),
            brain(3, pitch, chans),
        ],
        in_specs=[smem, vmem, vmem],
        out_specs=[vmem] * 4,
        scratch_shapes=[held(3, 6 * pitch, chans), held(9 * chans, 3 * chans)],
        compiler_params=params,
        name="edge",
    )(place, own, temporal_weight)

    def swap(parity):
        pairs = []
        for z in range(parity, planes - 1, 2):
            for j in range(SLABS):
                low, high = z * SLABS + j, (z + 1) * SLABS + j
                pairs += [(low, high), (high, low)]
        return pairs

    swap_a = lax.ppermute(send_a, "rows", swap(0))
    swap_b = lax.ppermute(send_b, "rows", swap(1))

    inner = plane_rows - 4
    t_mid, h_mid, o_mid = pl.pallas_call(
        inner_kernel,
        out_shape=[
            brain(inner * pitch, chans),
            brain(inner * pitch, chans),
            brain(inner - 2, tm, width, chans),
        ],
        in_specs=[smem] + [vmem] * 5,
        out_specs=[vmem] * 3,
        scratch_shapes=[
            held(3, (inner + 2) * pitch, chans),
            held((inner + 2) * pitch, chans),
            held(9 * chans, 3 * chans),
            held(3 * chans, 3 * chans),
            held(3 * chans, 3 * chans),
        ],
        compiler_params=params,
        cost_estimate=pl.CostEstimate(flops=10**9, bytes_accessed=4 * 10**6, transcendentals=10**5),
        name="inner",
    )(place, own, temporal_weight, t_edge, first_weight, second_weight)
    encoded = pl.pallas_call(
        lambda *refs: outer_kernel(tm, *refs),
        out_shape=brain(SLABS, tm, row_count, width, chans),
        in_specs=[smem] + [vmem] * 9,
        out_specs=vmem,
        scratch_shapes=[
            held(10 * pitch, chans),
            held(10 * pitch, chans),
            held(3 * chans, 3 * chans),
            held(3 * chans, 3 * chans),
        ],
        compiler_params=params,
        name="outer",
    )(place, t_edge, edges, t_mid, h_mid, o_mid, swap_a, swap_b, first_weight, second_weight)

    groups = [[z * SLABS + j for j in range(SLABS)] for z in range(planes)]
    encoded = lax.all_to_all(
        encoded, "rows", split_axis=0, concat_axis=0, tiled=True, axis_index_groups=groups
    )
    return jnp.transpose(encoded, (1, 2, 0, 3, 4)).reshape(tm, row_count, SLABS * width, chans)


def solution(mesh):
    placed = (P("tm", "rows", None, None), P(), P(), P())
    return jax.shard_map(
        per_device,
        mesh=mesh,
        in_specs=placed,
        out_specs=P(None, "rows", "tm", None),
        check_vma=False,
    )
```

time: 52.3 us -> 50.7 us (0.969)
  waiting for transfers between devices: 3.72 us -> 1.02 us
  Pallas kernels: 5.76 us -> 6.82 us
    ppermute x1, waiting for transfers between devices: 3.72 us -> 1.01 us  [per_device(): swap_b = lax.ppermute(send_b, 'rows', swap(1))]
    pallas_call x3 -> x4, Pallas kernels: 5.76 us -> 6.82 us  [the longest x1 2.68 us: per_device(): pl.pallas_call(inner_kernel, out_shape=[brain(inner * pitch, chans), brai...]
  transfers between devices with their start and end apart: 2 -> 2, of which waited for: 1 -> 1; matrix products, arithmetic and copies ran while one was open for 0% -> 0% of each run, Pallas kernels for 0% -> 5%
where the time goes in v3:
time: 50.7 us; the launch traced here: 50.4 us
  blocking collectives  31.8 us (63%)
  starting transfers between devices  8.86 us (17%)
  Pallas kernels  6.82 us (13%)
  local copies, waits for them, and re-layouts  1.87 us (4%)
  waiting for transfers between devices  1.02 us (2%)
    all_to_all x1, blocking collectives, per_device(): lax.all_to_all(cut, ('tm', 'rows'), split_axis=0, concat_axis=0, tiled=Tr...  21.9 us
    all_to_all x1, blocking collectives, per_device(): lax.all_to_all(encoded, 'rows', split_axis=0, concat_axis=0, tiled=True,...  9.93 us
    ppermute x1, starting transfers between devices, per_device(): swap_b = lax.ppermute(send_b, 'rows', swap(1))  6.85 us
    pallas_call x1, Pallas kernels, per_device(): pl.pallas_call(inner_kernel, out_shape=[brain(inner * pitch, chans), brai...  2.68 us
    pallas_call x1, Pallas kernels, per_device(): pl.pallas_call(lambda *refs: outer_kernel(tm, *refs), out_shape=brain(SLA...  2.21 us
    ppermute x1, starting transfers between devices, per_device(): swap_a = lax.ppermute(send_a, 'rows', swap(0))  2.02 us
    pallas_call x1, Pallas kernels, per_device(): pl.pallas_call(edge_kernel, out_shape=[brain(2, pitch, chans), jax.ShapeD...  1.79 us
    unnamed x8, local copies, waits for them, and re-layouts  1.06 us
  transfers between devices with their start and end apart: 2, of which 1 were waited for; matrix products, arithmetic and copies ran while one was open for 0% of the time, Pallas kernels for 5%

profile of v3, /device:TPU:96, one launch (start us, length us, event | category | flops | bytes accessed | tf_op | source)
XLA Modules:
  0.0 50.4 jit_solution(15300343758077391471)
XLA Ops:
  0.0 0.1 stack.19.place.refs_0_
  0.1 0.0 copy-start.1
  0.1 1.0 %copy-done.1 = bf16[2,2,512,128]{3,2,1,0:T(8,128)(2,1)S(1)} copy-done((bf16[2,2,512,128]{3,2,1,0:T(8,128)(2,1)S(1)}, bf16[2,2,512,128]{3,2,1,0:T(8,128)(2,1)}, u32[]{:S(2)}) %copy-start.1) | copy-done | bytes 524312
  1.1 0.1 windows.1
  1.3 0.0 copy-start
  1.3 21.9 %all_to_all.10 = bf16[32,2,2,24,128]{4,3,2,1,0:T(8,128)(2,1)S(1)} all-to-all(bf16[32,2,2,24,128]{4,3,2,1,0:T(8,128)(2,1)S(1)} %windows.1), channel_id=1, replica_groups={{0,1,2,3,64,65,66,67,128,129,130,131,192,193,194,195,256,257,258,259,32..., dimensions={0} | all-to-all | bytes 1572864 | tf_op jit(solution)/shard_map/all_to_all | solution.py:263
  23.1 0.0 copy-done
  23.2 0.0 copy-start.2
  23.2 0.0 copy-start.3
  23.2 1.8 %edge.1 = (bf16[2,192,128]{2,1,0:T(8,128)(2,1)S(1)}, f32[4,192,128]{2,1,0:T(8,128)S(1)}, bf16[3,192,128]{2,1,0:T(8,128)(2,1)S(1)}, bf16[3,192,128]{2,1,0:T(8,128)(2,1)S(1)}) custom-call(s32[5]{0:T(128)S(1)} %stack.19.place.refs_0_, bf16[8,4,2,2,24,128]{5,4,3,2,1,0:T(8,128)(2,1)S(1)} %bitcast.6, bf16[3,3,3,128,128]{4,3,2,1,0:T(8,128)(2,1)S(1)} %copy-done), custom_call_target="tpu_custom_call" | custom-call | tf_op jit(solution)/shard_map/edge/pallas_call | solution.py:267
  25.0 2.0 %collective-permute-start = (bf16[3,192,128]{2,1,0:T(8,128)(2,1)S(1)}, bf16[3,192,128]{2,1,0:T(8,128)(2,1)S(1)}, u32[]{:S(2)}, u32[]{:S(2)}) collective-permute-start(bf16[3,192,128]{2,1,0:T(8,128)(2,1)S(1)} %get-tuple-element.21), channel_id=1, source_target_pairs={{0,4},{4,0},{1,5},{5,1},{2,6},{6,2},{3,7},{7,3},{8,12},{12,8},{9,1... | collective-permute-start | bytes 442376 | tf_op jit(solution)/shard_map/ppermute | solution.py:290
  27.0 6.8 %collective-permute-start.1 = (bf16[3,192,128]{2,1,0:T(8,128)(2,1)S(1)}, bf16[3,192,128]{2,1,0:T(8,128)(2,1)S(1)}, u32[]{:S(2)}, u32[]{:S(2)}) collective-permute-start(bf16[3,192,128]{2,1,0:T(8,128)(2,1)S(1)} %get-tuple-element.22), channel_id=1, source_target_pairs={{4,8},{8,4},{5,9},{9,5},{6,10},{10,6},{7,11},{11,7},{12,16},{16,12... | collective-permute-start | bytes 442376 | tf_op jit(solution)/shard_map/ppermute | solution.py:291
  33.8 0.0 copy-done.2
  33.8 0.0 copy-done.3
  33.9 2.7 %inner.1 = (bf16[768,128]{1,0:T(8,128)(2,1)S(1)}, bf16[768,128]{1,0:T(8,128)(2,1)S(1)}, bf16[2,8,16,128]{3,2,1,0:T(8,128)(2,1)S(1)}) custom-call(s32[5]{0:T(128)S(1)} %stack.19.place.refs_0_, bf16[8,4,2,2,24,128]{5,4,3,2,1,0:T(8,128)(2,1)S(1)} %bitcast.7, bf16[3,3,3,128,128]{4,3,2,1,0:T(8,128)(2,1)S(1)} %copy-done, ...), custom_call_target="tpu_custom_call" | custom-call | flops 1000000000 | bytes 4000000 | tf_op jit(solution)/shard_map/inner/pallas_call | solution.py:294
  36.5 0.0 collective-permute-done.refs_6_
  36.5 1.0 %collective-permute-done.1.refs_7_ = bf16[3,192,128]{2,1,0:T(8,128)(2,1)S(1)} collective-permute-done((bf16[3,192,128]{2,1,0:T(8,128)(2,1)S(1)}, bf16[3,192,128]{2,1,0:T(8,128)(2,1)S(1)}, u32[]{:S(2)}, u32[]{:S(2)}) %collective-permute-start.1) | collective-permute-done | bytes 147488 | tf_op jit(solution)/shard_map/ppermute | solution.py:291
  37.6 2.2 %outer.1 = bf16[4,8,2,16,128]{4,3,2,1,0:T(8,128)(2,1)S(1)} custom-call(s32[5]{0:T(128)S(1)} %stack.19.place.refs_0_, bf16[2,192,128]{2,1,0:T(8,128)(2,1)S(1)} %get-tuple-element.16.t_edge.refs_1_, f32[4,192,128]{2,1,0:T(8,128)S(1)} %get-tuple-element.17.refs_2_, bf16[768,128]{1,0:T(8,128)(2,1)S(1)} %get-tuple-element.18.refs_3_, ...), custom_call_target="tpu_custom_call" | custom-call | tf_op jit(solution)/shard_map/outer/pallas_call | solution.py:314
  39.8 9.9 %all_to_all.11 = bf16[4,8,2,16,128]{4,3,2,1,0:T(8,128)(2,1)S(1)} all-to-all(bf16[4,8,2,16,128]{4,3,2,1,0:T(8,128)(2,1)S(1)} %outer.1), channel_id=1, replica_groups={{0,1,2,3},{4,5,6,7},{8,9,10,11},{12,13,14,15},{16,17,18,19},{20,21,22,2..., dimensions={0} | all-to-all | bytes 524288 | tf_op jit(solution)/shard_map/all_to_all | solution.py:330
  49.7 0.7 %copy.5 = bf16[8,2,4,16,128]{4,3,2,1,0:T(8,128)(2,1)} copy(bf16[8,2,4,16,128]{4,3,1,0,2:T(8,128)(2,1)S(1)} %bitcast.8) | data formatting | bytes 524288 | tf_op jit(solution)/shard_map/transpose | solution.py:333
Async XLA Ops:
  0.1 1.0 %copy-start.1 = (bf16[2,2,512,128]{3,2,1,0:T(8,128)(2,1)S(1)}, bf16[2,2,512,128]{3,2,1,0:T(8,128)(2,1)}, u32[]{:S(2)}) copy-start(bf16[2,2,512,128]{3,2,1,0:T(8,128)(2,1)} %frames) | copy-start | bytes 1572868
  1.3 21.9 %copy-start = (bf16[3,3,3,128,128]{4,3,2,1,0:T(8,128)(2,1)S(1)}, bf16[3,3,3,128,128]{4,3,2,1,0:T(8,128)(2,1)}, u32[]{:S(2)}) copy-start(bf16[3,3,3,128,128]{4,3,2,1,0:T(8,128)(2,1)} %weight.3) | copy-start | bytes 2654212
  23.2 10.7 %copy-start.2 = (bf16[3,3,128,128]{3,2,1,0:T(8,128)(2,1)S(1)}, bf16[3,3,128,128]{3,2,1,0:T(8,128)(2,1)}, u32[]{:S(2)}) copy-start(bf16[3,3,128,128]{3,2,1,0:T(8,128)(2,1)} %refs_8_.1) | copy-start | bytes 884740
  23.2 10.7 %copy-start.3 = (bf16[3,3,128,128]{3,2,1,0:T(8,128)(2,1)S(1)}, bf16[3,3,128,128]{3,2,1,0:T(8,128)(2,1)}, u32[]{:S(2)}) copy-start(bf16[3,3,128,128]{3,2,1,0:T(8,128)(2,1)} %refs_9_.1) | copy-start | bytes 884740
  25.0 11.6 %collective-permute-start = (bf16[3,192,128]{2,1,0:T(8,128)(2,1)S(1)}, bf16[3,192,128]{2,1,0:T(8,128)(2,1)S(1)}, u32[]{:S(2)}, u32[]{:S(2)}) collective-permute-start(bf16[3,192,128]{2,1,0:T(8,128)(2,1)S(1)} %get-tuple-element.21), channel_id=1, source_target_pairs={{0,4},{4,0},{1,5},{5,1},{2,6},{6,2},{3,7},{7,3},{8,12},{12,8},{9,1... | collective-permute-start | bytes 442376 | tf_op jit(solution)/shard_map/ppermute | solution.py:290
  27.0 10.6 %collective-permute-start.1 = (bf16[3,192,128]{2,1,0:T(8,128)(2,1)S(1)}, bf16[3,192,128]{2,1,0:T(8,128)(2,1)S(1)}, u32[]{:S(2)}, u32[]{:S(2)}) collective-permute-start(bf16[3,192,128]{2,1,0:T(8,128)(2,1)S(1)} %get-tuple-element.22), channel_id=1, source_target_pairs={{4,8},{8,4},{5,9},{9,5},{6,10},{10,6},{7,11},{11,7},{12,16},{16,12... | collective-permute-start | bytes 442376 | tf_op jit(solution)/shard_map/ppermute | solution.py:291

commit v4 on v3

--- a/solution.py
+++ b/solution.py
@@ -29,7 +29,7 @@
 
 
 def inside(place, value, row, frames, span):
-    first_col, first_row, last_col, last_row = place[1], place[2], place[3], place[4]
+    first_col, first_row, last_col, last_row = place[0], place[1], place[2], place[3]
     count, chans = value.shape[0] // (frames * span), value.shape[1]
     col = lax.broadcasted_iota(jnp.int32, (span, chans), 0) + first_col
     keep = (col >= 0) & (col < last_col)
@@ -75,6 +75,10 @@
         xs[0, here : here + 2 * span] = pair.astype(jnp.bfloat16)
 
 
+def silu(value):
+    return value * (0.5 * jnp.tanh(0.5 * value) + 0.5)
+
+
 def rows_of(ref, first, count, pitch):
     return ref[first * pitch : (first + count) * pitch]
 
@@ -83,11 +87,21 @@
     return jnp.concatenate([rows_of(ref, first + b, count, pitch) for b in range(3)], axis=1)
 
 
-def edge_kernel(place, own, weight, t_edge, edges, send_a, send_b, xs, wt):
+def temporal_taps(weight, row_taps):
+    return jnp.concatenate(
+        [
+            jnp.concatenate([weight[a, b, c] for c in range(3)], axis=1)
+            for b in row_taps
+            for a in range(3)
+        ],
+        axis=0,
+    )
+
+
+def edge_kernel(place, own, weight, t_edge, edges, send_down, send_up, xs):
     frames, span, chans = own.shape[0], own.shape[4], own.shape[5]
     rows = own.shape[1] * own.shape[3]
     pitch = frames * span
-    temporal_weight_to(wt, weight)
 
     for i in range(3):
         frames_to(xs, i * pitch, own, i)
@@ -103,15 +117,15 @@
     x = [taps_of(i) for i in range(6)]
     low = dot(
         jnp.concatenate([jnp.concatenate(x[0:2], axis=1), jnp.concatenate(x[1:3], axis=1)], axis=0),
-        wt[deep:],
+        temporal_taps(weight, (1, 2)),
     )
     high = dot(
         jnp.concatenate([jnp.concatenate(x[3:5], axis=1), jnp.concatenate(x[4:6], axis=1)], axis=0),
-        wt[: 2 * deep],
+        temporal_taps(weight, (0, 1)),
     )
     outer = jnp.dot(
         jnp.concatenate([x[0], x[5]], axis=0),
-        jnp.concatenate([wt[:deep], wt[2 * deep :]], axis=1),
+        jnp.concatenate([temporal_taps(weight, (b,)) for b in (0, 2)], axis=1),
         preferred_element_type=jnp.float32,
     )
     upper, lower = column_taps(outer[:, :deep]), column_taps(outer[:, deep:])
@@ -122,12 +136,10 @@
     far = inside(place, high[:pitch] + lower[pitch:], rows - 2, frames, span).astype(jnp.bfloat16)
     t_edge[0], t_edge[1] = near, far
 
-    even = place[0] == 1
-    up = (far, last.astype(jnp.bfloat16), after.astype(jnp.bfloat16))
-    down = (near, first.astype(jnp.bfloat16), before.astype(jnp.bfloat16))
-    for i in range(3):
-        send_a[i] = jnp.where(even, up[i], down[i])
-        send_b[i] = jnp.where(even, down[i], up[i])
+    for i, value in enumerate((far, last.astype(jnp.bfloat16), after.astype(jnp.bfloat16))):
+        send_up[i] = value
+    for i, value in enumerate((near, first.astype(jnp.bfloat16), before.astype(jnp.bfloat16))):
+        send_down[i] = value
 
 
 def crop(value, frames, span):
@@ -135,7 +147,37 @@
     return value.reshape(shape)[:, :, HALO : span - HALO].astype(jnp.bfloat16)
 
 
-def inner_kernel(place, own, weight, t_edge, w_first, w_second, t_mid, h_mid, o_mid, xs, tall, wt, w1, w2):
+def dot_taps(lhs, rhs):
+    lhs = jnp.concatenate([jnp.concatenate(blocks, axis=1) for blocks in lhs], axis=0)
+    return column_taps(jnp.dot(lhs, rhs, preferred_element_type=jnp.float32))
+
+
+def split_rows(value, pitch):
+    return [value[at : at + pitch] for at in range(0, value.shape[0], pitch)]
+
+
+def known_rows(first, second, before_last, last, weight):
+    pitch, chans = first.shape
+    none = jnp.zeros_like(first)
+    top = dot_taps([[none, first], [first, second]], weight[chans:])
+    end = dot_taps([[before_last, last], [last, none]], weight[: 2 * chans])
+    return split_rows(top, pitch) + split_rows(end, pitch)
+
+
+def outer_rows(top, end, weight, known):
+    pitch, chans = top[0].shape
+    none = jnp.zeros_like(top[0])
+    first, last = split_rows(dot_taps([top, end], weight[...]), pitch)
+    near = split_rows(dot_taps([top[1:], [top[2], none]], weight[: 2 * chans]), pitch)
+    far = split_rows(dot_taps([[none, end[0]], end[:2]], weight[chans:]), pitch)
+    inner = [value + known[i] for i, value in enumerate(near + far)]
+    return [first, *inner, last]
+
+
+def inner_kernel(
+    place, own, weight, t_edge, w_first, w_second, known_h, known_o, o_mid, w1, w2,
+    xs, tall, hs, wt,
+):
     frames, span = own.shape[0], own.shape[4]
     rows = own.shape[1] * own.shape[3]
     pitch = frames * span
@@ -148,75 +190,56 @@
         [xs[a, b * pitch : (b + rows - 4) * pitch] for b in range(3) for a in range(3)], axis=1
     )
     sums = column_taps(jnp.dot(lhs, wt[...], preferred_element_type=jnp.float32))
-    middle = inside(place, sums, 2, frames, span).astype(jnp.bfloat16)
-    t_mid[...] = middle
+
     tall[:pitch] = t_edge[0]
-    tall[pitch : (rows - 3) * pitch] = middle
+    tall[pitch : (rows - 3) * pitch] = inside(place, sums, 2, frames, span).astype(jnp.bfloat16)
     tall[(rows - 3) * pitch :] = t_edge[1]
-
+    inner = rows - 4
     sums = column_taps(
-        jnp.dot(row_taps(tall, 0, rows - 4, pitch), w1[...], preferred_element_type=jnp.float32)
-    )
-    active = sums * (0.5 * jnp.tanh(0.5 * sums) + 0.5)
-    h_mid[...] = inside(place, active, 2, frames, span).astype(jnp.bfloat16)
+        jnp.dot(row_taps(tall, 0, inner, pitch), w1[...], preferred_element_type=jnp.float32)
+    )
+    hs[...] = inside(place, silu(sums), 2, frames, span).astype(jnp.bfloat16)
+    temporal = [rows_of(tall, i, 1, pitch) for i in (0, 1, inner, inner + 1)]
+    for i, value in enumerate(known_rows(*temporal, w1)):
+        known_h[i] = value
 
     sums = column_taps(
-        jnp.dot(row_taps(h_mid, 0, rows - 6, pitch), w2[...], preferred_element_type=jnp.float32)
-    )
-    sums = sums + rows_of(t_mid, 1, rows - 6, pitch).astype(jnp.float32)
+        jnp.dot(row_taps(hs, 0, inner - 2, pitch), w2[...], preferred_element_type=jnp.float32)
+    )
+    sums = sums + rows_of(tall, 2, inner - 2, pitch).astype(jnp.float32)
     o_mid[...] = crop(sums, frames, span)
-
-
-def outer_kernel(
-    frames, place, t_edge, edges, t_mid, h_mid, o_mid, swap_a, swap_b, w_first, w_second,
-    out, tall, hs, w1, w2,
-):
+    hidden = [rows_of(hs, i, 1, pitch) for i in (0, 1, inner - 2, inner - 1)]
+    for i, value in enumerate(known_rows(*hidden, w2)):
+        known_o[i] = value + temporal[i].astype(jnp.float32)
+
+
+def outer_kernel(frames, place, edges, known_h, known_o, o_mid, below, above, w1, w2, out):
     rows = out.shape[0] * out.shape[2]
-    pitch = t_edge.shape[1]
+    pitch = edges.shape[1]
     span = pitch // frames
-    plane_weight_to(w1, w_first)
-    plane_weight_to(w2, w_second)
-
-    even = place[0] == 1
-
-    def above(i):
-        return jnp.where(even, swap_b[i], swap_a[i]).astype(jnp.float32)
-
-    def below(i):
-        return jnp.where(even, swap_a[i], swap_b[i]).astype(jnp.float32)
-
-    def fill(at, row, value):
-        value = inside(place, value, row, frames, span)
-        tall[at * pitch : (at + 1) * pitch] = value.astype(jnp.bfloat16)
-
-    fill(0, -2, above(0))
-    fill(1, -1, above(1) + edges[2])
-    fill(2, 0, above(2) + edges[0])
-    tall[3 * pitch : 4 * pitch] = t_edge[0]
-    tall[4 * pitch : 5 * pitch] = rows_of(t_mid, 0, 1, pitch)
-    tall[5 * pitch : 6 * pitch] = rows_of(t_mid, rows - 5, 1, pitch)
-    tall[6 * pitch : 7 * pitch] = t_edge[1]
-    fill(7, rows - 1, below(2) + edges[1])
-    fill(8, rows, below(1) + edges[3])
-    fill(9, rows + 1, below(0))
-
-    lhs = jnp.concatenate([row_taps(tall, s, 3, pitch) for s in (0, 5)], axis=0)
-    sums = column_taps(jnp.dot(lhs, w1[...], preferred_element_type=jnp.float32))
-    active = sums * (0.5 * jnp.tanh(0.5 * sums) + 0.5)
-    half = 3 * pitch
-    hs[:half] = inside(place, active[:half], -1, frames, span).astype(jnp.bfloat16)
-    hs[half : 5 * pitch] = rows_of(h_mid, 0, 2, pitch)
-    hs[5 * pitch : 7 * pitch] = rows_of(h_mid, rows - 6, 2, pitch)
-    hs[7 * pitch :] = inside(place, active[half:], rows - 2, frames, span).astype(jnp.bfloat16)
-
-    lhs = jnp.concatenate([row_taps(hs, s, 3, pitch) for s in (0, 5)], axis=0)
-    sums = column_taps(jnp.dot(lhs, w2[...], preferred_element_type=jnp.float32))
-    skip = jnp.concatenate([rows_of(tall, s, 3, pitch) for s in (2, 5)], axis=0)
-    done = crop(sums + skip.astype(jnp.float32), frames, span)
-    for i in range(3):
-        out[i // 2, :, i % 2] = done[i]
-        row = rows - 3 + i
-        out[row // 2, :, row % 2] = done[3 + i]
+
+    def shown(value, row):
+        return inside(place, value, row, frames, span).astype(jnp.bfloat16)
+
+    top = [
+        shown(above[0].astype(jnp.float32), -2),
+        shown(above[1] + edges[2], -1),
+        shown(above[2] + edges[0], 0),
+    ]
+    end = [
+        shown(below[2] + edges[1], rows - 1),
+        shown(below[1] + edges[3], rows),
+        shown(below[0].astype(jnp.float32), rows + 1),
+    ]
+    sums = outer_rows(top, end, w1, known_h)
+    places = (-1, 0, 1, rows - 2, rows - 1, rows)
+    hidden = [shown(silu(value), row) for value, row in zip(sums, places)]
+
+    sums = outer_rows(hidden[:3], hidden[3:], w2, known_o)
+    sums[0] = sums[0] + top[2].astype(jnp.float32)
+    sums[5] = sums[5] + end[0].astype(jnp.float32)
+    for value, row in zip(sums, (0, 1, 2, rows - 3, rows - 2, rows - 1)):
+        out[row // 2, :, row % 2] = crop(value, frames, span)[0]
     for row in range(3, rows - 3):
         out[row // 2, :, row % 2] = o_mid[row - 3]
 
@@ -234,7 +257,6 @@
     plane = slab // SLABS
     place = jnp.stack(
         [
-            (plane % 2 == 0).astype(jnp.int32),
             (column * SLABS + slab % SLABS) * width - HALO,
             plane * plane_rows,
             jnp.int32(col_count),
@@ -264,7 +286,7 @@
         cut, ("tm", "rows"), split_axis=0, concat_axis=0, tiled=True, axis_index_groups=members
     ).reshape(tm, SLABS, frame_count, row_count, span, chans)
 
-    t_edge, edges, send_a, send_b = pl.pallas_call(
+    t_edge, edges, send_down, send_up = pl.pallas_call(
         edge_kernel,
         out_shape=[
             brain(2, pitch, chans),
@@ -274,38 +296,33 @@
         ],
         in_specs=[smem, vmem, vmem],
         out_specs=[vmem] * 4,
-        scratch_shapes=[held(3, 6 * pitch, chans), held(9 * chans, 3 * chans)],
+        scratch_shapes=[held(3, 6 * pitch, chans)],
         compiler_params=params,
         name="edge",
     )(place, own, temporal_weight)
 
-    def swap(parity):
-        pairs = []
-        for z in range(parity, planes - 1, 2):
-            for j in range(SLABS):
-                low, high = z * SLABS + j, (z + 1) * SLABS + j
-                pairs += [(low, high), (high, low)]
-        return pairs
-
-    swap_a = lax.ppermute(send_a, "rows", swap(0))
-    swap_b = lax.ppermute(send_b, "rows", swap(1))
+    reach = range(slabs - SLABS)
+    above = lax.ppermute(send_up, "rows", [(r, r + SLABS) for r in reach])
+    below = lax.ppermute(send_down, "rows", [(r + SLABS, r) for r in reach])
 
     inner = plane_rows - 4
-    t_mid, h_mid, o_mid = pl.pallas_call(
+    partial = jax.ShapeDtypeStruct((4, pitch, chans), jnp.float32)
+    known_h, known_o, o_mid, w1, w2 = pl.pallas_call(
         inner_kernel,
         out_shape=[
-            brain(inner * pitch, chans),
-            brain(inner * pitch, chans),
+            partial,
+            partial,
             brain(inner - 2, tm, width, chans),
+            brain(3 * chans, 3 * chans),
+            brain(3 * chans, 3 * chans),
         ],
         in_specs=[smem] + [vmem] * 5,
-        out_specs=[vmem] * 3,
+        out_specs=[vmem] * 5,
         scratch_shapes=[
             held(3, (inner + 2) * pitch, chans),
             held((inner + 2) * pitch, chans),
+            held(inner * pitch, chans),
             held(9 * chans, 3 * chans),
-            held(3 * chans, 3 * chans),
-            held(3 * chans, 3 * chans),
         ],
         compiler_params=params,
         cost_estimate=pl.CostEstimate(flops=10**9, bytes_accessed=4 * 10**6, transcendentals=10**5),
@@ -314,17 +331,11 @@
     encoded = pl.pallas_call(
         lambda *refs: outer_kernel(tm, *refs),
         out_shape=brain(SLABS, tm, row_count, width, chans),
-        in_specs=[smem] + [vmem] * 9,
+        in_specs=[smem] + [vmem] * 8,
         out_specs=vmem,
-        scratch_shapes=[
-            held(10 * pitch, chans),
-            held(10 * pitch, chans),
-            held(3 * chans, 3 * chans),
-            held(3 * chans, 3 * chans),
-        ],
         compiler_params=params,
         name="outer",
-    )(place, t_edge, edges, t_mid, h_mid, o_mid, swap_a, swap_b, first_weight, second_weight)
+    )(place, edges, known_h, known_o, o_mid, below, above, w1, w2)
 
     groups = [[z * SLABS + j for j in range(SLABS)] for z in range(planes)]
     encoded = lax.all_to_all(

time: 50.7 us -> 50.1 us (0.988)
  the two profiles are of different devices: /device:TPU:96 before, /device:TPU:384 now
where the time goes in v4:
time: 50.1 us; the launch traced here: 49.8 us
  blocking collectives  31.8 us (63%)
  Pallas kernels  6.32 us (13%)
  starting transfers between devices  6.04 us (12%)
  waiting for transfers between devices  3.74 us (7%)
  local copies, waits for them, and re-layouts  1.79 us (4%)
    all_to_all x1, blocking collectives, per_device(): lax.all_to_all(cut, ('tm', 'rows'), split_axis=0, concat_axis=0, tiled=Tr...  21.9 us
    all_to_all x1, blocking collectives, per_device(): lax.all_to_all(encoded, 'rows', split_axis=0, concat_axis=0, tiled=True,...  9.93 us
    ppermute x1, starting transfers between devices, per_device(): below = lax.ppermute(send_down, 'rows', [(r + SLABS, r) for r in reach])  4.12 us
    ppermute x1, waiting for transfers between devices, per_device(): above = lax.ppermute(send_up, 'rows', [(r, r + SLABS) for r in reach])  3.74 us
    pallas_call x1, Pallas kernels, per_device(): pl.pallas_call(inner_kernel, out_shape=[partial, partial, brain(inner - 2...  2.89 us
    ppermute x1, starting transfers between devices, per_device(): above = lax.ppermute(send_up, 'rows', [(r, r + SLABS) for r in reach])  1.92 us
    pallas_call x1, Pallas kernels, per_device(): pl.pallas_call(edge_kernel, out_shape=[brain(2, pitch, chans), jax.ShapeD...  1.68 us
    pallas_call x1, Pallas kernels, per_device(): pl.pallas_call(lambda *refs: outer_kernel(tm, *refs), out_shape=brain(SLA...  1.62 us
  transfers between devices with their start and end apart: 2, of which 1 were waited for; matrix products, arithmetic and copies ran while one was open for 0% of the time, Pallas kernels for 6%

profile of v4, /device:TPU:384, one launch (start us, length us, event | category | flops | bytes accessed | tf_op | source)
XLA Modules:
  0.0 49.8 jit_solution(14055032807412940907)
XLA Ops:
  0.0 0.1 pad_add_fusion.place.refs_0_
  0.1 0.0 copy-start.1
  0.1 1.0 %copy-done.1 = bf16[2,2,512,128]{3,2,1,0:T(8,128)(2,1)S(1)} copy-done((bf16[2,2,512,128]{3,2,1,0:T(8,128)(2,1)S(1)}, bf16[2,2,512,128]{3,2,1,0:T(8,128)(2,1)}, u32[]{:S(2)}) %copy-start.1) | copy-done | bytes 524312
  1.1 0.1 windows.1
  1.3 0.0 copy-start
  1.3 21.9 %all_to_all.10 = bf16[32,2,2,24,128]{4,3,2,1,0:T(8,128)(2,1)S(1)} all-to-all(bf16[32,2,2,24,128]{4,3,2,1,0:T(8,128)(2,1)S(1)} %windows.1), channel_id=1, replica_groups={{0,1,2,3,64,65,66,67,128,129,130,131,192,193,194,195,256,257,258,259,32..., dimensions={0} | all-to-all | bytes 1572864 | tf_op jit(solution)/shard_map/all_to_all | solution.py:285
  23.1 0.0 copy-done
  23.1 0.0 copy-start.2
  23.1 0.0 copy-start.3
  23.1 1.7 %edge.1 = (bf16[2,192,128]{2,1,0:T(8,128)(2,1)S(1)}, f32[4,192,128]{2,1,0:T(8,128)S(1)}, bf16[3,192,128]{2,1,0:T(8,128)(2,1)S(1)}, bf16[3,192,128]{2,1,0:T(8,128)(2,1)S(1)}) custom-call(s32[4]{0:T(128)S(1)} %pad_add_fusion.place.refs_0_, bf16[8,4,2,2,24,128]{5,4,3,2,1,0:T(8,128)(2,1)S(1)} %bitcast.5, bf16[3,3,3,128,128]{4,3,2,1,0:T(8,128)(2,1)S(1)} %copy-done), custom_call_target="tpu_custom_call" | custom-call | tf_op jit(solution)/shard_map/edge/pallas_call | solution.py:289
  24.8 4.1 %collective-permute-start = (bf16[3,192,128]{2,1,0:T(8,128)(2,1)S(1)}, bf16[3,192,128]{2,1,0:T(8,128)(2,1)S(1)}, u32[]{:S(2)}, u32[]{:S(2)}) collective-permute-start(bf16[3,192,128]{2,1,0:T(8,128)(2,1)S(1)} %get-tuple-element.23), channel_id=1, source_target_pairs={{4,0},{5,1},{6,2},{7,3},{8,4},{9,5},{10,6},{11,7},{12,8},{13,9},{1... | collective-permute-start | bytes 442376 | tf_op jit(solution)/shard_map/ppermute | solution.py:306
  29.0 1.9 %collective-permute-start.1 = (bf16[3,192,128]{2,1,0:T(8,128)(2,1)S(1)}, bf16[3,192,128]{2,1,0:T(8,128)(2,1)S(1)}, u32[]{:S(2)}, u32[]{:S(2)}) collective-permute-start(bf16[3,192,128]{2,1,0:T(8,128)(2,1)S(1)} %get-tuple-element.24), channel_id=1, source_target_pairs={{0,4},{1,5},{2,6},{3,7},{4,8},{5,9},{6,10},{7,11},{8,12},{9,13},{1... | collective-permute-start | bytes 442376 | tf_op jit(solution)/shard_map/ppermute | solution.py:305
  30.9 0.0 copy-done.2
  30.9 0.0 copy-done.3
  30.9 2.9 %inner.1 = (f32[4,192,128]{2,1,0:T(8,128)S(1)}, f32[4,192,128]{2,1,0:T(8,128)S(1)}, bf16[2,8,16,128]{3,2,1,0:T(8,128)(2,1)S(1)}, bf16[384,384]{1,0:T(8,128)(2,1)S(1)}, bf16[384,384]{1,0:T(8,128)(2,1)S(1)}) custom-call(s32[4]{0:T(128)S(1)} %pad_add_fusion.place.refs_0_, bf16[8,4,2,2,24,128]{5,4,3,2,1,0:T(8,128)(2,1)S(1)} %bitcast.6, ...), custom_call_target="tpu_custom_call" | custom-call | flops 1000000000 | bytes 4000000 | tf_op jit(solution)/shard_map/inner/pallas_call | solution.py:310
  33.8 0.0 collective-permute-done.refs_5_
  33.8 3.7 %collective-permute-done.1.refs_6_ = bf16[3,192,128]{2,1,0:T(8,128)(2,1)S(1)} collective-permute-done((bf16[3,192,128]{2,1,0:T(8,128)(2,1)S(1)}, bf16[3,192,128]{2,1,0:T(8,128)(2,1)S(1)}, u32[]{:S(2)}, u32[]{:S(2)}) %collective-permute-start.1) | collective-permute-done | bytes 147488 | tf_op jit(solution)/shard_map/ppermute | solution.py:305
  37.6 1.6 %outer.1 = bf16[4,8,2,16,128]{4,3,2,1,0:T(8,128)(2,1)S(1)} custom-call(s32[4]{0:T(128)S(1)} %pad_add_fusion.place.refs_0_, f32[4,192,128]{2,1,0:T(8,128)S(1)} %get-tuple-element.18.refs_1_, f32[4,192,128]{2,1,0:T(8,128)S(1)} %get-tuple-element.20.refs_2_, f32[4,192,128]{2,1,0:T(8,128)S(1)} %get-tuple-element.21.refs_3_, ...), custom_call_target="tpu_custom_call" | custom-call | tf_op jit(solution)/shard_map/outer/pallas_call | solution.py:331
  39.2 9.9 %all_to_all.11 = bf16[4,8,2,16,128]{4,3,2,1,0:T(8,128)(2,1)S(1)} all-to-all(bf16[4,8,2,16,128]{4,3,2,1,0:T(8,128)(2,1)S(1)} %outer.1), channel_id=1, replica_groups={{0,1,2,3},{4,5,6,7},{8,9,10,11},{12,13,14,15},{16,17,18,19},{20,21,22,2..., dimensions={0} | all-to-all | bytes 524288 | tf_op jit(solution)/shard_map/all_to_all | solution.py:341
  49.1 0.7 %copy.5 = bf16[8,2,4,16,128]{4,3,2,1,0:T(8,128)(2,1)} copy(bf16[8,2,4,16,128]{4,3,1,0,2:T(8,128)(2,1)S(1)} %bitcast.7) | data formatting | bytes 524288 | tf_op jit(solution)/shard_map/transpose | solution.py:344
Async XLA Ops:
  0.1 1.0 %copy-start.1 = (bf16[2,2,512,128]{3,2,1,0:T(8,128)(2,1)S(1)}, bf16[2,2,512,128]{3,2,1,0:T(8,128)(2,1)}, u32[]{:S(2)}) copy-start(bf16[2,2,512,128]{3,2,1,0:T(8,128)(2,1)} %frames) | copy-start | bytes 1572868
  1.3 21.9 %copy-start = (bf16[3,3,3,128,128]{4,3,2,1,0:T(8,128)(2,1)S(1)}, bf16[3,3,3,128,128]{4,3,2,1,0:T(8,128)(2,1)}, u32[]{:S(2)}) copy-start(bf16[3,3,3,128,128]{4,3,2,1,0:T(8,128)(2,1)} %weight.3) | copy-start | bytes 2654212
  23.1 7.7 %copy-start.2 = (bf16[3,3,128,128]{3,2,1,0:T(8,128)(2,1)S(1)}, bf16[3,3,128,128]{3,2,1,0:T(8,128)(2,1)}, u32[]{:S(2)}) copy-start(bf16[3,3,128,128]{3,2,1,0:T(8,128)(2,1)} %w_first.1) | copy-start | bytes 884740
  23.1 7.8 %copy-start.3 = (bf16[3,3,128,128]{3,2,1,0:T(8,128)(2,1)S(1)}, bf16[3,3,128,128]{3,2,1,0:T(8,128)(2,1)}, u32[]{:S(2)}) copy-start(bf16[3,3,128,128]{3,2,1,0:T(8,128)(2,1)} %w_second.1) | copy-start | bytes 884740
  24.8 9.0 %collective-permute-start = (bf16[3,192,128]{2,1,0:T(8,128)(2,1)S(1)}, bf16[3,192,128]{2,1,0:T(8,128)(2,1)S(1)}, u32[]{:S(2)}, u32[]{:S(2)}) collective-permute-start(bf16[3,192,128]{2,1,0:T(8,128)(2,1)S(1)} %get-tuple-element.23), channel_id=1, source_target_pairs={{4,0},{5,1},{6,2},{7,3},{8,4},{9,5},{10,6},{11,7},{12,8},{13,9},{1... | collective-permute-start | bytes 442376 | tf_op jit(solution)/shard_map/ppermute | solution.py:306
  29.0 8.6 %collective-permute-start.1 = (bf16[3,192,128]{2,1,0:T(8,128)(2,1)S(1)}, bf16[3,192,128]{2,1,0:T(8,128)(2,1)S(1)}, u32[]{:S(2)}, u32[]{:S(2)}) collective-permute-start(bf16[3,192,128]{2,1,0:T(8,128)(2,1)S(1)} %get-tuple-element.24), channel_id=1, source_target_pairs={{0,4},{1,5},{2,6},{3,7},{4,8},{5,9},{6,10},{7,11},{8,12},{9,13},{1... | collective-permute-start | bytes 442376 | tf_op jit(solution)/shard_map/ppermute | solution.py:305

commit v5 on v4

--- a/solution.py
+++ b/solution.py
@@ -28,19 +28,10 @@
     return mid + pltpu.roll(left, 1, 0) + pltpu.roll(right, sums.shape[0] - 1, 0)
 
 
-def inside(place, value, row, frames, span):
-    first_col, first_row, last_col, last_row = place[0], place[1], place[2], place[3]
-    count, chans = value.shape[0] // (frames * span), value.shape[1]
-    col = lax.broadcasted_iota(jnp.int32, (span, chans), 0) + first_col
-    keep = (col >= 0) & (col < last_col)
-    value = jnp.where(keep[None], value.reshape(count * frames, span, chans), 0.0)
-    value = value.reshape(count, frames * span, chans)
-    kept = []
-    for i in range(count):
-        r = first_row + row + i
-        shown = jnp.where((r >= 0) & (r < last_row), 1.0, 0.0) if row + i < 0 or row + i >= 8 else None
-        kept.append(value[i] if shown is None else value[i] * shown)
-    return jnp.concatenate(kept, axis=0)
+def inside(value, mask):
+    rows, chans = value.shape
+    shown = value.reshape(rows // mask.shape[0], *mask.shape) * mask[...][None]
+    return shown.reshape(rows, chans)
 
 
 def temporal_weight_to(wt, weight):
@@ -98,7 +89,7 @@
     )
 
 
-def edge_kernel(place, own, weight, t_edge, edges, send_down, send_up, xs):
+def edge_kernel(masks, own, weight, t_edge, edges, send_down, send_up, xs):
     frames, span, chans = own.shape[0], own.shape[4], own.shape[5]
     rows = own.shape[1] * own.shape[3]
     pitch = frames * span
@@ -132,8 +123,8 @@
     first, last = low[:pitch], high[pitch:]
     before, after = lower[:pitch], upper[pitch:]
     edges[0], edges[1], edges[2], edges[3] = first, last, before, after
-    near = inside(place, low[pitch:] + upper[:pitch], 1, frames, span).astype(jnp.bfloat16)
-    far = inside(place, high[:pitch] + lower[pitch:], rows - 2, frames, span).astype(jnp.bfloat16)
+    near = inside(low[pitch:] + upper[:pitch], masks[0]).astype(jnp.bfloat16)
+    far = inside(high[:pitch] + lower[pitch:], masks[0]).astype(jnp.bfloat16)
     t_edge[0], t_edge[1] = near, far
 
     for i, value in enumerate((far, last.astype(jnp.bfloat16), after.astype(jnp.bfloat16))):
@@ -175,7 +166,7 @@
 
 
 def inner_kernel(
-    place, own, weight, t_edge, w_first, w_second, known_h, known_o, o_mid, w1, w2,
+    masks, own, weight, t_edge, w_first, w_second, known_h, known_o, o_mid, w1, w2,
     xs, tall, hs, wt,
 ):
     frames, span = own.shape[0], own.shape[4]
@@ -192,13 +183,13 @@
     sums = column_taps(jnp.dot(lhs, wt[...], preferred_element_type=jnp.float32))
 
     tall[:pitch] = t_edge[0]
-    tall[pitch : (rows - 3) * pitch] = inside(place, sums, 2, frames, span).astype(jnp.bfloat16)
+    tall[pitch : (rows - 3) * pitch] = inside(sums, masks[0]).astype(jnp.bfloat16)
     tall[(rows - 3) * pitch :] = t_edge[1]
     inner = rows - 4
     sums = column_taps(
         jnp.dot(row_taps(tall, 0, inner, pitch), w1[...], preferred_element_type=jnp.float32)
     )
-    hs[...] = inside(place, silu(sums), 2, frames, span).astype(jnp.bfloat16)
+    hs[...] = inside(silu(sums), masks[0]).astype(jnp.bfloat16)
     temporal = [rows_of(tall, i, 1, pitch) for i in (0, 1, inner, inner + 1)]
     for i, value in enumerate(known_rows(*temporal, w1)):
         known_h[i] = value
@@ -213,13 +204,14 @@
         known_o[i] = value + temporal[i].astype(jnp.float32)
 
 
-def outer_kernel(frames, place, edges, known_h, known_o, o_mid, below, above, w1, w2, out):
+def outer_kernel(frames, masks, edges, known_h, known_o, o_mid, below, above, w1, w2, out):
     rows = out.shape[0] * out.shape[2]
     pitch = edges.shape[1]
     span = pitch // frames
 
     def shown(value, row):
-        return inside(place, value, row, frames, span).astype(jnp.bfloat16)
+        mask = masks[1] if row < 0 else masks[2] if row >= rows else masks[0]
+        return inside(value, mask).astype(jnp.bfloat16)
 
     top = [
         shown(above[0].astype(jnp.float32), -2),
@@ -255,16 +247,13 @@
     pitch = tm * span
     column, slab = lax.axis_index("tm"), lax.axis_index("rows")
     plane = slab // SLABS
-    place = jnp.stack(
-        [
-            (column * SLABS + slab % SLABS) * width - HALO,
-            plane * plane_rows,
-            jnp.int32(col_count),
-            jnp.int32(slabs * row_count),
-        ]
-    ).astype(jnp.int32)
-    frames_in, place = lax.optimization_barrier((frames_in, place))
-    vmem, smem = pl.BlockSpec(memory_space=pltpu.VMEM), pl.BlockSpec(memory_space=pltpu.SMEM)
+    first_col = (column * SLABS + slab % SLABS) * width - HALO
+    col = lax.broadcasted_iota(jnp.int32, (3, span, chans), 1) + first_col
+    part = lax.broadcasted_iota(jnp.int32, (3, span, chans), 0)
+    shown = (col >= 0) & (col < col_count)
+    shown &= ((part != 1) | (plane > 0)) & ((part != 2) | (plane < planes - 1))
+    masks = shown.astype(jnp.float32)
+    vmem = pl.BlockSpec(memory_space=pltpu.VMEM)
     params = pltpu.CompilerParams(vmem_limit_bytes=VMEM_BYTES)
 
     def brain(*shape):
@@ -281,6 +270,7 @@
         compiler_params=params,
         name="windows",
     )(frames_in)
+    cut, masks = lax.optimization_barrier((cut, masks))
     members = [[m * slabs + z * SLABS + j for m in range(tm) for j in range(SLABS)] for z in range(planes)]
     own = lax.all_to_all(
         cut, ("tm", "rows"), split_axis=0, concat_axis=0, tiled=True, axis_index_groups=members
@@ -294,12 +284,12 @@
             brain(3, pitch, chans),
             brain(3, pitch, chans),
         ],
-        in_specs=[smem, vmem, vmem],
+        in_specs=[vmem] * 3,
         out_specs=[vmem] * 4,
         scratch_shapes=[held(3, 6 * pitch, chans)],
         compiler_params=params,
         name="edge",
-    )(place, own, temporal_weight)
+    )(masks, own, temporal_weight)
 
     reach = range(slabs - SLABS)
     above = lax.ppermute(send_up, "rows", [(r, r + SLABS) for r in reach])
@@ -316,7 +306,7 @@
             brain(3 * chans, 3 * chans),
             brain(3 * chans, 3 * chans),
         ],
-        in_specs=[smem] + [vmem] * 5,
+        in_specs=[vmem] * 6,
         out_specs=[vmem] * 5,
         scratch_shapes=[
             held(3, (inner + 2) * pitch, chans),
@@ -327,15 +317,15 @@
         compiler_params=params,
         cost_estimate=pl.CostEstimate(flops=10**9, bytes_accessed=4 * 10**6, transcendentals=10**5),
         name="inner",
-    )(place, own, temporal_weight, t_edge, first_weight, second_weight)
+    )(masks, own, temporal_weight, t_edge, first_weight, second_weight)
     encoded = pl.pallas_call(
         lambda *refs: outer_kernel(tm, *refs),
         out_shape=brain(SLABS, tm, row_count, width, chans),
-        in_specs=[smem] + [vmem] * 8,
+        in_specs=[vmem] * 9,
         out_specs=vmem,
         compiler_params=params,
         name="outer",
-    )(place, edges, known_h, known_o, o_mid, below, above, w1, w2)
+    )(masks, edges, known_h, known_o, o_mid, below, above, w1, w2)
 
     groups = [[z * SLABS + j for j in range(SLABS)] for z in range(planes)]
     encoded = lax.all_to_all(

time: 50.1 us -> 49 us (0.978)
  Pallas kernels: 6.32 us -> 4.68 us
  waiting for transfers between devices: 3.74 us -> 4.28 us
    pallas_call x1, Pallas kernels: 1.62 us -> 1.06 us  [per_device(): pl.pallas_call(lambda *refs: outer_kernel(tm, *refs), out_shape=brain(SLA...]
    pallas_call x1, Pallas kernels: 2.89 us -> 2.34 us  [per_device(): pl.pallas_call(inner_kernel, out_shape=[partial, partial, brain(inner - 2...]
    ppermute x1, waiting for transfers between devices: 3.74 us -> 4.28 us  [per_device(): above = lax.ppermute(send_up, 'rows', [(r, r + SLABS) for r in reach])]
    pallas_call x1, Pallas kernels: 1.68 us -> 1.14 us  [per_device(): pl.pallas_call(edge_kernel, out_shape=[brain(2, pitch, chans), jax.ShapeD...]
  transfers between devices with their start and end apart: 2 -> 2, of which waited for: 1 -> 1; matrix products, arithmetic and copies ran while one was open for 0% -> 0% of each run, Pallas kernels for 6% -> 5%
where the time goes in v5:
time: 49 us; the launch traced here: 48.8 us
  blocking collectives  31.8 us (65%)
  starting transfers between devices  6.05 us (12%)
  Pallas kernels  4.68 us (10%)
  waiting for transfers between devices  4.28 us (9%)
  local copies, waits for them, and re-layouts  1.78 us (4%)
    all_to_all x1, blocking collectives, per_device(): lax.all_to_all(cut, ('tm', 'rows'), split_axis=0, concat_axis=0, tiled=Tr...  21.9 us
    all_to_all x1, blocking collectives, per_device(): lax.all_to_all(encoded, 'rows', split_axis=0, concat_axis=0, tiled=True,...  9.93 us
    ppermute x1, waiting for transfers between devices, per_device(): above = lax.ppermute(send_up, 'rows', [(r, r + SLABS) for r in reach])  4.28 us
    ppermute x1, starting transfers between devices, per_device(): below = lax.ppermute(send_down, 'rows', [(r + SLABS, r) for r in reach])  4.13 us
    pallas_call x1, Pallas kernels, per_device(): pl.pallas_call(inner_kernel, out_shape=[partial, partial, brain(inner - 2...  2.34 us
    ppermute x1, starting transfers between devices, per_device(): above = lax.ppermute(send_up, 'rows', [(r, r + SLABS) for r in reach])  1.92 us
    pallas_call x1, Pallas kernels, per_device(): pl.pallas_call(edge_kernel, out_shape=[brain(2, pitch, chans), jax.ShapeD...  1.14 us
    pallas_call x1, Pallas kernels, per_device(): pl.pallas_call(lambda *refs: outer_kernel(tm, *refs), out_shape=brain(SLA...  1.06 us
  transfers between devices with their start and end apart: 2, of which 1 were waited for; matrix products, arithmetic and copies ran while one was open for 0% of the time, Pallas kernels for 5%

profile of v5, /device:TPU:384, one launch (start us, length us, event | category | flops | bytes accessed | tf_op | source)
XLA Modules:
  0.0 48.8 jit_solution(3107236970791156177)
XLA Ops:
  0.0 0.0 copy-start.1
  0.0 1.0 %copy-done.1 = bf16[2,2,512,128]{3,2,1,0:T(8,128)(2,1)S(1)} copy-done((bf16[2,2,512,128]{3,2,1,0:T(8,128)(2,1)S(1)}, bf16[2,2,512,128]{3,2,1,0:T(8,128)(2,1)}, u32[]{:S(2)}) %copy-start.1) | copy-done | bytes 524312
  1.1 0.1 windows.1
  1.2 0.0 copy-start
  1.2 0.1 and_convert_fusion.masks.refs_0_
  1.3 21.9 %all_to_all.10 = bf16[32,2,2,24,128]{4,3,2,1,0:T(8,128)(2,1)S(1)} all-to-all(bf16[32,2,2,24,128]{4,3,2,1,0:T(8,128)(2,1)S(1)} %windows.1), channel_id=1, replica_groups={{0,1,2,3,64,65,66,67,128,129,130,131,192,193,194,195,256,257,258,259,32..., dimensions={0} | all-to-all | bytes 1572864 | tf_op jit(solution)/shard_map/all_to_all | solution.py:275
  23.2 0.0 copy-done
  23.2 0.0 copy-start.2
  23.2 0.0 copy-start.3
  23.2 1.1 %edge.1 = (bf16[2,192,128]{2,1,0:T(8,128)(2,1)S(1)}, f32[4,192,128]{2,1,0:T(8,128)S(1)}, bf16[3,192,128]{2,1,0:T(8,128)(2,1)S(1)}, bf16[3,192,128]{2,1,0:T(8,128)(2,1)S(1)}) custom-call(f32[3,24,128]{2,1,0:T(8,128)S(1)} %and_convert_fusion.masks.refs_0_, bf16[8,4,2,2,24,128]{5,4,3,2,1,0:T(8,128)(2,1)S(1)} %bitcast.3, bf16[3,3,3,128,128]{4,3,2,1,0:T(8,128)(2,1)S(1)} %copy-done), custom_call_target="tpu_custom_call" | custom-call | tf_op jit(solution)/shard_map/edge/pallas_call | solution.py:279
  24.3 4.1 %collective-permute-start = (bf16[3,192,128]{2,1,0:T(8,128)(2,1)S(1)}, bf16[3,192,128]{2,1,0:T(8,128)(2,1)S(1)}, u32[]{:S(2)}, u32[]{:S(2)}) collective-permute-start(bf16[3,192,128]{2,1,0:T(8,128)(2,1)S(1)} %get-tuple-element.23), channel_id=1, source_target_pairs={{4,0},{5,1},{6,2},{7,3},{8,4},{9,5},{10,6},{11,7},{12,8},{13,9},{1... | collective-permute-start | bytes 442376 | tf_op jit(solution)/shard_map/ppermute | solution.py:296
  28.4 1.9 %collective-permute-start.1 = (bf16[3,192,128]{2,1,0:T(8,128)(2,1)S(1)}, bf16[3,192,128]{2,1,0:T(8,128)(2,1)S(1)}, u32[]{:S(2)}, u32[]{:S(2)}) collective-permute-start(bf16[3,192,128]{2,1,0:T(8,128)(2,1)S(1)} %get-tuple-element.24), channel_id=1, source_target_pairs={{0,4},{1,5},{2,6},{3,7},{4,8},{5,9},{6,10},{7,11},{8,12},{9,13},{1... | collective-permute-start | bytes 442376 | tf_op jit(solution)/shard_map/ppermute | solution.py:295
  30.4 0.0 copy-done.2
  30.4 0.0 copy-done.3
  30.4 2.3 %inner.1 = (f32[4,192,128]{2,1,0:T(8,128)S(1)}, f32[4,192,128]{2,1,0:T(8,128)S(1)}, bf16[2,8,16,128]{3,2,1,0:T(8,128)(2,1)S(1)}, bf16[384,384]{1,0:T(8,128)(2,1)S(1)}, bf16[384,384]{1,0:T(8,128)(2,1)S(1)}) custom-call(f32[3,24,128]{2,1,0:T(8,128)S(1)} %and_convert_fusion.masks.refs_0_, bf16[8,4,2,2,24,128]{5,4,3,2,1,0:T(8,128)(2,1)S(1)} %bitcast.4, ...), custom_call_target="tpu_custom_call" | custom-call | flops 1000000000 | bytes 4000000 | tf_op jit(solution)/shard_map/inner/pallas_call | solution.py:300
  32.7 0.0 collective-permute-done.refs_5_
  32.7 4.3 %collective-permute-done.1.refs_6_ = bf16[3,192,128]{2,1,0:T(8,128)(2,1)S(1)} collective-permute-done((bf16[3,192,128]{2,1,0:T(8,128)(2,1)S(1)}, bf16[3,192,128]{2,1,0:T(8,128)(2,1)S(1)}, u32[]{:S(2)}, u32[]{:S(2)}) %collective-permute-start.1) | collective-permute-done | bytes 147488 | tf_op jit(solution)/shard_map/ppermute | solution.py:295
  37.0 1.1 %outer.1 = bf16[4,8,2,16,128]{4,3,2,1,0:T(8,128)(2,1)S(1)} custom-call(f32[3,24,128]{2,1,0:T(8,128)S(1)} %and_convert_fusion.masks.refs_0_, f32[4,192,128]{2,1,0:T(8,128)S(1)} %get-tuple-element.18.refs_1_, f32[4,192,128]{2,1,0:T(8,128)S(1)} %get-tuple-element.20.refs_2_, f32[4,192,128]{2,1,0:T(8,128)S(1)} %get-tuple-element.21.refs_3_, ...), custom_call_target="tpu_custom_call" | custom-call | tf_op jit(solution)/shard_map/outer/pallas_call | solution.py:321
  38.1 9.9 %all_to_all.11 = bf16[4,8,2,16,128]{4,3,2,1,0:T(8,128)(2,1)S(1)} all-to-all(bf16[4,8,2,16,128]{4,3,2,1,0:T(8,128)(2,1)S(1)} %outer.1), channel_id=1, replica_groups={{0,1,2,3},{4,5,6,7},{8,9,10,11},{12,13,14,15},{16,17,18,19},{20,21,22,2..., dimensions={0} | all-to-all | bytes 524288 | tf_op jit(solution)/shard_map/all_to_all | solution.py:331
  48.0 0.7 %copy.5 = bf16[8,2,4,16,128]{4,3,2,1,0:T(8,128)(2,1)} copy(bf16[8,2,4,16,128]{4,3,1,0,2:T(8,128)(2,1)S(1)} %bitcast.5) | data formatting | bytes 524288 | tf_op jit(solution)/shard_map/transpose | solution.py:334
  (2 shorter events, 0.0 us)
Async XLA Ops:
  0.0 1.0 %copy-start.1 = (bf16[2,2,512,128]{3,2,1,0:T(8,128)(2,1)S(1)}, bf16[2,2,512,128]{3,2,1,0:T(8,128)(2,1)}, u32[]{:S(2)}) copy-start(bf16[2,2,512,128]{3,2,1,0:T(8,128)(2,1)} %frames.1) | copy-start | bytes 1572868
  1.2 22.0 %copy-start = (bf16[3,3,3,128,128]{4,3,2,1,0:T(8,128)(2,1)S(1)}, bf16[3,3,3,128,128]{4,3,2,1,0:T(8,128)(2,1)}, u32[]{:S(2)}) copy-start(bf16[3,3,3,128,128]{4,3,2,1,0:T(8,128)(2,1)} %weight.3) | copy-start | bytes 2654212
  23.2 7.2 %copy-start.2 = (bf16[3,3,128,128]{3,2,1,0:T(8,128)(2,1)S(1)}, bf16[3,3,128,128]{3,2,1,0:T(8,128)(2,1)}, u32[]{:S(2)}) copy-start(bf16[3,3,128,128]{3,2,1,0:T(8,128)(2,1)} %w_first.1) | copy-start | bytes 884740
  23.2 7.2 %copy-start.3 = (bf16[3,3,128,128]{3,2,1,0:T(8,128)(2,1)S(1)}, bf16[3,3,128,128]{3,2,1,0:T(8,128)(2,1)}, u32[]{:S(2)}) copy-start(bf16[3,3,128,128]{3,2,1,0:T(8,128)(2,1)} %w_second.1) | copy-start | bytes 884740
  24.3 8.4 %collective-permute-start = (bf16[3,192,128]{2,1,0:T(8,128)(2,1)S(1)}, bf16[3,192,128]{2,1,0:T(8,128)(2,1)S(1)}, u32[]{:S(2)}, u32[]{:S(2)}) collective-permute-start(bf16[3,192,128]{2,1,0:T(8,128)(2,1)S(1)} %get-tuple-element.23), channel_id=1, source_target_pairs={{4,0},{5,1},{6,2},{7,3},{8,4},{9,5},{10,6},{11,7},{12,8},{13,9},{1... | collective-permute-start | bytes 442376 | tf_op jit(solution)/shard_map/ppermute | solution.py:296
  28.4 8.6 %collective-permute-start.1 = (bf16[3,192,128]{2,1,0:T(8,128)(2,1)S(1)}, bf16[3,192,128]{2,1,0:T(8,128)(2,1)S(1)}, u32[]{:S(2)}, u32[]{:S(2)}) collective-permute-start(bf16[3,192,128]{2,1,0:T(8,128)(2,1)S(1)} %get-tuple-element.24), channel_id=1, source_target_pairs={{0,4},{1,5},{2,6},{3,7},{4,8},{5,9},{6,10},{7,11},{8,12},{9,13},{1... | collective-permute-start | bytes 442376 | tf_op jit(solution)/shard_map/ppermute | solution.py:295

commit v6 on v5

--- a/solution.py
+++ b/solution.py
@@ -6,20 +6,27 @@
 from jax.sharding import PartitionSpec as P
 
 SLABS = 4
-HALO = 4
+HALO = 3
+PLANE_ROWS = 8
+WIDTH = 16
+SPAN = 24
+KEPT = 20
 VMEM_BYTES = 32 * 1024 * 1024
 
 
 def windows_kernel(frames, out):
-    count, span = out.shape[0], out.shape[3]
-    width = span - 2 * HALO
-    for f in range(out.shape[1]):
-        for r in range(out.shape[2]):
-            row = frames[f, r].astype(jnp.float32)
-            edge = jnp.zeros((HALO, row.shape[1]), jnp.float32)
-            row = jnp.concatenate([edge, row, edge], axis=0)
-            for k in range(count):
-                out[k, f, r] = row[k * width : k * width + span].astype(jnp.bfloat16)
+    count = out.shape[0]
+    parts = [(f, r) for f in range(frames.shape[0]) for r in range(frames.shape[1])]
+    size = out.shape[1] // len(parts)
+    width = size - 2 * HALO
+    padded = []
+    for f, r in parts:
+        row = frames[f, r].astype(jnp.float32)
+        edge = jnp.zeros((HALO, row.shape[1]), jnp.float32)
+        padded.append(jnp.concatenate([edge, row, edge], axis=0))
+    for k in range(count):
+        cut = [row[k * width : k * width + size] for row in padded]
+        out[k] = jnp.concatenate(cut, axis=0).astype(jnp.bfloat16)
 
 
 def column_taps(sums):
@@ -50,20 +57,26 @@
             wt[b * chans : (b + 1) * chans, c * chans : (c + 1) * chans] = weight[b, c]
 
 
-def frames_to(xs, at, own, row):
-    frames, span, chans = own.shape[0], own.shape[4], own.shape[5]
+def frames_to(xs, at, own, row, rows_each):
+    frames, chans = own.shape[0], own.shape[3]
+    size = own.shape[2] // (2 * rows_each)
 
     def pick(m, f):
-        return own[m, row // 2, f, row % 2].astype(jnp.float32)
+        part = own[m, row // rows_each].astype(jnp.float32)
+        start = (f * rows_each + row % rows_each) * size
+        part = part[start : start + SPAN]
+        if part.shape[0] < SPAN:
+            part = jnp.concatenate([part, jnp.zeros((SPAN - part.shape[0], chans), jnp.float32)], axis=0)
+        return part
 
     for t in range(0, frames, 2):
-        here = at + t * span
+        here = at + t * SPAN
         for a, f in ((1, 0), (2, 1)):
             pair = jnp.concatenate([pick(t, f), pick(t + 1, f)], axis=0)
-            xs[a, here : here + 2 * span] = pair.astype(jnp.bfloat16)
-        before = pick(t - 1, 1) if t else jnp.zeros((span, chans), jnp.float32)
+            xs[a, here : here + 2 * SPAN] = pair.astype(jnp.bfloat16)
+        before = pick(t - 1, 1) if t else jnp.zeros((SPAN, chans), jnp.float32)
         pair = jnp.concatenate([before, pick(t, 1)], axis=0)
-        xs[0, here : here + 2 * span] = pair.astype(jnp.bfloat16)
+        xs[0, here : here + 2 * SPAN] = pair.astype(jnp.bfloat16)
 
 
 def silu(value):
@@ -89,14 +102,30 @@
     )
 
 
+def pack(value):
+    kept = [value[at + 1 : at + 1 + KEPT] for at in range(0, value.shape[0], SPAN)]
+    return jnp.concatenate(kept, axis=0).astype(jnp.bfloat16)
+
+
+def unpack(packed):
+    value = packed.astype(jnp.float32)
+    before = jnp.zeros((1, value.shape[1]), jnp.float32)
+    after = jnp.zeros((SPAN - KEPT - 1, value.shape[1]), jnp.float32)
+    parts = []
+    for at in range(0, value.shape[0], KEPT):
+        parts += [before, value[at : at + KEPT], after]
+    return jnp.concatenate(parts, axis=0)
+
+
 def edge_kernel(masks, own, weight, t_edge, edges, send_down, send_up, xs):
-    frames, span, chans = own.shape[0], own.shape[4], own.shape[5]
-    rows = own.shape[1] * own.shape[3]
+    frames, span, chans = own.shape[0], SPAN, own.shape[3]
+    rows_each = PLANE_ROWS // own.shape[1]
+    rows = own.shape[1] * rows_each
     pitch = frames * span
 
     for i in range(3):
-        frames_to(xs, i * pitch, own, i)
-        frames_to(xs, (3 + i) * pitch, own, rows - 3 + i)
+        frames_to(xs, i * pitch, own, i, rows_each)
+        frames_to(xs, (3 + i) * pitch, own, rows - 3 + i, rows_each)
 
     def taps_of(i):
         return jnp.concatenate([xs[a, i * pitch : (i + 1) * pitch] for a in range(3)], axis=1)
@@ -123,19 +152,18 @@
     first, last = low[:pitch], high[pitch:]
     before, after = lower[:pitch], upper[pitch:]
     edges[0], edges[1], edges[2], edges[3] = first, last, before, after
-    near = inside(low[pitch:] + upper[:pitch], masks[0]).astype(jnp.bfloat16)
-    far = inside(high[:pitch] + lower[pitch:], masks[0]).astype(jnp.bfloat16)
-    t_edge[0], t_edge[1] = near, far
-
-    for i, value in enumerate((far, last.astype(jnp.bfloat16), after.astype(jnp.bfloat16))):
-        send_up[i] = value
-    for i, value in enumerate((near, first.astype(jnp.bfloat16), before.astype(jnp.bfloat16))):
-        send_down[i] = value
+    near = inside(low[pitch:] + upper[:pitch], masks[0])
+    far = inside(high[:pitch] + lower[pitch:], masks[0])
+    t_edge[0], t_edge[1] = near.astype(jnp.bfloat16), far.astype(jnp.bfloat16)
+    for i, value in enumerate((far, last, after)):
+        send_up[i] = pack(value)
+    for i, value in enumerate((near, first, before)):
+        send_down[i] = pack(value)
 
 
 def crop(value, frames, span):
     shape = (value.shape[0] // (frames * span), frames, span, value.shape[1])
-    return value.reshape(shape)[:, :, HALO : span - HALO].astype(jnp.bfloat16)
+    return value.reshape(shape)[:, :, HALO : HALO + WIDTH].astype(jnp.bfloat16)
 
 
 def dot_taps(lhs, rhs):
@@ -169,14 +197,15 @@
     masks, own, weight, t_edge, w_first, w_second, known_h, known_o, o_mid, w1, w2,
     xs, tall, hs, wt,
 ):
-    frames, span = own.shape[0], own.shape[4]
-    rows = own.shape[1] * own.shape[3]
+    frames, span = own.shape[0], SPAN
+    rows_each = PLANE_ROWS // own.shape[1]
+    rows = own.shape[1] * rows_each
     pitch = frames * span
     temporal_weight_to(wt, weight)
     plane_weight_to(w1, w_first)
     plane_weight_to(w2, w_second)
     for row in range(1, rows - 1):
-        frames_to(xs, (row - 1) * pitch, own, row)
+        frames_to(xs, (row - 1) * pitch, own, row, rows_each)
     lhs = jnp.concatenate(
         [xs[a, b * pitch : (b + rows - 4) * pitch] for b in range(3) for a in range(3)], axis=1
     )
@@ -214,14 +243,14 @@
         return inside(value, mask).astype(jnp.bfloat16)
 
     top = [
-        shown(above[0].astype(jnp.float32), -2),
-        shown(above[1] + edges[2], -1),
-        shown(above[2] + edges[0], 0),
+        shown(unpack(above[0]), -2),
+        shown(unpack(above[1]) + edges[2], -1),
+        shown(unpack(above[2]) + edges[0], 0),
     ]
     end = [
-        shown(below[2] + edges[1], rows - 1),
-        shown(below[1] + edges[3], rows),
-        shown(below[0].astype(jnp.float32), rows + 1),
+        shown(unpack(below[2]) + edges[1], rows - 1),
+        shown(unpack(below[1]) + edges[3], rows),
+        shown(unpack(below[0]), rows + 1),
     ]
     sums = outer_rows(top, end, w1, known_h)
     places = (-1, 0, 1, rows - 2, rows - 1, rows)
@@ -242,7 +271,8 @@
     frame_count, row_count, col_count, chans = frames_in.shape
     count = tm * SLABS
     width = col_count // count
-    span = width + 2 * HALO
+    span = SPAN
+    size = width + 2 * HALO
     plane_rows = SLABS * row_count
     pitch = tm * span
     column, slab = lax.axis_index("tm"), lax.axis_index("rows")
@@ -264,7 +294,7 @@
 
     cut = pl.pallas_call(
         windows_kernel,
-        out_shape=brain(count, frame_count, row_count, span, chans),
+        out_shape=brain(count, frame_count * row_count * size, chans),
         in_specs=[vmem],
         out_specs=vmem,
         compiler_params=params,
@@ -274,15 +304,15 @@
     members = [[m * slabs + z * SLABS + j for m in range(tm) for j in range(SLABS)] for z in range(planes)]
     own = lax.all_to_all(
         cut, ("tm", "rows"), split_axis=0, concat_axis=0, tiled=True, axis_index_groups=members
-    ).reshape(tm, SLABS, frame_count, row_count, span, chans)
+    ).reshape(tm, SLABS, frame_count * row_count * size, chans)
 
     t_edge, edges, send_down, send_up = pl.pallas_call(
         edge_kernel,
         out_shape=[
             brain(2, pitch, chans),
             jax.ShapeDtypeStruct((4, pitch, chans), jnp.float32),
-            brain(3, pitch, chans),
-            brain(3, pitch, chans),
+            brain(3, tm * KEPT, chans),
+            brain(3, tm * KEPT, chans),
         ],
         in_specs=[vmem] * 3,
         out_specs=[vmem] * 4,

time: 49 us -> 48 us (0.980)
  blocking collectives: 31.8 us -> 31.2 us
  waiting for transfers between devices: 4.28 us -> 3.76 us
    all_to_all x1, blocking collectives: 21.9 us -> 21.1 us  [per_device(): lax.all_to_all(cut, ('tm', 'rows'), split_axis=0, concat_axis=0, tiled=Tr...]
    ppermute x1, waiting for transfers between devices: 4.28 us -> 3.75 us  [per_device(): above = lax.ppermute(send_up, 'rows', [(r, r + SLABS) for r in reach])]
where the time goes in v6:
time: 48 us; the launch traced here: 47.7 us
  blocking collectives  31.2 us (65%)
  starting transfers between devices  6.05 us (13%)
  Pallas kernels  4.77 us (10%)
  waiting for transfers between devices  3.76 us (8%)
  local copies, waits for them, and re-layouts  1.78 us (4%)
    all_to_all x1, blocking collectives, per_device(): lax.all_to_all(cut, ('tm', 'rows'), split_axis=0, concat_axis=0, tiled=Tr...  21.1 us
    all_to_all x1, blocking collectives, per_device(): lax.all_to_all(encoded, 'rows', split_axis=0, concat_axis=0, tiled=True,...  10.1 us
    ppermute x1, starting transfers between devices, per_device(): below = lax.ppermute(send_down, 'rows', [(r + SLABS, r) for r in reach])  4.13 us
    ppermute x1, waiting for transfers between devices, per_device(): above = lax.ppermute(send_up, 'rows', [(r, r + SLABS) for r in reach])  3.75 us
    pallas_call x1, Pallas kernels, per_device(): pl.pallas_call(inner_kernel, out_shape=[partial, partial, brain(inner - 2...  2.34 us
    ppermute x1, starting transfers between devices, per_device(): above = lax.ppermute(send_up, 'rows', [(r, r + SLABS) for r in reach])  1.92 us
    pallas_call x1, Pallas kernels, per_device(): pl.pallas_call(edge_kernel, out_shape=[brain(2, pitch, chans), jax.ShapeD...  1.15 us
    pallas_call x1, Pallas kernels, per_device(): pl.pallas_call(lambda *refs: outer_kernel(tm, *refs), out_shape=brain(SLA...  1.08 us
  transfers between devices with their start and end apart: 2, of which 1 were waited for; matrix products, arithmetic and copies ran while one was open for 0% of the time, Pallas kernels for 5%

profile of v6, /device:TPU:384, one launch (start us, length us, event | category | flops | bytes accessed | tf_op | source)
XLA Modules:
  0.0 47.7 jit_solution(4833733099969049609)
XLA Ops:
  0.0 0.0 copy-start.1
  0.0 1.0 %copy-done.1 = bf16[2,2,512,128]{3,2,1,0:T(8,128)(2,1)S(1)} copy-done((bf16[2,2,512,128]{3,2,1,0:T(8,128)(2,1)S(1)}, bf16[2,2,512,128]{3,2,1,0:T(8,128)(2,1)}, u32[]{:S(2)}) %copy-start.1) | copy-done | bytes 524312
  1.1 0.2 windows.1
  1.3 0.0 copy-start
  1.3 0.1 and_convert_fusion.masks.refs_0_
  1.4 21.1 %all_to_all.10 = bf16[32,88,128]{2,1,0:T(8,128)(2,1)S(1)} all-to-all(bf16[32,88,128]{2,1,0:T(8,128)(2,1)S(1)} %windows.1), channel_id=1, replica_groups={{0,1,2,3,64,65,66,67,128,129,130,131,192,193,194,195,256,257,258,259,32..., dimensions={0} | all-to-all | bytes 1441792 | tf_op jit(solution)/shard_map/all_to_all | solution.py:305
  22.5 0.0 copy-done
  22.5 0.0 copy-start.2
  22.5 0.0 copy-start.3
  22.5 1.1 %edge.1 = (bf16[2,192,128]{2,1,0:T(8,128)(2,1)S(1)}, f32[4,192,128]{2,1,0:T(8,128)S(1)}, bf16[3,160,128]{2,1,0:T(8,128)(2,1)S(1)}, bf16[3,160,128]{2,1,0:T(8,128)(2,1)S(1)}) custom-call(f32[3,24,128]{2,1,0:T(8,128)S(1)} %and_convert_fusion.masks.refs_0_, bf16[8,4,88,128]{3,2,1,0:T(8,128)(2,1)S(1)} %bitcast.3, bf16[3,3,3,128,128]{4,3,2,1,0:T(8,128)(2,1)S(1)} %copy-done), custom_call_target="tpu_custom_call" | custom-call | tf_op jit(solution)/shard_map/edge/pallas_call | solution.py:309
  23.7 4.1 %collective-permute-start = (bf16[3,160,128]{2,1,0:T(8,128)(2,1)S(1)}, bf16[3,160,128]{2,1,0:T(8,128)(2,1)S(1)}, u32[]{:S(2)}, u32[]{:S(2)}) collective-permute-start(bf16[3,160,128]{2,1,0:T(8,128)(2,1)S(1)} %get-tuple-element.23), channel_id=1, source_target_pairs={{4,0},{5,1},{6,2},{7,3},{8,4},{9,5},{10,6},{11,7},{12,8},{13,9},{1... | collective-permute-start | bytes 368648 | tf_op jit(solution)/shard_map/ppermute | solution.py:326
  27.8 1.9 %collective-permute-start.1 = (bf16[3,160,128]{2,1,0:T(8,128)(2,1)S(1)}, bf16[3,160,128]{2,1,0:T(8,128)(2,1)S(1)}, u32[]{:S(2)}, u32[]{:S(2)}) collective-permute-start(bf16[3,160,128]{2,1,0:T(8,128)(2,1)S(1)} %get-tuple-element.24), channel_id=1, source_target_pairs={{0,4},{1,5},{2,6},{3,7},{4,8},{5,9},{6,10},{7,11},{8,12},{9,13},{1... | collective-permute-start | bytes 368648 | tf_op jit(solution)/shard_map/ppermute | solution.py:325
  29.7 0.0 copy-done.2
  29.7 0.0 copy-done.3
  29.7 2.3 %inner.1 = (f32[4,192,128]{2,1,0:T(8,128)S(1)}, f32[4,192,128]{2,1,0:T(8,128)S(1)}, bf16[2,8,16,128]{3,2,1,0:T(8,128)(2,1)S(1)}, bf16[384,384]{1,0:T(8,128)(2,1)S(1)}, bf16[384,384]{1,0:T(8,128)(2,1)S(1)}) custom-call(f32[3,24,128]{2,1,0:T(8,128)S(1)} %and_convert_fusion.masks.refs_0_, bf16[8,4,88,128]{3,2,1,0:T(8,128)(2,1)S(1)} %bitcast.4, ...), custom_call_target="tpu_custom_call" | custom-call | flops 1000000000 | bytes 4000000 | tf_op jit(solution)/shard_map/inner/pallas_call | solution.py:330
  32.1 0.0 collective-permute-done.refs_5_
  32.1 3.8 %collective-permute-done.1.refs_6_ = bf16[3,160,128]{2,1,0:T(8,128)(2,1)S(1)} collective-permute-done((bf16[3,160,128]{2,1,0:T(8,128)(2,1)S(1)}, bf16[3,160,128]{2,1,0:T(8,128)(2,1)S(1)}, u32[]{:S(2)}, u32[]{:S(2)}) %collective-permute-start.1) | collective-permute-done | bytes 122912 | tf_op jit(solution)/shard_map/ppermute | solution.py:325
  35.9 1.1 %outer.1 = bf16[4,8,2,16,128]{4,3,2,1,0:T(8,128)(2,1)S(1)} custom-call(f32[3,24,128]{2,1,0:T(8,128)S(1)} %and_convert_fusion.masks.refs_0_, f32[4,192,128]{2,1,0:T(8,128)S(1)} %get-tuple-element.18.refs_1_, f32[4,192,128]{2,1,0:T(8,128)S(1)} %get-tuple-element.20.refs_2_, f32[4,192,128]{2,1,0:T(8,128)S(1)} %get-tuple-element.21.refs_3_, ...), custom_call_target="tpu_custom_call" | custom-call | tf_op jit(solution)/shard_map/outer/pallas_call | solution.py:351
  36.9 10.1 %all_to_all.11 = bf16[4,8,2,16,128]{4,3,2,1,0:T(8,128)(2,1)S(1)} all-to-all(bf16[4,8,2,16,128]{4,3,2,1,0:T(8,128)(2,1)S(1)} %outer.1), channel_id=1, replica_groups={{0,1,2,3},{4,5,6,7},{8,9,10,11},{12,13,14,15},{16,17,18,19},{20,21,22,2..., dimensions={0} | all-to-all | bytes 524288 | tf_op jit(solution)/shard_map/all_to_all | solution.py:361
  47.0 0.7 %copy.5 = bf16[8,2,4,16,128]{4,3,2,1,0:T(8,128)(2,1)} copy(bf16[8,2,4,16,128]{4,3,1,0,2:T(8,128)(2,1)S(1)} %bitcast.5) | data formatting | bytes 524288 | tf_op jit(solution)/shard_map/transpose | solution.py:364
  (2 shorter events, 0.0 us)
Async XLA Ops:
  0.0 1.0 %copy-start.1 = (bf16[2,2,512,128]{3,2,1,0:T(8,128)(2,1)S(1)}, bf16[2,2,512,128]{3,2,1,0:T(8,128)(2,1)}, u32[]{:S(2)}) copy-start(bf16[2,2,512,128]{3,2,1,0:T(8,128)(2,1)} %frames.1) | copy-start | bytes 1572868
  1.3 21.2 %copy-start = (bf16[3,3,3,128,128]{4,3,2,1,0:T(8,128)(2,1)S(1)}, bf16[3,3,3,128,128]{4,3,2,1,0:T(8,128)(2,1)}, u32[]{:S(2)}) copy-start(bf16[3,3,3,128,128]{4,3,2,1,0:T(8,128)(2,1)} %weight.3) | copy-start | bytes 2654212
  22.5 7.2 %copy-start.2 = (bf16[3,3,128,128]{3,2,1,0:T(8,128)(2,1)S(1)}, bf16[3,3,128,128]{3,2,1,0:T(8,128)(2,1)}, u32[]{:S(2)}) copy-start(bf16[3,3,128,128]{3,2,1,0:T(8,128)(2,1)} %w_first.1) | copy-start | bytes 884740
  22.5 7.2 %copy-start.3 = (bf16[3,3,128,128]{3,2,1,0:T(8,128)(2,1)S(1)}, bf16[3,3,128,128]{3,2,1,0:T(8,128)(2,1)}, u32[]{:S(2)}) copy-start(bf16[3,3,128,128]{3,2,1,0:T(8,128)(2,1)} %w_second.1) | copy-start | bytes 884740
  23.7 8.4 %collective-permute-start = (bf16[3,160,128]{2,1,0:T(8,128)(2,1)S(1)}, bf16[3,160,128]{2,1,0:T(8,128)(2,1)S(1)}, u32[]{:S(2)}, u32[]{:S(2)}) collective-permute-start(bf16[3,160,128]{2,1,0:T(8,128)(2,1)S(1)} %get-tuple-element.23), channel_id=1, source_target_pairs={{4,0},{5,1},{6,2},{7,3},{8,4},{9,5},{10,6},{11,7},{12,8},{13,9},{1... | collective-permute-start | bytes 368648 | tf_op jit(solution)/shard_map/ppermute | solution.py:326
  27.8 8.1 %collective-permute-start.1 = (bf16[3,160,128]{2,1,0:T(8,128)(2,1)S(1)}, bf16[3,160,128]{2,1,0:T(8,128)(2,1)S(1)}, u32[]{:S(2)}, u32[]{:S(2)}) collective-permute-start(bf16[3,160,128]{2,1,0:T(8,128)(2,1)S(1)} %get-tuple-element.24), channel_id=1, source_target_pairs={{0,4},{1,5},{2,6},{3,7},{4,8},{5,9},{6,10},{7,11},{8,12},{9,13},{1... | collective-permute-start | bytes 368648 | tf_op jit(solution)/shard_map/ppermute | solution.py:325

commit v7 on v6

--- a/solution.py
+++ b/solution.py
@@ -102,6 +102,11 @@
     )
 
 
+def halves(value):
+    high = value.astype(jnp.bfloat16).astype(jnp.float32)
+    return high, value - high
+
+
 def pack(value):
     kept = [value[at + 1 : at + 1 + KEPT] for at in range(0, value.shape[0], SPAN)]
     return jnp.concatenate(kept, axis=0).astype(jnp.bfloat16)
@@ -155,9 +160,9 @@
     near = inside(low[pitch:] + upper[:pitch], masks[0])
     far = inside(high[:pitch] + lower[pitch:], masks[0])
     t_edge[0], t_edge[1] = near.astype(jnp.bfloat16), far.astype(jnp.bfloat16)
-    for i, value in enumerate((far, last, after)):
+    for i, value in enumerate((far, *halves(last), *halves(after))):
         send_up[i] = pack(value)
-    for i, value in enumerate((near, first, before)):
+    for i, value in enumerate((near, *halves(first), *halves(before))):
         send_down[i] = pack(value)
 
 
@@ -244,12 +249,12 @@
 
     top = [
         shown(unpack(above[0]), -2),
-        shown(unpack(above[1]) + edges[2], -1),
-        shown(unpack(above[2]) + edges[0], 0),
+        shown(unpack(above[1]) + unpack(above[2]) + edges[2], -1),
+        shown(unpack(above[3]) + unpack(above[4]) + edges[0], 0),
     ]
     end = [
-        shown(unpack(below[2]) + edges[1], rows - 1),
-        shown(unpack(below[1]) + edges[3], rows),
+        shown(unpack(below[3]) + unpack(below[4]) + edges[1], rows - 1),
+        shown(unpack(below[1]) + unpack(below[2]) + edges[3], rows),
         shown(unpack(below[0]), rows + 1),
     ]
     sums = outer_rows(top, end, w1, known_h)
@@ -311,8 +316,8 @@
         out_shape=[
             brain(2, pitch, chans),
             jax.ShapeDtypeStruct((4, pitch, chans), jnp.float32),
-            brain(3, tm * KEPT, chans),
-            brain(3, tm * KEPT, chans),
+            brain(5, tm * KEPT, chans),
+            brain(5, tm * KEPT, chans),
         ],
         in_specs=[vmem] * 3,
         out_specs=[vmem] * 4,

time: 48 us -> 49.7 us (1.035)
  waiting for transfers between devices: 3.76 us -> 5.52 us
    ppermute x1, waiting for transfers between devices: 3.75 us -> 5.06 us  [per_device(): above = lax.ppermute(send_up, 'rows', [(r, r + SLABS) for r in reach])]
  transfers between devices with their start and end apart: 2 -> 2, of which waited for: 1 -> 2; matrix products, arithmetic and copies ran while one was open for 0% -> 0% of each run, Pallas kernels for 5% -> 5%
where the time goes in v7:
time: 49.7 us; the launch traced here: 49.4 us
  blocking collectives  31.1 us (63%)
  starting transfers between devices  6.05 us (12%)
  waiting for transfers between devices  5.52 us (11%)
  Pallas kernels  4.81 us (10%)
  local copies, waits for them, and re-layouts  1.78 us (4%)
    all_to_all x1, blocking collectives, per_device(): lax.all_to_all(cut, ('tm', 'rows'), split_axis=0, concat_axis=0, tiled=Tr...  21.1 us
    all_to_all x1, blocking collectives, per_device(): lax.all_to_all(encoded, 'rows', split_axis=0, concat_axis=0, tiled=True,...  9.93 us
    ppermute x1, waiting for transfers between devices, per_device(): above = lax.ppermute(send_up, 'rows', [(r, r + SLABS) for r in reach])  5.06 us
    ppermute x1, starting transfers between devices, per_device(): below = lax.ppermute(send_down, 'rows', [(r + SLABS, r) for r in reach])  4.13 us
    pallas_call x1, Pallas kernels, per_device(): pl.pallas_call(inner_kernel, out_shape=[partial, partial, brain(inner - 2...  2.35 us
    ppermute x1, starting transfers between devices, per_device(): above = lax.ppermute(send_up, 'rows', [(r, r + SLABS) for r in reach])  1.92 us
    pallas_call x1, Pallas kernels, per_device(): pl.pallas_call(edge_kernel, out_shape=[brain(2, pitch, chans), jax.ShapeD...  1.17 us
    pallas_call x1, Pallas kernels, per_device(): pl.pallas_call(lambda *refs: outer_kernel(tm, *refs), out_shape=brain(SLA...  1.1 us
  transfers between devices with their start and end apart: 2, of which 2 were waited for; matrix products, arithmetic and copies ran while one was open for 0% of the time, Pallas kernels for 5%

profile of v7, /device:TPU:384, one launch (start us, length us, event | category | flops | bytes accessed | tf_op | source)
XLA Modules:
  0.0 49.4 jit_solution(5234621887766942779)
XLA Ops:
  0.0 0.0 copy-start.1
  0.0 1.0 %copy-done.1 = bf16[2,2,512,128]{3,2,1,0:T(8,128)(2,1)S(1)} copy-done((bf16[2,2,512,128]{3,2,1,0:T(8,128)(2,1)S(1)}, bf16[2,2,512,128]{3,2,1,0:T(8,128)(2,1)}, u32[]{:S(2)}) %copy-start.1) | copy-done | bytes 524312
  1.1 0.2 windows.1
  1.3 0.0 copy-start
  1.3 0.1 and_convert_fusion.masks.refs_0_
  1.4 21.1 %all_to_all.10 = bf16[32,88,128]{2,1,0:T(8,128)(2,1)S(1)} all-to-all(bf16[32,88,128]{2,1,0:T(8,128)(2,1)S(1)} %windows.1), channel_id=1, replica_groups={{0,1,2,3,64,65,66,67,128,129,130,131,192,193,194,195,256,257,258,259,32..., dimensions={0} | all-to-all | bytes 1441792 | tf_op jit(solution)/shard_map/all_to_all | solution.py:310
  22.5 0.0 copy-done
  22.5 0.0 copy-start.2
  22.5 0.0 copy-start.3
  22.5 1.2 %edge.1 = (bf16[2,192,128]{2,1,0:T(8,128)(2,1)S(1)}, f32[4,192,128]{2,1,0:T(8,128)S(1)}, bf16[5,160,128]{2,1,0:T(8,128)(2,1)S(1)}, bf16[5,160,128]{2,1,0:T(8,128)(2,1)S(1)}) custom-call(f32[3,24,128]{2,1,0:T(8,128)S(1)} %and_convert_fusion.masks.refs_0_, bf16[8,4,88,128]{3,2,1,0:T(8,128)(2,1)S(1)} %bitcast.3, bf16[3,3,3,128,128]{4,3,2,1,0:T(8,128)(2,1)S(1)} %copy-done), custom_call_target="tpu_custom_call" | custom-call | tf_op jit(solution)/shard_map/edge/pallas_call | solution.py:314
  23.7 4.1 %collective-permute-start = (bf16[5,160,128]{2,1,0:T(8,128)(2,1)S(1)}, bf16[5,160,128]{2,1,0:T(8,128)(2,1)S(1)}, u32[]{:S(2)}, u32[]{:S(2)}) collective-permute-start(bf16[5,160,128]{2,1,0:T(8,128)(2,1)S(1)} %get-tuple-element.23), channel_id=1, source_target_pairs={{4,0},{5,1},{6,2},{7,3},{8,4},{9,5},{10,6},{11,7},{12,8},{13,9},{1... | collective-permute-start | bytes 614408 | tf_op jit(solution)/shard_map/ppermute | solution.py:331
  27.8 1.9 %collective-permute-start.1 = (bf16[5,160,128]{2,1,0:T(8,128)(2,1)S(1)}, bf16[5,160,128]{2,1,0:T(8,128)(2,1)S(1)}, u32[]{:S(2)}, u32[]{:S(2)}) collective-permute-start(bf16[5,160,128]{2,1,0:T(8,128)(2,1)S(1)} %get-tuple-element.24), channel_id=1, source_target_pairs={{0,4},{1,5},{2,6},{3,7},{4,8},{5,9},{6,10},{7,11},{8,12},{9,13},{1... | collective-permute-start | bytes 614408 | tf_op jit(solution)/shard_map/ppermute | solution.py:330
  29.7 0.0 copy-done.2
  29.8 0.0 copy-done.3
  29.8 2.3 %inner.1 = (f32[4,192,128]{2,1,0:T(8,128)S(1)}, f32[4,192,128]{2,1,0:T(8,128)S(1)}, bf16[2,8,16,128]{3,2,1,0:T(8,128)(2,1)S(1)}, bf16[384,384]{1,0:T(8,128)(2,1)S(1)}, bf16[384,384]{1,0:T(8,128)(2,1)S(1)}) custom-call(f32[3,24,128]{2,1,0:T(8,128)S(1)} %and_convert_fusion.masks.refs_0_, bf16[8,4,88,128]{3,2,1,0:T(8,128)(2,1)S(1)} %bitcast.4, ...), custom_call_target="tpu_custom_call" | custom-call | flops 1000000000 | bytes 4000000 | tf_op jit(solution)/shard_map/inner/pallas_call | solution.py:335
  32.1 0.5 collective-permute-done.refs_5_
  32.6 5.1 %collective-permute-done.1.refs_6_ = bf16[5,160,128]{2,1,0:T(8,128)(2,1)S(1)} collective-permute-done((bf16[5,160,128]{2,1,0:T(8,128)(2,1)S(1)}, bf16[5,160,128]{2,1,0:T(8,128)(2,1)S(1)}, u32[]{:S(2)}, u32[]{:S(2)}) %collective-permute-start.1) | collective-permute-done | bytes 204832 | tf_op jit(solution)/shard_map/ppermute | solution.py:330
  37.6 1.1 %outer.1 = bf16[4,8,2,16,128]{4,3,2,1,0:T(8,128)(2,1)S(1)} custom-call(f32[3,24,128]{2,1,0:T(8,128)S(1)} %and_convert_fusion.masks.refs_0_, f32[4,192,128]{2,1,0:T(8,128)S(1)} %get-tuple-element.18.refs_1_, f32[4,192,128]{2,1,0:T(8,128)S(1)} %get-tuple-element.20.refs_2_, f32[4,192,128]{2,1,0:T(8,128)S(1)} %get-tuple-element.21.refs_3_, ...), custom_call_target="tpu_custom_call" | custom-call | tf_op jit(solution)/shard_map/outer/pallas_call | solution.py:356
  38.7 9.9 %all_to_all.11 = bf16[4,8,2,16,128]{4,3,2,1,0:T(8,128)(2,1)S(1)} all-to-all(bf16[4,8,2,16,128]{4,3,2,1,0:T(8,128)(2,1)S(1)} %outer.1), channel_id=1, replica_groups={{0,1,2,3},{4,5,6,7},{8,9,10,11},{12,13,14,15},{16,17,18,19},{20,21,22,2..., dimensions={0} | all-to-all | bytes 524288 | tf_op jit(solution)/shard_map/all_to_all | solution.py:366
  48.7 0.7 %copy.5 = bf16[8,2,4,16,128]{4,3,2,1,0:T(8,128)(2,1)} copy(bf16[8,2,4,16,128]{4,3,1,0,2:T(8,128)(2,1)S(1)} %bitcast.5) | data formatting | bytes 524288 | tf_op jit(solution)/shard_map/transpose | solution.py:369
  (2 shorter events, 0.0 us)
Async XLA Ops:
  0.0 1.0 %copy-start.1 = (bf16[2,2,512,128]{3,2,1,0:T(8,128)(2,1)S(1)}, bf16[2,2,512,128]{3,2,1,0:T(8,128)(2,1)}, u32[]{:S(2)}) copy-start(bf16[2,2,512,128]{3,2,1,0:T(8,128)(2,1)} %frames.1) | copy-start | bytes 1572868
  1.3 21.2 %copy-start = (bf16[3,3,3,128,128]{4,3,2,1,0:T(8,128)(2,1)S(1)}, bf16[3,3,3,128,128]{4,3,2,1,0:T(8,128)(2,1)}, u32[]{:S(2)}) copy-start(bf16[3,3,3,128,128]{4,3,2,1,0:T(8,128)(2,1)} %weight.3) | copy-start | bytes 2654212
  22.5 7.2 %copy-start.2 = (bf16[3,3,128,128]{3,2,1,0:T(8,128)(2,1)S(1)}, bf16[3,3,128,128]{3,2,1,0:T(8,128)(2,1)}, u32[]{:S(2)}) copy-start(bf16[3,3,128,128]{3,2,1,0:T(8,128)(2,1)} %w_first.1) | copy-start | bytes 884740
  22.5 7.3 %copy-start.3 = (bf16[3,3,128,128]{3,2,1,0:T(8,128)(2,1)S(1)}, bf16[3,3,128,128]{3,2,1,0:T(8,128)(2,1)}, u32[]{:S(2)}) copy-start(bf16[3,3,128,128]{3,2,1,0:T(8,128)(2,1)} %w_second.1) | copy-start | bytes 884740
  23.7 8.9 %collective-permute-start = (bf16[5,160,128]{2,1,0:T(8,128)(2,1)S(1)}, bf16[5,160,128]{2,1,0:T(8,128)(2,1)S(1)}, u32[]{:S(2)}, u32[]{:S(2)}) collective-permute-start(bf16[5,160,128]{2,1,0:T(8,128)(2,1)S(1)} %get-tuple-element.23), channel_id=1, source_target_pairs={{4,0},{5,1},{6,2},{7,3},{8,4},{9,5},{10,6},{11,7},{12,8},{13,9},{1... | collective-permute-start | bytes 614408 | tf_op jit(solution)/shard_map/ppermute | solution.py:331
  27.8 9.8 %collective-permute-start.1 = (bf16[5,160,128]{2,1,0:T(8,128)(2,1)S(1)}, bf16[5,160,128]{2,1,0:T(8,128)(2,1)S(1)}, u32[]{:S(2)}, u32[]{:S(2)}) collective-permute-start(bf16[5,160,128]{2,1,0:T(8,128)(2,1)S(1)} %get-tuple-element.24), channel_id=1, source_target_pairs={{0,4},{1,5},{2,6},{3,7},{4,8},{5,9},{6,10},{7,11},{8,12},{9,13},{1... | collective-permute-start | bytes 614408 | tf_op jit(solution)/shard_map/ppermute | solution.py:330

commit v8 on v6

--- a/solution.py
+++ b/solution.py
@@ -130,30 +130,20 @@
     def taps_of(i):
         return jnp.concatenate([xs[a, i * pitch : (i + 1) * pitch] for a in range(3)], axis=1)
 
-    def dot(lhs, rhs):
-        return column_taps(jnp.dot(lhs, rhs, preferred_element_type=jnp.float32))
-
     deep = 3 * chans
     x = [taps_of(i) for i in range(6)]
-    low = dot(
-        jnp.concatenate([jnp.concatenate(x[0:2], axis=1), jnp.concatenate(x[1:3], axis=1)], axis=0),
-        temporal_taps(weight, (1, 2)),
-    )
-    high = dot(
-        jnp.concatenate([jnp.concatenate(x[3:5], axis=1), jnp.concatenate(x[4:6], axis=1)], axis=0),
-        temporal_taps(weight, (0, 1)),
-    )
-    outer = jnp.dot(
-        jnp.concatenate([x[0], x[5]], axis=0),
-        jnp.concatenate([temporal_taps(weight, (b,)) for b in (0, 2)], axis=1),
+    sums = jnp.dot(
+        jnp.concatenate([jnp.concatenate(pair, axis=1) for pair in (x[0:2], x[4:6])], axis=0),
+        jnp.concatenate([temporal_taps(weight, taps) for taps in ((1, 2), (0, 1))], axis=1),
         preferred_element_type=jnp.float32,
     )
-    upper, lower = column_taps(outer[:, :deep]), column_taps(outer[:, deep:])
-    first, last = low[:pitch], high[pitch:]
-    before, after = lower[:pitch], upper[pitch:]
+    lower, upper = column_taps(sums[:, :deep]), column_taps(sums[:, deep:])
+    first, last = lower[:pitch], upper[pitch:]
+    second, before = split_rows(dot_taps([[x[2]], [x[0]]], temporal_taps(weight, (2,))), pitch)
+    third, after = split_rows(dot_taps([[x[3]], [x[5]]], temporal_taps(weight, (0,))), pitch)
     edges[0], edges[1], edges[2], edges[3] = first, last, before, after
-    near = inside(low[pitch:] + upper[:pitch], masks[0])
-    far = inside(high[:pitch] + lower[pitch:], masks[0])
+    near = inside(upper[:pitch] + second, masks[0])
+    far = inside(lower[pitch:] + third, masks[0])
     t_edge[0], t_edge[1] = near.astype(jnp.bfloat16), far.astype(jnp.bfloat16)
     for i, value in enumerate((far, last, after)):
         send_up[i] = pack(value)
@@ -183,14 +173,18 @@
     return split_rows(top, pitch) + split_rows(end, pitch)
 
 
-def outer_rows(top, end, weight, known):
-    pitch, chans = top[0].shape
-    none = jnp.zeros_like(top[0])
-    first, last = split_rows(dot_taps([top, end], weight[...]), pitch)
-    near = split_rows(dot_taps([top[1:], [top[2], none]], weight[: 2 * chans]), pitch)
-    far = split_rows(dot_taps([[none, end[0]], end[:2]], weight[chans:]), pitch)
-    inner = [value + known[i] for i, value in enumerate(near + far)]
-    return [first, *inner, last]
+def top_rows(rows, weight, known):
+    none, chans = jnp.zeros_like(rows[0]), rows[0].shape[1]
+    first = dot_taps([rows], weight[...])
+    near = split_rows(dot_taps([rows[1:], [rows[2], none]], weight[: 2 * chans]), none.shape[0])
+    return [first, near[0] + known[0], near[1] + known[1]]
+
+
+def end_rows(rows, weight, known):
+    none, chans = jnp.zeros_like(rows[0]), rows[0].shape[1]
+    last = dot_taps([rows], weight[...])
+    far = split_rows(dot_taps([[none, rows[0]], rows[:2]], weight[chans:]), none.shape[0])
+    return [far[0] + known[2], far[1] + known[3], last]
 
 
 def inner_kernel(
@@ -233,36 +227,39 @@
         known_o[i] = value + temporal[i].astype(jnp.float32)
 
 
-def outer_kernel(frames, masks, edges, known_h, known_o, o_mid, below, above, w1, w2, out):
-    rows = out.shape[0] * out.shape[2]
-    pitch = edges.shape[1]
-    span = pitch // frames
-
-    def shown(value, row):
-        mask = masks[1] if row < 0 else masks[2] if row >= rows else masks[0]
-        return inside(value, mask).astype(jnp.bfloat16)
-
-    top = [
-        shown(unpack(above[0]), -2),
-        shown(unpack(above[1]) + edges[2], -1),
-        shown(unpack(above[2]) + edges[0], 0),
+def shown(value, mask):
+    return inside(value, mask).astype(jnp.bfloat16)
+
+
+def end_kernel(masks, edges, known_h, known_o, below, w1, w2, o_end):
+    rows = [
+        shown(unpack(below[2]) + edges[1], masks[0]),
+        shown(unpack(below[1]) + edges[3], masks[2]),
+        shown(unpack(below[0]), masks[2]),
     ]
-    end = [
-        shown(unpack(below[2]) + edges[1], rows - 1),
-        shown(unpack(below[1]) + edges[3], rows),
-        shown(unpack(below[0]), rows + 1),
+    hidden = end_rows(rows, w1, known_h)
+    hidden = [shown(silu(value), masks[part]) for value, part in zip(hidden, (0, 0, 2))]
+    sums = end_rows(hidden, w2, known_o)
+    sums[2] = sums[2] + rows[0].astype(jnp.float32)
+    for i, value in enumerate(sums):
+        o_end[i] = crop(value, value.shape[0] // SPAN, SPAN)[0]
+
+
+def top_kernel(masks, edges, known_h, known_o, above, w1, w2, o_mid, o_end, out):
+    rows = [
+        shown(unpack(above[0]), masks[1]),
+        shown(unpack(above[1]) + edges[2], masks[1]),
+        shown(unpack(above[2]) + edges[0], masks[0]),
     ]
-    sums = outer_rows(top, end, w1, known_h)
-    places = (-1, 0, 1, rows - 2, rows - 1, rows)
-    hidden = [shown(silu(value), row) for value, row in zip(sums, places)]
-
-    sums = outer_rows(hidden[:3], hidden[3:], w2, known_o)
-    sums[0] = sums[0] + top[2].astype(jnp.float32)
-    sums[5] = sums[5] + end[0].astype(jnp.float32)
-    for value, row in zip(sums, (0, 1, 2, rows - 3, rows - 2, rows - 1)):
-        out[row // 2, :, row % 2] = crop(value, frames, span)[0]
-    for row in range(3, rows - 3):
-        out[row // 2, :, row % 2] = o_mid[row - 3]
+    hidden = top_rows(rows, w1, known_h)
+    hidden = [shown(silu(value), masks[part]) for value, part in zip(hidden, (1, 0, 0))]
+    sums = top_rows(hidden, w2, known_o)
+    sums[0] = sums[0] + rows[2].astype(jnp.float32)
+    done = [crop(value, value.shape[0] // SPAN, SPAN)[0] for value in sums]
+    done += [o_mid[i] for i in range(o_mid.shape[0])] + [o_end[i] for i in range(3)]
+    each = out.shape[2]
+    for row, value in enumerate(done):
+        out[row // each, :, row % each] = value
 
 
 def per_device(frames_in, temporal_weight, first_weight, second_weight):
@@ -348,14 +345,23 @@
         cost_estimate=pl.CostEstimate(flops=10**9, bytes_accessed=4 * 10**6, transcendentals=10**5),
         name="inner",
     )(masks, own, temporal_weight, t_edge, first_weight, second_weight)
+    o_end = pl.pallas_call(
+        end_kernel,
+        out_shape=brain(3, tm, width, chans),
+        in_specs=[vmem] * 7,
+        out_specs=vmem,
+        compiler_params=params,
+        cost_estimate=pl.CostEstimate(flops=4 * 10**8, bytes_accessed=10**6, transcendentals=10**5),
+        name="end",
+    )(masks, edges, known_h, known_o, below, w1, w2)
     encoded = pl.pallas_call(
-        lambda *refs: outer_kernel(tm, *refs),
+        top_kernel,
         out_shape=brain(SLABS, tm, row_count, width, chans),
         in_specs=[vmem] * 9,
         out_specs=vmem,
         compiler_params=params,
-        name="outer",
-    )(masks, edges, known_h, known_o, o_mid, below, above, w1, w2)
+        name="top",
+    )(masks, edges, known_h, known_o, above, w1, w2, o_mid, o_end)
 
     groups = [[z * SLABS + j for j in range(SLABS)] for z in range(planes)]
     encoded = lax.all_to_all(

time: 48 us -> 47.5 us (0.990)
  waiting for transfers between devices: 3.76 us -> 3.05 us
    ppermute x1, waiting for transfers between devices: 3.75 us -> 3.05 us  [per_device(): above = lax.ppermute(send_up, 'rows', [(r, r + SLABS) for r in reach])]
    pallas_call x1 -> x2, Pallas kernels: 1.08 us -> 1.39 us  [the longest x1 0.7 us: per_device(): pl.pallas_call(end_kernel, out_shape=brain(3, tm, width, chans), in_specs...]
  transfers between devices with their start and end apart: 2 -> 2, of which waited for: 1 -> 1; matrix products, arithmetic and copies ran while one was open for 0% -> 0% of each run, Pallas kernels for 5% -> 6%
where the time goes in v8:
time: 47.5 us; the launch traced here: 47.2 us
  blocking collectives  31.2 us (66%)
  starting transfers between devices  6.04 us (13%)
  Pallas kernels  4.96 us (10%)
  waiting for transfers between devices  3.05 us (6%)
  local copies, waits for them, and re-layouts  1.78 us (4%)
    all_to_all x1, blocking collectives, per_device(): lax.all_to_all(cut, ('tm', 'rows'), split_axis=0, concat_axis=0, tiled=Tr...  21.1 us
    all_to_all x1, blocking collectives, per_device(): lax.all_to_all(encoded, 'rows', split_axis=0, concat_axis=0, tiled=True,...  10.1 us
    ppermute x1, starting transfers between devices, per_device(): below = lax.ppermute(send_down, 'rows', [(r + SLABS, r) for r in reach])  4.12 us
    ppermute x1, waiting for transfers between devices, per_device(): above = lax.ppermute(send_up, 'rows', [(r, r + SLABS) for r in reach])  3.05 us
    pallas_call x1, Pallas kernels, per_device(): pl.pallas_call(inner_kernel, out_shape=[partial, partial, brain(inner - 2...  2.35 us
    ppermute x1, starting transfers between devices, per_device(): above = lax.ppermute(send_up, 'rows', [(r, r + SLABS) for r in reach])  1.92 us
    unnamed x8, local copies, waits for them, and re-layouts  1.05 us
    pallas_call x1, Pallas kernels, per_device(): pl.pallas_call(edge_kernel, out_shape=[brain(2, pitch, chans), jax.ShapeD...  1.03 us
  transfers between devices with their start and end apart: 2, of which 1 were waited for; matrix products, arithmetic and copies ran while one was open for 0% of the time, Pallas kernels for 6%

profile of v8, /device:TPU:384, one launch (start us, length us, event | category | flops | bytes accessed | tf_op | source)
XLA Modules:
  0.0 47.2 jit_solution(15937590737215484708)
XLA Ops:
  0.0 0.0 copy-start.1
  0.0 1.0 %copy-done.1 = bf16[2,2,512,128]{3,2,1,0:T(8,128)(2,1)S(1)} copy-done((bf16[2,2,512,128]{3,2,1,0:T(8,128)(2,1)S(1)}, bf16[2,2,512,128]{3,2,1,0:T(8,128)(2,1)}, u32[]{:S(2)}) %copy-start.1) | copy-done | bytes 524312
  1.1 0.2 windows.1
  1.3 0.0 copy-start
  1.3 0.1 and_convert_fusion.masks
  1.4 21.1 %all_to_all.10 = bf16[32,88,128]{2,1,0:T(8,128)(2,1)S(1)} all-to-all(bf16[32,88,128]{2,1,0:T(8,128)(2,1)S(1)} %windows.1), channel_id=1, replica_groups={{0,1,2,3,64,65,66,67,128,129,130,131,192,193,194,195,256,257,258,259,32..., dimensions={0} | all-to-all | bytes 1441792 | tf_op jit(solution)/shard_map/all_to_all | solution.py:302
  22.5 0.0 copy-done
  22.5 0.0 copy-start.2
  22.5 0.0 copy-start.3
  22.5 1.0 %edge.1 = (bf16[2,192,128]{2,1,0:T(8,128)(2,1)S(1)}, f32[4,192,128]{2,1,0:T(8,128)S(1)}, bf16[3,160,128]{2,1,0:T(8,128)(2,1)S(1)}, bf16[3,160,128]{2,1,0:T(8,128)(2,1)S(1)}) custom-call(f32[3,24,128]{2,1,0:T(8,128)S(1)} %and_convert_fusion.masks, bf16[8,4,88,128]{3,2,1,0:T(8,128)(2,1)S(1)} %bitcast.3, bf16[3,3,3,128,128]{4,3,2,1,0:T(8,128)(2,1)S(1)} %copy-done), custom_call_target="tpu_custom_call" | custom-call | tf_op jit(solution)/shard_map/edge/pallas_call | solution.py:306
  23.5 4.1 %collective-permute-start.1 = (bf16[3,160,128]{2,1,0:T(8,128)(2,1)S(1)}, bf16[3,160,128]{2,1,0:T(8,128)(2,1)S(1)}, u32[]{:S(2)}, u32[]{:S(2)}) collective-permute-start(bf16[3,160,128]{2,1,0:T(8,128)(2,1)S(1)} %get-tuple-element.26), channel_id=1, source_target_pairs={{4,0},{5,1},{6,2},{7,3},{8,4},{9,5},{10,6},{11,7},{12,8},{13,9},{1... | collective-permute-start | bytes 368648 | tf_op jit(solution)/shard_map/ppermute | solution.py:323
  27.7 1.9 %collective-permute-start = (bf16[3,160,128]{2,1,0:T(8,128)(2,1)S(1)}, bf16[3,160,128]{2,1,0:T(8,128)(2,1)S(1)}, u32[]{:S(2)}, u32[]{:S(2)}) collective-permute-start(bf16[3,160,128]{2,1,0:T(8,128)(2,1)S(1)} %get-tuple-element.22), channel_id=1, source_target_pairs={{0,4},{1,5},{2,6},{3,7},{4,8},{5,9},{6,10},{7,11},{8,12},{9,13},{1... | collective-permute-start | bytes 368648 | tf_op jit(solution)/shard_map/ppermute | solution.py:322
  29.6 0.0 copy-done.2
  29.6 0.0 copy-done.3
  29.6 2.3 %inner.1 = (f32[4,192,128]{2,1,0:T(8,128)S(1)}, f32[4,192,128]{2,1,0:T(8,128)S(1)}, bf16[2,8,16,128]{3,2,1,0:T(8,128)(2,1)S(1)}, bf16[384,384]{1,0:T(8,128)(2,1)S(1)}, bf16[384,384]{1,0:T(8,128)(2,1)S(1)}) custom-call(f32[3,24,128]{2,1,0:T(8,128)S(1)} %and_convert_fusion.masks, bf16[8,4,88,128]{3,2,1,0:T(8,128)(2,1)S(1)} %bitcast.4, ...), custom_call_target="tpu_custom_call" | custom-call | flops 1000000000 | bytes 4000000 | tf_op jit(solution)/shard_map/inner/pallas_call | solution.py:327
  32.0 0.0 collective-permute-done.1.below
  32.0 0.7 %end.1.o_end = bf16[3,8,16,128]{3,2,1,0:T(8,128)(2,1)S(1)} custom-call(f32[3,24,128]{2,1,0:T(8,128)S(1)} %and_convert_fusion.masks, f32[4,192,128]{2,1,0:T(8,128)S(1)} %get-tuple-element.18.edges, f32[4,192,128]{2,1,0:T(8,128)S(1)} %get-tuple-element.20.known_h, f32[4,192,128]{2,1,0:T(8,128)S(1)} %get-tuple-element.21.known_o, ...), custom_call_target="tpu_custom_call" | custom-call | flops 400000000 | bytes 1000000 | tf_op jit(solution)/shard_map/end/pallas_call | solution.py:348
  32.7 3.0 %collective-permute-done.above = bf16[3,160,128]{2,1,0:T(8,128)(2,1)S(1)} collective-permute-done((bf16[3,160,128]{2,1,0:T(8,128)(2,1)S(1)}, bf16[3,160,128]{2,1,0:T(8,128)(2,1)S(1)}, u32[]{:S(2)}, u32[]{:S(2)}) %collective-permute-start) | collective-permute-done | bytes 122912 | tf_op jit(solution)/shard_map/ppermute | solution.py:322
  35.7 0.7 %top.1 = bf16[4,8,2,16,128]{4,3,2,1,0:T(8,128)(2,1)S(1)} custom-call(f32[3,24,128]{2,1,0:T(8,128)S(1)} %and_convert_fusion.masks, f32[4,192,128]{2,1,0:T(8,128)S(1)} %get-tuple-element.18.edges, f32[4,192,128]{2,1,0:T(8,128)S(1)} %get-tuple-element.20.known_h, f32[4,192,128]{2,1,0:T(8,128)S(1)} %get-tuple-element.21.known_o, ...), custom_call_target="tpu_custom_call" | custom-call | tf_op jit(solution)/shard_map/top/pallas_call | solution.py:357
  36.4 10.1 %all_to_all.11 = bf16[4,8,2,16,128]{4,3,2,1,0:T(8,128)(2,1)S(1)} all-to-all(bf16[4,8,2,16,128]{4,3,2,1,0:T(8,128)(2,1)S(1)} %top.1), channel_id=1, replica_groups={{0,1,2,3},{4,5,6,7},{8,9,10,11},{12,13,14,15},{16,17,18,19},{20,21,22,2..., dimensions={0} | all-to-all | bytes 524288 | tf_op jit(solution)/shard_map/all_to_all | solution.py:367
  46.5 0.7 %copy.5 = bf16[8,2,4,16,128]{4,3,2,1,0:T(8,128)(2,1)} copy(bf16[8,2,4,16,128]{4,3,1,0,2:T(8,128)(2,1)S(1)} %bitcast.5) | data formatting | bytes 524288 | tf_op jit(solution)/shard_map/transpose | solution.py:370
  (2 shorter events, 0.0 us)
Async XLA Ops:
  0.0 1.0 %copy-start.1 = (bf16[2,2,512,128]{3,2,1,0:T(8,128)(2,1)S(1)}, bf16[2,2,512,128]{3,2,1,0:T(8,128)(2,1)}, u32[]{:S(2)}) copy-start(bf16[2,2,512,128]{3,2,1,0:T(8,128)(2,1)} %frames.1) | copy-start | bytes 1572868
  1.3 21.2 %copy-start = (bf16[3,3,3,128,128]{4,3,2,1,0:T(8,128)(2,1)S(1)}, bf16[3,3,3,128,128]{4,3,2,1,0:T(8,128)(2,1)}, u32[]{:S(2)}) copy-start(bf16[3,3,3,128,128]{4,3,2,1,0:T(8,128)(2,1)} %weight.3) | copy-start | bytes 2654212
  22.5 7.1 %copy-start.2 = (bf16[3,3,128,128]{3,2,1,0:T(8,128)(2,1)S(1)}, bf16[3,3,128,128]{3,2,1,0:T(8,128)(2,1)}, u32[]{:S(2)}) copy-start(bf16[3,3,128,128]{3,2,1,0:T(8,128)(2,1)} %w_first.1) | copy-start | bytes 884740
  22.5 7.1 %copy-start.3 = (bf16[3,3,128,128]{3,2,1,0:T(8,128)(2,1)S(1)}, bf16[3,3,128,128]{3,2,1,0:T(8,128)(2,1)}, u32[]{:S(2)}) copy-start(bf16[3,3,128,128]{3,2,1,0:T(8,128)(2,1)} %w_second.1) | copy-start | bytes 884740
  23.5 8.4 %collective-permute-start.1 = (bf16[3,160,128]{2,1,0:T(8,128)(2,1)S(1)}, bf16[3,160,128]{2,1,0:T(8,128)(2,1)S(1)}, u32[]{:S(2)}, u32[]{:S(2)}) collective-permute-start(bf16[3,160,128]{2,1,0:T(8,128)(2,1)S(1)} %get-tuple-element.26), channel_id=1, source_target_pairs={{4,0},{5,1},{6,2},{7,3},{8,4},{9,5},{10,6},{11,7},{12,8},{13,9},{1... | collective-permute-start | bytes 368648 | tf_op jit(solution)/shard_map/ppermute | solution.py:323
  27.7 8.1 %collective-permute-start = (bf16[3,160,128]{2,1,0:T(8,128)(2,1)S(1)}, bf16[3,160,128]{2,1,0:T(8,128)(2,1)S(1)}, u32[]{:S(2)}, u32[]{:S(2)}) collective-permute-start(bf16[3,160,128]{2,1,0:T(8,128)(2,1)S(1)} %get-tuple-element.22), channel_id=1, source_target_pairs={{0,4},{1,5},{2,6},{3,7},{4,8},{5,9},{6,10},{7,11},{8,12},{9,13},{1... | collective-permute-start | bytes 368648 | tf_op jit(solution)/shard_map/ppermute | solution.py:322

commit v9 on v8

--- a/solution.py
+++ b/solution.py
@@ -102,6 +102,11 @@
     )
 
 
+def halves(value):
+    high = value.astype(jnp.bfloat16).astype(jnp.float32)
+    return high, value - high
+
+
 def pack(value):
     kept = [value[at + 1 : at + 1 + KEPT] for at in range(0, value.shape[0], SPAN)]
     return jnp.concatenate(kept, axis=0).astype(jnp.bfloat16)
@@ -145,9 +150,9 @@
     near = inside(upper[:pitch] + second, masks[0])
     far = inside(lower[pitch:] + third, masks[0])
     t_edge[0], t_edge[1] = near.astype(jnp.bfloat16), far.astype(jnp.bfloat16)
-    for i, value in enumerate((far, last, after)):
+    for i, value in enumerate((far, *halves(last), *halves(after))):
         send_up[i] = pack(value)
-    for i, value in enumerate((near, first, before)):
+    for i, value in enumerate((near, *halves(first), *halves(before))):
         send_down[i] = pack(value)
 
 
@@ -233,8 +238,8 @@
 
 def end_kernel(masks, edges, known_h, known_o, below, w1, w2, o_end):
     rows = [
-        shown(unpack(below[2]) + edges[1], masks[0]),
-        shown(unpack(below[1]) + edges[3], masks[2]),
+        shown(unpack(below[3]) + unpack(below[4]) + edges[1], masks[0]),
+        shown(unpack(below[1]) + unpack(below[2]) + edges[3], masks[2]),
         shown(unpack(below[0]), masks[2]),
     ]
     hidden = end_rows(rows, w1, known_h)
@@ -248,8 +253,8 @@
 def top_kernel(masks, edges, known_h, known_o, above, w1, w2, o_mid, o_end, out):
     rows = [
         shown(unpack(above[0]), masks[1]),
-        shown(unpack(above[1]) + edges[2], masks[1]),
-        shown(unpack(above[2]) + edges[0], masks[0]),
+        shown(unpack(above[1]) + unpack(above[2]) + edges[2], masks[1]),
+        shown(unpack(above[3]) + unpack(above[4]) + edges[0], masks[0]),
     ]
     hidden = top_rows(rows, w1, known_h)
     hidden = [shown(silu(value), masks[part]) for value, part in zip(hidden, (1, 0, 0))]
@@ -308,8 +313,8 @@
         out_shape=[
             brain(2, pitch, chans),
             jax.ShapeDtypeStruct((4, pitch, chans), jnp.float32),
-            brain(3, tm * KEPT, chans),
-            brain(3, tm * KEPT, chans),
+            brain(5, tm * KEPT, chans),
+            brain(5, tm * KEPT, chans),
         ],
         in_specs=[vmem] * 3,
         out_specs=[vmem] * 4,

time: 47.5 us -> 49.1 us (1.034)
  waiting for transfers between devices: 3.05 us -> 4.79 us
    ppermute x1, waiting for transfers between devices: 3.05 us -> 4.34 us  [per_device(): above = lax.ppermute(send_up, 'rows', [(r, r + SLABS) for r in reach])]
  transfers between devices with their start and end apart: 2 -> 2, of which waited for: 1 -> 2; matrix products, arithmetic and copies ran while one was open for 0% -> 0% of each run, Pallas kernels for 6% -> 6%
where the time goes in v9:
time: 49.1 us; the launch traced here: 48.9 us
  blocking collectives  31.1 us (63%)
  starting transfers between devices  6.05 us (12%)
  Pallas kernels  5.01 us (10%)
  waiting for transfers between devices  4.79 us (10%)
  local copies, waits for them, and re-layouts  1.78 us (4%)
    all_to_all x1, blocking collectives, per_device(): lax.all_to_all(cut, ('tm', 'rows'), split_axis=0, concat_axis=0, tiled=Tr...  21.1 us
    all_to_all x1, blocking collectives, per_device(): lax.all_to_all(encoded, 'rows', split_axis=0, concat_axis=0, tiled=True,...  9.93 us
    ppermute x1, waiting for transfers between devices, per_device(): above = lax.ppermute(send_up, 'rows', [(r, r + SLABS) for r in reach])  4.34 us
    ppermute x1, starting transfers between devices, per_device(): below = lax.ppermute(send_down, 'rows', [(r + SLABS, r) for r in reach])  4.13 us
    pallas_call x1, Pallas kernels, per_device(): pl.pallas_call(inner_kernel, out_shape=[partial, partial, brain(inner - 2...  2.35 us
    ppermute x1, starting transfers between devices, per_device(): above = lax.ppermute(send_up, 'rows', [(r, r + SLABS) for r in reach])  1.92 us
    pallas_call x1, Pallas kernels, per_device(): pl.pallas_call(edge_kernel, out_shape=[brain(2, pitch, chans), jax.ShapeD...  1.05 us
    unnamed x8, local copies, waits for them, and re-layouts  1.05 us
  transfers between devices with their start and end apart: 2, of which 2 were waited for; matrix products, arithmetic and copies ran while one was open for 0% of the time, Pallas kernels for 6%

profile of v9, /device:TPU:384, one launch (start us, length us, event | category | flops | bytes accessed | tf_op | source)
XLA Modules:
  0.0 48.9 jit_solution(11176796457809542829)
XLA Ops:
  0.0 0.0 copy-start.1
  0.0 1.0 %copy-done.1 = bf16[2,2,512,128]{3,2,1,0:T(8,128)(2,1)S(1)} copy-done((bf16[2,2,512,128]{3,2,1,0:T(8,128)(2,1)S(1)}, bf16[2,2,512,128]{3,2,1,0:T(8,128)(2,1)}, u32[]{:S(2)}) %copy-start.1) | copy-done | bytes 524312
  1.1 0.2 windows.1
  1.3 0.0 copy-start
  1.3 0.1 and_convert_fusion.masks
  1.4 21.1 %all_to_all.10 = bf16[32,88,128]{2,1,0:T(8,128)(2,1)S(1)} all-to-all(bf16[32,88,128]{2,1,0:T(8,128)(2,1)S(1)} %windows.1), channel_id=1, replica_groups={{0,1,2,3,64,65,66,67,128,129,130,131,192,193,194,195,256,257,258,259,32..., dimensions={0} | all-to-all | bytes 1441792 | tf_op jit(solution)/shard_map/all_to_all | solution.py:307
  22.5 0.0 copy-done
  22.5 0.0 copy-start.2
  22.5 0.0 copy-start.3
  22.5 1.1 %edge.1 = (bf16[2,192,128]{2,1,0:T(8,128)(2,1)S(1)}, f32[4,192,128]{2,1,0:T(8,128)S(1)}, bf16[5,160,128]{2,1,0:T(8,128)(2,1)S(1)}, bf16[5,160,128]{2,1,0:T(8,128)(2,1)S(1)}) custom-call(f32[3,24,128]{2,1,0:T(8,128)S(1)} %and_convert_fusion.masks, bf16[8,4,88,128]{3,2,1,0:T(8,128)(2,1)S(1)} %bitcast.3, bf16[3,3,3,128,128]{4,3,2,1,0:T(8,128)(2,1)S(1)} %copy-done), custom_call_target="tpu_custom_call" | custom-call | tf_op jit(solution)/shard_map/edge/pallas_call | solution.py:311
  23.6 4.1 %collective-permute-start.1 = (bf16[5,160,128]{2,1,0:T(8,128)(2,1)S(1)}, bf16[5,160,128]{2,1,0:T(8,128)(2,1)S(1)}, u32[]{:S(2)}, u32[]{:S(2)}) collective-permute-start(bf16[5,160,128]{2,1,0:T(8,128)(2,1)S(1)} %get-tuple-element.26), channel_id=1, source_target_pairs={{4,0},{5,1},{6,2},{7,3},{8,4},{9,5},{10,6},{11,7},{12,8},{13,9},{1... | collective-permute-start | bytes 614408 | tf_op jit(solution)/shard_map/ppermute | solution.py:328
  27.7 1.9 %collective-permute-start = (bf16[5,160,128]{2,1,0:T(8,128)(2,1)S(1)}, bf16[5,160,128]{2,1,0:T(8,128)(2,1)S(1)}, u32[]{:S(2)}, u32[]{:S(2)}) collective-permute-start(bf16[5,160,128]{2,1,0:T(8,128)(2,1)S(1)} %get-tuple-element.22), channel_id=1, source_target_pairs={{0,4},{1,5},{2,6},{3,7},{4,8},{5,9},{6,10},{7,11},{8,12},{9,13},{1... | collective-permute-start | bytes 614408 | tf_op jit(solution)/shard_map/ppermute | solution.py:327
  29.6 0.0 copy-done.2
  29.6 0.0 copy-done.3
  29.7 2.3 %inner.1 = (f32[4,192,128]{2,1,0:T(8,128)S(1)}, f32[4,192,128]{2,1,0:T(8,128)S(1)}, bf16[2,8,16,128]{3,2,1,0:T(8,128)(2,1)S(1)}, bf16[384,384]{1,0:T(8,128)(2,1)S(1)}, bf16[384,384]{1,0:T(8,128)(2,1)S(1)}) custom-call(f32[3,24,128]{2,1,0:T(8,128)S(1)} %and_convert_fusion.masks, bf16[8,4,88,128]{3,2,1,0:T(8,128)(2,1)S(1)} %bitcast.4, ...), custom_call_target="tpu_custom_call" | custom-call | flops 1000000000 | bytes 4000000 | tf_op jit(solution)/shard_map/inner/pallas_call | solution.py:332
  32.0 0.4 collective-permute-done.1.below
  32.5 0.7 %end.1.o_end = bf16[3,8,16,128]{3,2,1,0:T(8,128)(2,1)S(1)} custom-call(f32[3,24,128]{2,1,0:T(8,128)S(1)} %and_convert_fusion.masks, f32[4,192,128]{2,1,0:T(8,128)S(1)} %get-tuple-element.18.edges, f32[4,192,128]{2,1,0:T(8,128)S(1)} %get-tuple-element.20.known_h, f32[4,192,128]{2,1,0:T(8,128)S(1)} %get-tuple-element.21.known_o, ...), custom_call_target="tpu_custom_call" | custom-call | flops 400000000 | bytes 1000000 | tf_op jit(solution)/shard_map/end/pallas_call | solution.py:353
  33.2 4.3 %collective-permute-done.above = bf16[5,160,128]{2,1,0:T(8,128)(2,1)S(1)} collective-permute-done((bf16[5,160,128]{2,1,0:T(8,128)(2,1)S(1)}, bf16[5,160,128]{2,1,0:T(8,128)(2,1)S(1)}, u32[]{:S(2)}, u32[]{:S(2)}) %collective-permute-start) | collective-permute-done | bytes 204832 | tf_op jit(solution)/shard_map/ppermute | solution.py:327
  37.5 0.7 %top.1 = bf16[4,8,2,16,128]{4,3,2,1,0:T(8,128)(2,1)S(1)} custom-call(f32[3,24,128]{2,1,0:T(8,128)S(1)} %and_convert_fusion.masks, f32[4,192,128]{2,1,0:T(8,128)S(1)} %get-tuple-element.18.edges, f32[4,192,128]{2,1,0:T(8,128)S(1)} %get-tuple-element.20.known_h, f32[4,192,128]{2,1,0:T(8,128)S(1)} %get-tuple-element.21.known_o, ...), custom_call_target="tpu_custom_call" | custom-call | tf_op jit(solution)/shard_map/top/pallas_call | solution.py:362
  38.2 9.9 %all_to_all.11 = bf16[4,8,2,16,128]{4,3,2,1,0:T(8,128)(2,1)S(1)} all-to-all(bf16[4,8,2,16,128]{4,3,2,1,0:T(8,128)(2,1)S(1)} %top.1), channel_id=1, replica_groups={{0,1,2,3},{4,5,6,7},{8,9,10,11},{12,13,14,15},{16,17,18,19},{20,21,22,2..., dimensions={0} | all-to-all | bytes 524288 | tf_op jit(solution)/shard_map/all_to_all | solution.py:372
  48.2 0.7 %copy.5 = bf16[8,2,4,16,128]{4,3,2,1,0:T(8,128)(2,1)} copy(bf16[8,2,4,16,128]{4,3,1,0,2:T(8,128)(2,1)S(1)} %bitcast.5) | data formatting | bytes 524288 | tf_op jit(solution)/shard_map/transpose | solution.py:375
  (2 shorter events, 0.0 us)
Async XLA Ops:
  0.0 1.0 %copy-start.1 = (bf16[2,2,512,128]{3,2,1,0:T(8,128)(2,1)S(1)}, bf16[2,2,512,128]{3,2,1,0:T(8,128)(2,1)}, u32[]{:S(2)}) copy-start(bf16[2,2,512,128]{3,2,1,0:T(8,128)(2,1)} %frames.1) | copy-start | bytes 1572868
  1.3 21.2 %copy-start = (bf16[3,3,3,128,128]{4,3,2,1,0:T(8,128)(2,1)S(1)}, bf16[3,3,3,128,128]{4,3,2,1,0:T(8,128)(2,1)}, u32[]{:S(2)}) copy-start(bf16[3,3,3,128,128]{4,3,2,1,0:T(8,128)(2,1)} %weight.3) | copy-start | bytes 2654212
  22.5 7.1 %copy-start.2 = (bf16[3,3,128,128]{3,2,1,0:T(8,128)(2,1)S(1)}, bf16[3,3,128,128]{3,2,1,0:T(8,128)(2,1)}, u32[]{:S(2)}) copy-start(bf16[3,3,128,128]{3,2,1,0:T(8,128)(2,1)} %w_first.1) | copy-start | bytes 884740
  22.5 7.1 %copy-start.3 = (bf16[3,3,128,128]{3,2,1,0:T(8,128)(2,1)S(1)}, bf16[3,3,128,128]{3,2,1,0:T(8,128)(2,1)}, u32[]{:S(2)}) copy-start(bf16[3,3,128,128]{3,2,1,0:T(8,128)(2,1)} %w_second.1) | copy-start | bytes 884740
  23.6 8.9 %collective-permute-start.1 = (bf16[5,160,128]{2,1,0:T(8,128)(2,1)S(1)}, bf16[5,160,128]{2,1,0:T(8,128)(2,1)S(1)}, u32[]{:S(2)}, u32[]{:S(2)}) collective-permute-start(bf16[5,160,128]{2,1,0:T(8,128)(2,1)S(1)} %get-tuple-element.26), channel_id=1, source_target_pairs={{4,0},{5,1},{6,2},{7,3},{8,4},{9,5},{10,6},{11,7},{12,8},{13,9},{1... | collective-permute-start | bytes 614408 | tf_op jit(solution)/shard_map/ppermute | solution.py:328
  27.7 9.8 %collective-permute-start = (bf16[5,160,128]{2,1,0:T(8,128)(2,1)S(1)}, bf16[5,160,128]{2,1,0:T(8,128)(2,1)S(1)}, u32[]{:S(2)}, u32[]{:S(2)}) collective-permute-start(bf16[5,160,128]{2,1,0:T(8,128)(2,1)S(1)} %get-tuple-element.22), channel_id=1, source_target_pairs={{0,4},{1,5},{2,6},{3,7},{4,8},{5,9},{6,10},{7,11},{8,12},{9,13},{1... | collective-permute-start | bytes 614408 | tf_op jit(solution)/shard_map/ppermute | solution.py:327

commit v10 on v8

--- a/solution.py
+++ b/solution.py
@@ -104,17 +104,7 @@
 
 def pack(value):
     kept = [value[at + 1 : at + 1 + KEPT] for at in range(0, value.shape[0], SPAN)]
-    return jnp.concatenate(kept, axis=0).astype(jnp.bfloat16)
-
-
-def unpack(packed):
-    value = packed.astype(jnp.float32)
-    before = jnp.zeros((1, value.shape[1]), jnp.float32)
-    after = jnp.zeros((SPAN - KEPT - 1, value.shape[1]), jnp.float32)
-    parts = []
-    for at in range(0, value.shape[0], KEPT):
-        parts += [before, value[at : at + KEPT], after]
-    return jnp.concatenate(parts, axis=0)
+    return jnp.concatenate(kept, axis=0)
 
 
 def edge_kernel(masks, own, weight, t_edge, edges, send_down, send_up, xs):
@@ -141,14 +131,15 @@
     first, last = lower[:pitch], upper[pitch:]
     second, before = split_rows(dot_taps([[x[2]], [x[0]]], temporal_taps(weight, (2,))), pitch)
     third, after = split_rows(dot_taps([[x[3]], [x[5]]], temporal_taps(weight, (0,))), pitch)
-    edges[0], edges[1], edges[2], edges[3] = first, last, before, after
     near = inside(upper[:pitch] + second, masks[0])
     far = inside(lower[pitch:] + third, masks[0])
     t_edge[0], t_edge[1] = near.astype(jnp.bfloat16), far.astype(jnp.bfloat16)
-    for i, value in enumerate((far, last, after)):
-        send_up[i] = pack(value)
-    for i, value in enumerate((near, first, before)):
-        send_down[i] = pack(value)
+    first, last, before, after = [pack(value) for value in (first, last, before, after)]
+    edges[0], edges[1], edges[2], edges[3] = first, last, before, after
+    for i, value in enumerate((pack(far), last, after)):
+        send_up[i] = value.astype(jnp.bfloat16)
+    for i, value in enumerate((pack(near), first, before)):
+        send_down[i] = value.astype(jnp.bfloat16)
 
 
 def crop(value, frames, span):
@@ -188,7 +179,7 @@
 
 
 def inner_kernel(
-    masks, own, weight, t_edge, w_first, w_second, known_h, known_o, o_mid, w1, w2,
+    masks, own, weight, t_edge, w_first, w_second, known_h, known_o, o_mid, shown, w1, w2,
     xs, tall, hs, wt,
 ):
     frames, span = own.shape[0], SPAN
@@ -215,7 +206,7 @@
     hs[...] = inside(silu(sums), masks[0]).astype(jnp.bfloat16)
     temporal = [rows_of(tall, i, 1, pitch) for i in (0, 1, inner, inner + 1)]
     for i, value in enumerate(known_rows(*temporal, w1)):
-        known_h[i] = value
+        known_h[i] = pack(value)
 
     sums = column_taps(
         jnp.dot(row_taps(hs, 0, inner - 2, pitch), w2[...], preferred_element_type=jnp.float32)
@@ -224,38 +215,43 @@
     o_mid[...] = crop(sums, frames, span)
     hidden = [rows_of(hs, i, 1, pitch) for i in (0, 1, inner - 2, inner - 1)]
     for i, value in enumerate(known_rows(*hidden, w2)):
-        known_o[i] = value + temporal[i].astype(jnp.float32)
-
-
-def shown(value, mask):
-    return inside(value, mask).astype(jnp.bfloat16)
-
-
-def end_kernel(masks, edges, known_h, known_o, below, w1, w2, o_end):
+        known_o[i] = pack(value + temporal[i].astype(jnp.float32))
+    for i in range(3):
+        shown[i] = pack(jnp.concatenate([masks[i]] * frames, axis=0))
+
+
+def cut(value, frames):
+    kept = [value[at + HALO - 1 : at + HALO - 1 + WIDTH] for at in range(0, value.shape[0], KEPT)]
+    return jnp.concatenate(kept, axis=0).reshape(frames, WIDTH, value.shape[1]).astype(jnp.bfloat16)
+
+
+def end_kernel(shown, edges, known_h, known_o, below, w1, w2, o_end):
     rows = [
-        shown(unpack(below[2]) + edges[1], masks[0]),
-        shown(unpack(below[1]) + edges[3], masks[2]),
-        shown(unpack(below[0]), masks[2]),
+        (below[2] + edges[1]) * shown[0],
+        (below[1] + edges[3]) * shown[2],
+        below[0] * shown[2],
     ]
+    rows = [row.astype(jnp.bfloat16) for row in rows]
     hidden = end_rows(rows, w1, known_h)
-    hidden = [shown(silu(value), masks[part]) for value, part in zip(hidden, (0, 0, 2))]
+    hidden = [(silu(v) * shown[part]).astype(jnp.bfloat16) for v, part in zip(hidden, (0, 0, 2))]
     sums = end_rows(hidden, w2, known_o)
     sums[2] = sums[2] + rows[0].astype(jnp.float32)
     for i, value in enumerate(sums):
-        o_end[i] = crop(value, value.shape[0] // SPAN, SPAN)[0]
-
-
-def top_kernel(masks, edges, known_h, known_o, above, w1, w2, o_mid, o_end, out):
+        o_end[i] = cut(value, o_end.shape[1])
+
+
+def top_kernel(shown, edges, known_h, known_o, above, w1, w2, o_mid, o_end, out):
     rows = [
-        shown(unpack(above[0]), masks[1]),
-        shown(unpack(above[1]) + edges[2], masks[1]),
-        shown(unpack(above[2]) + edges[0], masks[0]),
+        above[0] * shown[1],
+        (above[1] + edges[2]) * shown[1],
+        (above[2] + edges[0]) * shown[0],
     ]
+    rows = [row.astype(jnp.bfloat16) for row in rows]
     hidden = top_rows(rows, w1, known_h)
-    hidden = [shown(silu(value), masks[part]) for value, part in zip(hidden, (1, 0, 0))]
+    hidden = [(silu(v) * shown[part]).astype(jnp.bfloat16) for v, part in zip(hidden, (1, 0, 0))]
     sums = top_rows(hidden, w2, known_o)
     sums[0] = sums[0] + rows[2].astype(jnp.float32)
-    done = [crop(value, value.shape[0] // SPAN, SPAN)[0] for value in sums]
+    done = [cut(value, out.shape[1]) for value in sums]
     done += [o_mid[i] for i in range(o_mid.shape[0])] + [o_end[i] for i in range(3)]
     each = out.shape[2]
     for row, value in enumerate(done):
@@ -277,9 +273,9 @@
     first_col = (column * SLABS + slab % SLABS) * width - HALO
     col = lax.broadcasted_iota(jnp.int32, (3, span, chans), 1) + first_col
     part = lax.broadcasted_iota(jnp.int32, (3, span, chans), 0)
-    shown = (col >= 0) & (col < col_count)
-    shown &= ((part != 1) | (plane > 0)) & ((part != 2) | (plane < planes - 1))
-    masks = shown.astype(jnp.float32)
+    visible = (col >= 0) & (col < col_count)
+    visible &= ((part != 1) | (plane > 0)) & ((part != 2) | (plane < planes - 1))
+    masks = visible.astype(jnp.float32)
     vmem = pl.BlockSpec(memory_space=pltpu.VMEM)
     params = pltpu.CompilerParams(vmem_limit_bytes=VMEM_BYTES)
 
@@ -307,7 +303,7 @@
         edge_kernel,
         out_shape=[
             brain(2, pitch, chans),
-            jax.ShapeDtypeStruct((4, pitch, chans), jnp.float32),
+            jax.ShapeDtypeStruct((4, tm * KEPT, chans), jnp.float32),
             brain(3, tm * KEPT, chans),
             brain(3, tm * KEPT, chans),
         ],
@@ -323,18 +319,19 @@
     below = lax.ppermute(send_down, "rows", [(r + SLABS, r) for r in reach])
 
     inner = plane_rows - 4
-    partial = jax.ShapeDtypeStruct((4, pitch, chans), jnp.float32)
-    known_h, known_o, o_mid, w1, w2 = pl.pallas_call(
+    partial = jax.ShapeDtypeStruct((4, tm * KEPT, chans), jnp.float32)
+    known_h, known_o, o_mid, shown, w1, w2 = pl.pallas_call(
         inner_kernel,
         out_shape=[
             partial,
             partial,
             brain(inner - 2, tm, width, chans),
+            jax.ShapeDtypeStruct((3, tm * KEPT, chans), jnp.float32),
             brain(3 * chans, 3 * chans),
             brain(3 * chans, 3 * chans),
         ],
         in_specs=[vmem] * 6,
-        out_specs=[vmem] * 5,
+        out_specs=[vmem] * 6,
         scratch_shapes=[
             held(3, (inner + 2) * pitch, chans),
             held((inner + 2) * pitch, chans),
@@ -353,7 +350,7 @@
         compiler_params=params,
         cost_estimate=pl.CostEstimate(flops=4 * 10**8, bytes_accessed=10**6, transcendentals=10**5),
         name="end",
-    )(masks, edges, known_h, known_o, below, w1, w2)
+    )(shown, edges, known_h, known_o, below, w1, w2)
     encoded = pl.pallas_call(
         top_kernel,
         out_shape=brain(SLABS, tm, row_count, width, chans),
@@ -361,7 +358,7 @@
         out_specs=vmem,
         compiler_params=params,
         name="top",
-    )(masks, edges, known_h, known_o, above, w1, w2, o_mid, o_end)
+    )(shown, edges, known_h, known_o, above, w1, w2, o_mid, o_end)
 
     groups = [[z * SLABS + j for j in range(SLABS)] for z in range(planes)]
     encoded = lax.all_to_all(

time: 47.5 us -> 47.4 us (level)
  no operation moved by 1% of the time
where the time goes in v10:
time: 47.4 us; the launch traced here: 47.2 us
  blocking collectives  31.2 us (66%)
  starting transfers between devices  6.05 us (13%)
  Pallas kernels  4.86 us (10%)
  waiting for transfers between devices  3.12 us (7%)
  local copies, waits for them, and re-layouts  1.78 us (4%)
    all_to_all x1, blocking collectives, per_device(): lax.all_to_all(cut, ('tm', 'rows'), split_axis=0, concat_axis=0, tiled=Tr...  21.1 us
    all_to_all x1, blocking collectives, per_device(): lax.all_to_all(encoded, 'rows', split_axis=0, concat_axis=0, tiled=True,...  10 us
    ppermute x1, starting transfers between devices, per_device(): below = lax.ppermute(send_down, 'rows', [(r + SLABS, r) for r in reach])  4.13 us
    ppermute x1, waiting for transfers between devices, per_device(): above = lax.ppermute(send_up, 'rows', [(r, r + SLABS) for r in reach])  3.11 us
    pallas_call x1, Pallas kernels, per_device(): pl.pallas_call(inner_kernel, out_shape=[partial, partial, brain(inner - 2...  2.35 us
    ppermute x1, starting transfers between devices, per_device(): above = lax.ppermute(send_up, 'rows', [(r, r + SLABS) for r in reach])  1.92 us
    unnamed x8, local copies, waits for them, and re-layouts  1.05 us
    pallas_call x1, Pallas kernels, per_device(): pl.pallas_call(edge_kernel, out_shape=[brain(2, pitch, chans), jax.ShapeD...  1.03 us
  transfers between devices with their start and end apart: 2, of which 1 were waited for; matrix products, arithmetic and copies ran while one was open for 0% of the time, Pallas kernels for 6%

profile of v10, /device:TPU:384, one launch (start us, length us, event | category | flops | bytes accessed | tf_op | source)
XLA Modules:
  0.0 47.2 jit_solution(16233747984030617692)
XLA Ops:
  0.0 0.0 copy-start.1
  0.0 1.0 %copy-done.1 = bf16[2,2,512,128]{3,2,1,0:T(8,128)(2,1)S(1)} copy-done((bf16[2,2,512,128]{3,2,1,0:T(8,128)(2,1)S(1)}, bf16[2,2,512,128]{3,2,1,0:T(8,128)(2,1)}, u32[]{:S(2)}) %copy-start.1) | copy-done | bytes 524312
  1.1 0.2 windows.1
  1.3 0.0 copy-start
  1.3 0.1 and_convert_fusion.masks
  1.4 21.1 %all_to_all.10 = bf16[32,88,128]{2,1,0:T(8,128)(2,1)S(1)} all-to-all(bf16[32,88,128]{2,1,0:T(8,128)(2,1)S(1)} %windows.1), channel_id=1, replica_groups={{0,1,2,3,64,65,66,67,128,129,130,131,192,193,194,195,256,257,258,259,32..., dimensions={0} | all-to-all | bytes 1441792 | tf_op jit(solution)/shard_map/all_to_all | solution.py:298
  22.5 0.0 copy-done
  22.5 0.0 copy-start.2
  22.5 0.0 copy-start.3
  22.5 1.0 %edge.1 = (bf16[2,192,128]{2,1,0:T(8,128)(2,1)S(1)}, f32[4,160,128]{2,1,0:T(8,128)S(1)}, bf16[3,160,128]{2,1,0:T(8,128)(2,1)S(1)}, bf16[3,160,128]{2,1,0:T(8,128)(2,1)S(1)}) custom-call(f32[3,24,128]{2,1,0:T(8,128)S(1)} %and_convert_fusion.masks, bf16[8,4,88,128]{3,2,1,0:T(8,128)(2,1)S(1)} %bitcast.3, bf16[3,3,3,128,128]{4,3,2,1,0:T(8,128)(2,1)S(1)} %copy-done), custom_call_target="tpu_custom_call" | custom-call | tf_op jit(solution)/shard_map/edge/pallas_call | solution.py:302
  23.5 4.1 %collective-permute-start.1 = (bf16[3,160,128]{2,1,0:T(8,128)(2,1)S(1)}, bf16[3,160,128]{2,1,0:T(8,128)(2,1)S(1)}, u32[]{:S(2)}, u32[]{:S(2)}) collective-permute-start(bf16[3,160,128]{2,1,0:T(8,128)(2,1)S(1)} %get-tuple-element.28), channel_id=1, source_target_pairs={{4,0},{5,1},{6,2},{7,3},{8,4},{9,5},{10,6},{11,7},{12,8},{13,9},{1... | collective-permute-start | bytes 368648 | tf_op jit(solution)/shard_map/ppermute | solution.py:319
  27.7 1.9 %collective-permute-start = (bf16[3,160,128]{2,1,0:T(8,128)(2,1)S(1)}, bf16[3,160,128]{2,1,0:T(8,128)(2,1)S(1)}, u32[]{:S(2)}, u32[]{:S(2)}) collective-permute-start(bf16[3,160,128]{2,1,0:T(8,128)(2,1)S(1)} %get-tuple-element.24), channel_id=1, source_target_pairs={{0,4},{1,5},{2,6},{3,7},{4,8},{5,9},{6,10},{7,11},{8,12},{9,13},{1... | collective-permute-start | bytes 368648 | tf_op jit(solution)/shard_map/ppermute | solution.py:318
  29.6 0.0 copy-done.2
  29.6 0.0 copy-done.3
  29.6 2.4 %inner.1 = (f32[4,160,128]{2,1,0:T(8,128)S(1)}, f32[4,160,128]{2,1,0:T(8,128)S(1)}, bf16[2,8,16,128]{3,2,1,0:T(8,128)(2,1)S(1)}, f32[3,160,128]{2,1,0:T(8,128)S(...) custom-call(f32[3,24,128]{2,1,0:T(8,128)S(1)} %and_convert_fusion.masks, ...), custom_call_target="tpu_custom_call" | custom-call | flops 1000000000 | bytes 4000000 | tf_op jit(solution)/shard_map/inner/pallas_call | solution.py:323
  32.0 0.0 collective-permute-done.1.below
  32.0 0.6 %end.1.o_end = bf16[3,8,16,128]{3,2,1,0:T(8,128)(2,1)S(1)} custom-call(f32[3,160,128]{2,1,0:T(8,128)S(1)} %get-tuple-element.20.shown, f32[4,160,128]{2,1,0:T(8,128)S(1)} %get-tuple-element.21.edges, f32[4,160,128]{2,1,0:T(8,128)S(1)} %get-tuple-element.22.known_h, f32[4,160,128]{2,1,0:T(8,128)S(1)} %get-tuple-element.23.known_o, ...), custom_call_target="tpu_custom_call" | custom-call | flops 400000000 | bytes 1000000 | tf_op jit(solution)/shard_map/end/pallas_call | solution.py:345
  32.6 3.1 %collective-permute-done.above = bf16[3,160,128]{2,1,0:T(8,128)(2,1)S(1)} collective-permute-done((bf16[3,160,128]{2,1,0:T(8,128)(2,1)S(1)}, bf16[3,160,128]{2,1,0:T(8,128)(2,1)S(1)}, u32[]{:S(2)}, u32[]{:S(2)}) %collective-permute-start) | collective-permute-done | bytes 122912 | tf_op jit(solution)/shard_map/ppermute | solution.py:318
  35.8 0.7 %top.1 = bf16[4,8,2,16,128]{4,3,2,1,0:T(8,128)(2,1)S(1)} custom-call(f32[3,160,128]{2,1,0:T(8,128)S(1)} %get-tuple-element.20.shown, f32[4,160,128]{2,1,0:T(8,128)S(1)} %get-tuple-element.21.edges, f32[4,160,128]{2,1,0:T(8,128)S(1)} %get-tuple-element.22.known_h, f32[4,160,128]{2,1,0:T(8,128)S(1)} %get-tuple-element.23.known_o, ...), custom_call_target="tpu_custom_call" | custom-call | tf_op jit(solution)/shard_map/top/pallas_call | solution.py:354
  36.4 10.0 %all_to_all.11 = bf16[4,8,2,16,128]{4,3,2,1,0:T(8,128)(2,1)S(1)} all-to-all(bf16[4,8,2,16,128]{4,3,2,1,0:T(8,128)(2,1)S(1)} %top.1), channel_id=1, replica_groups={{0,1,2,3},{4,5,6,7},{8,9,10,11},{12,13,14,15},{16,17,18,19},{20,21,22,2..., dimensions={0} | all-to-all | bytes 524288 | tf_op jit(solution)/shard_map/all_to_all | solution.py:364
  46.5 0.7 %copy.5 = bf16[8,2,4,16,128]{4,3,2,1,0:T(8,128)(2,1)} copy(bf16[8,2,4,16,128]{4,3,1,0,2:T(8,128)(2,1)S(1)} %bitcast.5) | data formatting | bytes 524288 | tf_op jit(solution)/shard_map/transpose | solution.py:367
  (2 shorter events, 0.0 us)
Async XLA Ops:
  0.0 1.0 %copy-start.1 = (bf16[2,2,512,128]{3,2,1,0:T(8,128)(2,1)S(1)}, bf16[2,2,512,128]{3,2,1,0:T(8,128)(2,1)}, u32[]{:S(2)}) copy-start(bf16[2,2,512,128]{3,2,1,0:T(8,128)(2,1)} %frames.1) | copy-start | bytes 1572868
  1.3 21.2 %copy-start = (bf16[3,3,3,128,128]{4,3,2,1,0:T(8,128)(2,1)S(1)}, bf16[3,3,3,128,128]{4,3,2,1,0:T(8,128)(2,1)}, u32[]{:S(2)}) copy-start(bf16[3,3,3,128,128]{4,3,2,1,0:T(8,128)(2,1)} %weight.3) | copy-start | bytes 2654212
  22.5 7.1 %copy-start.2 = (bf16[3,3,128,128]{3,2,1,0:T(8,128)(2,1)S(1)}, bf16[3,3,128,128]{3,2,1,0:T(8,128)(2,1)}, u32[]{:S(2)}) copy-start(bf16[3,3,128,128]{3,2,1,0:T(8,128)(2,1)} %w_first.1) | copy-start | bytes 884740
  22.5 7.1 %copy-start.3 = (bf16[3,3,128,128]{3,2,1,0:T(8,128)(2,1)S(1)}, bf16[3,3,128,128]{3,2,1,0:T(8,128)(2,1)}, u32[]{:S(2)}) copy-start(bf16[3,3,128,128]{3,2,1,0:T(8,128)(2,1)} %w_second.1) | copy-start | bytes 884740
  23.5 8.4 %collective-permute-start.1 = (bf16[3,160,128]{2,1,0:T(8,128)(2,1)S(1)}, bf16[3,160,128]{2,1,0:T(8,128)(2,1)S(1)}, u32[]{:S(2)}, u32[]{:S(2)}) collective-permute-start(bf16[3,160,128]{2,1,0:T(8,128)(2,1)S(1)} %get-tuple-element.28), channel_id=1, source_target_pairs={{4,0},{5,1},{6,2},{7,3},{8,4},{9,5},{10,6},{11,7},{12,8},{13,9},{1... | collective-permute-start | bytes 368648 | tf_op jit(solution)/shard_map/ppermute | solution.py:319
  27.7 8.1 %collective-permute-start = (bf16[3,160,128]{2,1,0:T(8,128)(2,1)S(1)}, bf16[3,160,128]{2,1,0:T(8,128)(2,1)S(1)}, u32[]{:S(2)}, u32[]{:S(2)}) collective-permute-start(bf16[3,160,128]{2,1,0:T(8,128)(2,1)S(1)} %get-tuple-element.24), channel_id=1, source_target_pairs={{0,4},{1,5},{2,6},{3,7},{4,8},{5,9},{6,10},{7,11},{8,12},{9,13},{1... | collective-permute-start | bytes 368648 | tf_op jit(solution)/shard_map/ppermute | solution.py:318

commit v11 on v10

--- a/solution.py
+++ b/solution.py
@@ -57,26 +57,47 @@
             wt[b * chans : (b + 1) * chans, c * chans : (c + 1) * chans] = weight[b, c]
 
 
-def frames_to(xs, at, own, row, rows_each):
-    frames, chans = own.shape[0], own.shape[3]
-    size = own.shape[2] // (2 * rows_each)
-
-    def pick(m, f):
-        part = own[m, row // rows_each].astype(jnp.float32)
-        start = (f * rows_each + row % rows_each) * size
-        part = part[start : start + SPAN]
-        if part.shape[0] < SPAN:
-            part = jnp.concatenate([part, jnp.zeros((SPAN - part.shape[0], chans), jnp.float32)], axis=0)
-        return part
-
+def part_of(rows, index, size):
+    part = rows[index * size : index * size + SPAN]
+    if part.shape[0] < SPAN:
+        none = jnp.zeros((SPAN - part.shape[0], part.shape[1]), jnp.float32)
+        part = jnp.concatenate([part, none], axis=0)
+    return part
+
+
+def frames_to(xs, at, frames, pick):
     for t in range(0, frames, 2):
         here = at + t * SPAN
         for a, f in ((1, 0), (2, 1)):
             pair = jnp.concatenate([pick(t, f), pick(t + 1, f)], axis=0)
             xs[a, here : here + 2 * SPAN] = pair.astype(jnp.bfloat16)
-        before = pick(t - 1, 1) if t else jnp.zeros((SPAN, chans), jnp.float32)
-        pair = jnp.concatenate([before, pick(t, 1)], axis=0)
-        xs[0, here : here + 2 * SPAN] = pair.astype(jnp.bfloat16)
+        last = pick(t, 1)
+        before = pick(t - 1, 1) if t else jnp.zeros_like(last)
+        xs[0, here : here + 2 * SPAN] = jnp.concatenate([before, last], axis=0).astype(jnp.bfloat16)
+
+
+def own_row(own, row):
+    rows_each = PLANE_ROWS // own.shape[1]
+    size = own.shape[2] // (2 * rows_each)
+
+    def pick(m, f):
+        part = f * rows_each + row % rows_each
+        return part_of(own[m, row // rows_each].astype(jnp.float32), part, size)
+
+    return pick
+
+
+def sent_row(below, row):
+    size = below.shape[1] // 6
+
+    def pick(m, f):
+        return part_of(below[m].astype(jnp.float32), f * 2 + row if row < 2 else 4 + f, size)
+
+    return pick
+
+
+def taps_of(xs, i, pitch):
+    return jnp.concatenate([xs[a, i * pitch : (i + 1) * pitch] for a in range(3)], axis=1)
 
 
 def silu(value):
@@ -107,39 +128,36 @@
     return jnp.concatenate(kept, axis=0)
 
 
-def edge_kernel(masks, own, weight, t_edge, edges, send_down, send_up, xs):
-    frames, span, chans = own.shape[0], SPAN, own.shape[3]
-    rows_each = PLANE_ROWS // own.shape[1]
-    rows = own.shape[1] * rows_each
-    pitch = frames * span
-
+def down_kernel(own, send):
+    size = own.shape[2] // 4
+    for m in range(own.shape[0]):
+        third = own[m, 1].astype(jnp.float32)
+        third = [third[:size], third[2 * size : 3 * size]]
+        rows = jnp.concatenate([own[m, 0].astype(jnp.float32), *third], axis=0)
+        send[m] = rows.astype(jnp.bfloat16)
+
+
+def both_taps(pair, weights):
+    deep = weights.shape[1] // 2
+    lhs = jnp.concatenate(pair, axis=1)
+    sums = jnp.dot(lhs, weights, preferred_element_type=jnp.float32)
+    return column_taps(sums[:, :deep]), column_taps(sums[:, deep:])
+
+
+def edge_kernel(masks, own, weight, far, edges, send_up, xs):
+    frames = own.shape[0]
+    pitch = frames * SPAN
     for i in range(3):
-        frames_to(xs, i * pitch, own, i, rows_each)
-        frames_to(xs, (3 + i) * pitch, own, rows - 3 + i, rows_each)
-
-    def taps_of(i):
-        return jnp.concatenate([xs[a, i * pitch : (i + 1) * pitch] for a in range(3)], axis=1)
-
-    deep = 3 * chans
-    x = [taps_of(i) for i in range(6)]
-    sums = jnp.dot(
-        jnp.concatenate([jnp.concatenate(pair, axis=1) for pair in (x[0:2], x[4:6])], axis=0),
-        jnp.concatenate([temporal_taps(weight, taps) for taps in ((1, 2), (0, 1))], axis=1),
-        preferred_element_type=jnp.float32,
-    )
-    lower, upper = column_taps(sums[:, :deep]), column_taps(sums[:, deep:])
-    first, last = lower[:pitch], upper[pitch:]
-    second, before = split_rows(dot_taps([[x[2]], [x[0]]], temporal_taps(weight, (2,))), pitch)
-    third, after = split_rows(dot_taps([[x[3]], [x[5]]], temporal_taps(weight, (0,))), pitch)
-    near = inside(upper[:pitch] + second, masks[0])
-    far = inside(lower[pitch:] + third, masks[0])
-    t_edge[0], t_edge[1] = near.astype(jnp.bfloat16), far.astype(jnp.bfloat16)
-    first, last, before, after = [pack(value) for value in (first, last, before, after)]
-    edges[0], edges[1], edges[2], edges[3] = first, last, before, after
-    for i, value in enumerate((pack(far), last, after)):
+        frames_to(xs, i * pitch, frames, own_row(own, PLANE_ROWS - 3 + i))
+    x = [taps_of(xs, i, pitch) for i in range(3)]
+    weights = jnp.concatenate([temporal_taps(weight, taps) for taps in ((1, 2), (0, 1))], axis=1)
+    lower, upper = both_taps(x[1:], weights)
+    third, after = split_rows(dot_taps([[x[0]], [x[2]]], temporal_taps(weight, (0,))), pitch)
+    value = inside(lower + third, masks[0])
+    far[...] = value.astype(jnp.bfloat16)
+    edges[0], edges[1] = last, after = pack(upper), pack(after)
+    for i, value in enumerate((pack(value), last, after)):
         send_up[i] = value.astype(jnp.bfloat16)
-    for i, value in enumerate((pack(near), first, before)):
-        send_down[i] = value.astype(jnp.bfloat16)
 
 
 def crop(value, frames, span):
@@ -179,26 +197,30 @@
 
 
 def inner_kernel(
-    masks, own, weight, t_edge, w_first, w_second, known_h, known_o, o_mid, shown, w1, w2,
+    masks, own, weight, far, w_first, w_second, edges, known_h, known_o, o_mid, shown, w1, w2,
     xs, tall, hs, wt,
 ):
-    frames, span = own.shape[0], SPAN
-    rows_each = PLANE_ROWS // own.shape[1]
-    rows = own.shape[1] * rows_each
+    frames, span, rows = own.shape[0], SPAN, PLANE_ROWS
     pitch = frames * span
+    deep = wt.shape[1]
     temporal_weight_to(wt, weight)
     plane_weight_to(w1, w_first)
     plane_weight_to(w2, w_second)
-    for row in range(1, rows - 1):
-        frames_to(xs, (row - 1) * pitch, own, row, rows_each)
+    for row in range(rows - 1):
+        frames_to(xs, row * pitch, frames, own_row(own, row))
     lhs = jnp.concatenate(
-        [xs[a, b * pitch : (b + rows - 4) * pitch] for b in range(3) for a in range(3)], axis=1
+        [xs[a, (b + 1) * pitch : (b + rows - 3) * pitch] for b in range(3) for a in range(3)], axis=1
     )
     sums = column_taps(jnp.dot(lhs, wt[...], preferred_element_type=jnp.float32))
 
-    tall[:pitch] = t_edge[0]
+    x = [taps_of(xs, i, pitch) for i in range(3)]
+    lower, upper = both_taps(x[:2], jnp.concatenate([wt[deep:], wt[: 2 * deep]], axis=1))
+    second, before = split_rows(dot_taps([[x[2]], [x[0]]], wt[2 * deep :]), pitch)
+    edges[0], edges[1] = pack(lower), pack(before)
+
+    tall[:pitch] = inside(upper + second, masks[0]).astype(jnp.bfloat16)
     tall[pitch : (rows - 3) * pitch] = inside(sums, masks[0]).astype(jnp.bfloat16)
-    tall[(rows - 3) * pitch :] = t_edge[1]
+    tall[(rows - 3) * pitch :] = far[...]
     inner = rows - 4
     sums = column_taps(
         jnp.dot(row_taps(tall, 0, inner, pitch), w1[...], preferred_element_type=jnp.float32)
@@ -225,11 +247,19 @@
     return jnp.concatenate(kept, axis=0).reshape(frames, WIDTH, value.shape[1]).astype(jnp.bfloat16)
 
 
-def end_kernel(shown, edges, known_h, known_o, below, w1, w2, o_end):
+def end_kernel(shown, weight, edges, known_h, known_o, below, w1, w2, o_end, xs):
+    frames = below.shape[0]
+    pitch = frames * SPAN
+    for i in range(3):
+        frames_to(xs, i * pitch, frames, sent_row(below, i))
+    x = [taps_of(xs, i, pitch) for i in range(3)]
+    weights = jnp.concatenate([temporal_taps(weight, taps) for taps in ((1, 2), (0, 1))], axis=1)
+    lower, upper = both_taps(x[:2], weights)
+    third, first = split_rows(dot_taps([[x[2]], [x[0]]], temporal_taps(weight, (2,))), pitch)
     rows = [
-        (below[2] + edges[1]) * shown[0],
-        (below[1] + edges[3]) * shown[2],
-        below[0] * shown[2],
+        (pack(first) + edges[0]) * shown[0],
+        (pack(lower) + edges[1]) * shown[2],
+        pack(upper + third) * shown[2],
     ]
     rows = [row.astype(jnp.bfloat16) for row in rows]
     hidden = end_rows(rows, w1, known_h)
@@ -243,7 +273,7 @@
 def top_kernel(shown, edges, known_h, known_o, above, w1, w2, o_mid, o_end, out):
     rows = [
         above[0] * shown[1],
-        (above[1] + edges[2]) * shown[1],
+        (above[1] + edges[1]) * shown[1],
         (above[2] + edges[0]) * shown[0],
     ]
     rows = [row.astype(jnp.bfloat16) for row in rows]
@@ -299,41 +329,46 @@
         cut, ("tm", "rows"), split_axis=0, concat_axis=0, tiled=True, axis_index_groups=members
     ).reshape(tm, SLABS, frame_count * row_count * size, chans)
 
-    t_edge, edges, send_down, send_up = pl.pallas_call(
+    reach = range(slabs - SLABS)
+    send_down = pl.pallas_call(
+        down_kernel,
+        out_shape=brain(tm, 6 * size, chans),
+        in_specs=[vmem],
+        out_specs=vmem,
+        compiler_params=params,
+        name="down",
+    )(own)
+    partial = jax.ShapeDtypeStruct((2, tm * KEPT, chans), jnp.float32)
+    far, edges_end, send_up = pl.pallas_call(
         edge_kernel,
-        out_shape=[
-            brain(2, pitch, chans),
-            jax.ShapeDtypeStruct((4, tm * KEPT, chans), jnp.float32),
-            brain(3, tm * KEPT, chans),
-            brain(3, tm * KEPT, chans),
-        ],
+        out_shape=[brain(pitch, chans), partial, brain(3, tm * KEPT, chans)],
         in_specs=[vmem] * 3,
-        out_specs=[vmem] * 4,
-        scratch_shapes=[held(3, 6 * pitch, chans)],
-        compiler_params=params,
+        out_specs=[vmem] * 3,
+        scratch_shapes=[held(3, 3 * pitch, chans)],
+        compiler_params=params,
+        cost_estimate=pl.CostEstimate(flops=4 * 10**8, bytes_accessed=10**6, transcendentals=0),
         name="edge",
     )(masks, own, temporal_weight)
-
-    reach = range(slabs - SLABS)
     above = lax.ppermute(send_up, "rows", [(r, r + SLABS) for r in reach])
     below = lax.ppermute(send_down, "rows", [(r + SLABS, r) for r in reach])
 
     inner = plane_rows - 4
-    partial = jax.ShapeDtypeStruct((4, tm * KEPT, chans), jnp.float32)
-    known_h, known_o, o_mid, shown, w1, w2 = pl.pallas_call(
+    known = jax.ShapeDtypeStruct((4, tm * KEPT, chans), jnp.float32)
+    edges_top, known_h, known_o, o_mid, shown, w1, w2 = pl.pallas_call(
         inner_kernel,
         out_shape=[
             partial,
-            partial,
+            known,
+            known,
             brain(inner - 2, tm, width, chans),
             jax.ShapeDtypeStruct((3, tm * KEPT, chans), jnp.float32),
             brain(3 * chans, 3 * chans),
             brain(3 * chans, 3 * chans),
         ],
         in_specs=[vmem] * 6,
-        out_specs=[vmem] * 6,
+        out_specs=[vmem] * 7,
         scratch_shapes=[
-            held(3, (inner + 2) * pitch, chans),
+            held(3, (inner + 3) * pitch, chans),
             held((inner + 2) * pitch, chans),
             held(inner * pitch, chans),
             held(9 * chans, 3 * chans),
@@ -341,16 +376,17 @@
         compiler_params=params,
         cost_estimate=pl.CostEstimate(flops=10**9, bytes_accessed=4 * 10**6, transcendentals=10**5),
         name="inner",
-    )(masks, own, temporal_weight, t_edge, first_weight, second_weight)
+    )(masks, own, temporal_weight, far, first_weight, second_weight)
     o_end = pl.pallas_call(
         end_kernel,
         out_shape=brain(3, tm, width, chans),
-        in_specs=[vmem] * 7,
+        in_specs=[vmem] * 8,
         out_specs=vmem,
+        scratch_shapes=[held(3, 3 * pitch, chans)],
         compiler_params=params,
         cost_estimate=pl.CostEstimate(flops=4 * 10**8, bytes_accessed=10**6, transcendentals=10**5),
         name="end",
-    )(shown, edges, known_h, known_o, below, w1, w2)
+    )(shown, temporal_weight, edges_end, known_h, known_o, below, w1, w2)
     encoded = pl.pallas_call(
         top_kernel,
         out_shape=brain(SLABS, tm, row_count, width, chans),
@@ -358,7 +394,7 @@
         out_specs=vmem,
         compiler_params=params,
         name="top",
-    )(shown, edges, known_h, known_o, above, w1, w2, o_mid, o_end)
+    )(shown, edges_top, known_h, known_o, above, w1, w2, o_mid, o_end)
 
     groups = [[z * SLABS + j for j in range(SLABS)] for z in range(planes)]
     encoded = lax.all_to_all(

time: 47.4 us -> 47.7 us (level)
  the two profiles are of different devices: /device:TPU:384 before, /device:TPU:1 now
where the time goes in v11:
time: 47.7 us; the launch traced here: 47.4 us
  blocking collectives  33.6 us (70%)
  Pallas kernels  5.59 us (12%)
  starting transfers between devices  5.42 us (11%)
  local copies, waits for them, and re-layouts  1.79 us (4%)
  waiting for transfers between devices  0.81 us (2%)
    all_to_all x1, blocking collectives, per_device(): lax.all_to_all(cut, ('tm', 'rows'), split_axis=0, concat_axis=0, tiled=Tr...  23.4 us
    all_to_all x1, blocking collectives, per_device(): lax.all_to_all(encoded, 'rows', split_axis=0, concat_axis=0, tiled=True,...  10.2 us
    ppermute x1, starting transfers between devices, per_device(): above = lax.ppermute(send_up, 'rows', [(r, r + SLABS) for r in reach])  3.99 us
    pallas_call x1, Pallas kernels, per_device(): pl.pallas_call(inner_kernel, out_shape=[partial, known, known, brain(inne...  2.87 us
    ppermute x1, starting transfers between devices, per_device(): below = lax.ppermute(send_down, 'rows', [(r + SLABS, r) for r in reach])  1.42 us
    pallas_call x1, Pallas kernels, per_device(): pl.pallas_call(end_kernel, out_shape=brain(3, tm, width, chans), in_specs...  1.22 us
    unnamed x8, local copies, waits for them, and re-layouts  1.06 us
  transfers between devices with their start and end apart: 2, of which 1 were waited for; matrix products, arithmetic and copies ran while one was open for 0% of the time, Pallas kernels for 10%

profile of v11, /device:TPU:1, one launch (start us, length us, event | category | flops | bytes accessed | tf_op | source)
XLA Modules:
  0.0 47.4 jit_solution(16615719270648200504)
XLA Ops:
  0.0 0.0 copy-start.1
  0.0 1.0 %copy-done.1 = bf16[2,2,512,128]{3,2,1,0:T(8,128)(2,1)S(1)} copy-done((bf16[2,2,512,128]{3,2,1,0:T(8,128)(2,1)S(1)}, bf16[2,2,512,128]{3,2,1,0:T(8,128)(2,1)}, u32[]{:S(2)}) %copy-start.1) | copy-done | bytes 524312
  1.0 0.2 windows.1
  1.3 0.1 and_convert_fusion.masks
  1.4 0.0 copy-start
  1.4 23.4 %all_to_all.10 = bf16[32,88,128]{2,1,0:T(8,128)(2,1)S(1)} all-to-all(bf16[32,88,128]{2,1,0:T(8,128)(2,1)S(1)} %windows.1), channel_id=1, replica_groups={{0,1,2,3,64,65,66,67,128,129,130,131,192,193,194,195,256,257,258,259,32..., dimensions={0} | all-to-all | bytes 1441792 | tf_op jit(solution)/shard_map/all_to_all | solution.py:328
  24.8 0.0 copy-start.2
  24.8 0.0 copy-start.3
  24.8 1.4 %collective-permute-start.1 = (bf16[8,132,128]{2,1,0:T(8,128)(2,1)S(1)}, bf16[8,132,128]{2,1,0:T(8,128)(2,1)S(1)}, u32[]{:S(2)}, u32[]{:S(2)}) collective-permute-start(bf16[8,132,128]{2,1,0:T(8,128)(2,1)S(1)} %down.1), channel_id=1, source_target_pairs={{4,0},{5,1},{6,2},{7,3},{8,4},{9,5},{10,6},{11,7},{12,8},{13,9},{1... | collective-permute-start | bytes 811016 | tf_op jit(solution)/shard_map/ppermute | solution.py:353
  26.3 0.0 copy-done
  26.3 0.6 %edge.1 = (bf16[192,128]{1,0:T(8,128)(2,1)S(1)}, f32[2,160,128]{2,1,0:T(8,128)S(1)}, bf16[3,160,128]{2,1,0:T(8,128)(2,1)S(1)}) custom-call(f32[3,24,128]{2,1,0:T(8,128)S(1)} %and_convert_fusion.masks, bf16[8,4,88,128]{3,2,1,0:T(8,128)(2,1)S(1)} %bitcast.4, bf16[3,3,3,128,128]{4,3,2,1,0:T(8,128)(2,1)S(1)} %copy-done), custom_call_target="tpu_custom_call" | custom-call | flops 400000000 | bytes 1000000 | tf_op jit(solution)/shard_map/edge/pallas_call | solution.py:342
  26.9 4.0 %collective-permute-start = (bf16[3,160,128]{2,1,0:T(8,128)(2,1)S(1)}, bf16[3,160,128]{2,1,0:T(8,128)(2,1)S(1)}, u32[]{:S(2)}, u32[]{:S(2)}) collective-permute-start(bf16[3,160,128]{2,1,0:T(8,128)(2,1)S(1)} %get-tuple-element.24), channel_id=1, source_target_pairs={{0,4},{1,5},{2,6},{3,7},{4,8},{5,9},{6,10},{7,11},{8,12},{9,13},{1... | collective-permute-start | bytes 368648 | tf_op jit(solution)/shard_map/ppermute | solution.py:352
  30.9 0.0 copy-done.2
  30.9 0.0 copy-done.3
  30.9 2.9 %inner.1 = (f32[2,160,128]{2,1,0:T(8,128)S(1)}, f32[4,160,128]{2,1,0:T(8,128)S(1)}, f32[4,160,128]{2,1,0:T(8,128)S(1)}, bf16[2,8,16,128]{3,2,1,0:T(8,128)(2,1)S(...) custom-call(f32[3,24,128]{2,1,0:T(8,128)S(1)} %and_convert_fusion.masks, ...), custom_call_target="tpu_custom_call" | custom-call | flops 1000000000 | bytes 4000000 | tf_op jit(solution)/shard_map/inner/pallas_call | solution.py:357
  33.8 0.8 %collective-permute-done.1.below = bf16[8,132,128]{2,1,0:T(8,128)(2,1)S(1)} collective-permute-done((bf16[8,132,128]{2,1,0:T(8,128)(2,1)S(1)}, bf16[8,132,128]{2,1,0:T(8,128)(2,1)S(1)}, u32[]{:S(2)}, u32[]{:S(2)}) %collective-permute-start.1) | collective-permute-done | bytes 270368 | tf_op jit(solution)/shard_map/ppermute | solution.py:353
  34.6 1.2 %end.1.o_end = bf16[3,8,16,128]{3,2,1,0:T(8,128)(2,1)S(1)} custom-call(f32[3,160,128]{2,1,0:T(8,128)S(1)} %get-tuple-element.20.shown, bf16[3,3,3,128,128]{4,3,2,1,0:T(8,128)(2,1)S(1)} %copy-done, f32[2,160,128]{2,1,0:T(8,128)S(1)} %get-tuple-element.28.edges, f32[4,160,128]{2,1,0:T(8,128)S(1)} %get-tuple-element.22.known_h, ...), custom_call_target="tpu_custom_call" | custom-call | flops 400000000 | bytes 1000000 | tf_op jit(solution)/shard_map/end/pallas_call | solution.py:380
  35.8 0.0 collective-permute-done.above
  35.8 0.6 %top.1 = bf16[4,8,2,16,128]{4,3,2,1,0:T(8,128)(2,1)S(1)} custom-call(f32[3,160,128]{2,1,0:T(8,128)S(1)} %get-tuple-element.20.shown, f32[2,160,128]{2,1,0:T(8,128)S(1)} %get-tuple-element.21.edges, f32[4,160,128]{2,1,0:T(8,128)S(1)} %get-tuple-element.22.known_h, f32[4,160,128]{2,1,0:T(8,128)S(1)} %get-tuple-element.23.known_o, ...), custom_call_target="tpu_custom_call" | custom-call | tf_op jit(solution)/shard_map/top/pallas_call | solution.py:390
  36.5 10.2 %all_to_all.11 = bf16[4,8,2,16,128]{4,3,2,1,0:T(8,128)(2,1)S(1)} all-to-all(bf16[4,8,2,16,128]{4,3,2,1,0:T(8,128)(2,1)S(1)} %top.1), channel_id=1, replica_groups={{0,1,2,3},{4,5,6,7},{8,9,10,11},{12,13,14,15},{16,17,18,19},{20,21,22,2..., dimensions={0} | all-to-all | bytes 524288 | tf_op jit(solution)/shard_map/all_to_all | solution.py:400
  46.7 0.7 %copy.5 = bf16[8,2,4,16,128]{4,3,2,1,0:T(8,128)(2,1)} copy(bf16[8,2,4,16,128]{4,3,1,0,2:T(8,128)(2,1)S(1)} %bitcast.6) | data formatting | bytes 524288 | tf_op jit(solution)/shard_map/transpose | solution.py:403
  (3 shorter events, 0.1 us)
Async XLA Ops:
  0.0 1.0 %copy-start.1 = (bf16[2,2,512,128]{3,2,1,0:T(8,128)(2,1)S(1)}, bf16[2,2,512,128]{3,2,1,0:T(8,128)(2,1)}, u32[]{:S(2)}) copy-start(bf16[2,2,512,128]{3,2,1,0:T(8,128)(2,1)} %frames.1) | copy-start | bytes 1572868
  1.4 24.9 %copy-start = (bf16[3,3,3,128,128]{4,3,2,1,0:T(8,128)(2,1)S(1)}, bf16[3,3,3,128,128]{4,3,2,1,0:T(8,128)(2,1)}, u32[]{:S(2)}) copy-start(bf16[3,3,3,128,128]{4,3,2,1,0:T(8,128)(2,1)} %weight.5) | copy-start | bytes 2654212
  24.8 6.1 %copy-start.2 = (bf16[3,3,128,128]{3,2,1,0:T(8,128)(2,1)S(1)}, bf16[3,3,128,128]{3,2,1,0:T(8,128)(2,1)}, u32[]{:S(2)}) copy-start(bf16[3,3,128,128]{3,2,1,0:T(8,128)(2,1)} %w_first.1) | copy-start | bytes 884740
  24.8 6.1 %copy-start.3 = (bf16[3,3,128,128]{3,2,1,0:T(8,128)(2,1)S(1)}, bf16[3,3,128,128]{3,2,1,0:T(8,128)(2,1)}, u32[]{:S(2)}) copy-start(bf16[3,3,128,128]{3,2,1,0:T(8,128)(2,1)} %w_second.1) | copy-start | bytes 884740
  24.8 9.8 %collective-permute-start.1 = (bf16[8,132,128]{2,1,0:T(8,128)(2,1)S(1)}, bf16[8,132,128]{2,1,0:T(8,128)(2,1)S(1)}, u32[]{:S(2)}, u32[]{:S(2)}) collective-permute-start(bf16[8,132,128]{2,1,0:T(8,128)(2,1)S(1)} %down.1), channel_id=1, source_target_pairs={{4,0},{5,1},{6,2},{7,3},{8,4},{9,5},{10,6},{11,7},{12,8},{13,9},{1... | collective-permute-start | bytes 811016 | tf_op jit(solution)/shard_map/ppermute | solution.py:353
  26.9 8.9 %collective-permute-start = (bf16[3,160,128]{2,1,0:T(8,128)(2,1)S(1)}, bf16[3,160,128]{2,1,0:T(8,128)(2,1)S(1)}, u32[]{:S(2)}, u32[]{:S(2)}) collective-permute-start(bf16[3,160,128]{2,1,0:T(8,128)(2,1)S(1)} %get-tuple-element.24), channel_id=1, source_target_pairs={{0,4},{1,5},{2,6},{3,7},{4,8},{5,9},{6,10},{7,11},{8,12},{9,13},{1... | collective-permute-start | bytes 368648 | tf_op jit(solution)/shard_map/ppermute | solution.py:352

commit v12 on v11

--- a/solution.py
+++ b/solution.py
@@ -123,6 +123,11 @@
     )
 
 
+def halves(value):
+    high = value.astype(jnp.bfloat16).astype(jnp.float32)
+    return high, value - high
+
+
 def pack(value):
     kept = [value[at + 1 : at + 1 + KEPT] for at in range(0, value.shape[0], SPAN)]
     return jnp.concatenate(kept, axis=0)
@@ -156,7 +161,7 @@
     value = inside(lower + third, masks[0])
     far[...] = value.astype(jnp.bfloat16)
     edges[0], edges[1] = last, after = pack(upper), pack(after)
-    for i, value in enumerate((pack(value), last, after)):
+    for i, value in enumerate((pack(value), *halves(last), *halves(after))):
         send_up[i] = value.astype(jnp.bfloat16)
 
 
@@ -270,11 +275,15 @@
         o_end[i] = cut(value, o_end.shape[1])
 
 
+def join(ref, i):
+    return ref[i].astype(jnp.float32) + ref[i + 1].astype(jnp.float32)
+
+
 def top_kernel(shown, edges, known_h, known_o, above, w1, w2, o_mid, o_end, out):
     rows = [
         above[0] * shown[1],
-        (above[1] + edges[1]) * shown[1],
-        (above[2] + edges[0]) * shown[0],
+        (join(above, 1) + edges[1]) * shown[1],
+        (join(above, 3) + edges[0]) * shown[0],
     ]
     rows = [row.astype(jnp.bfloat16) for row in rows]
     hidden = top_rows(rows, w1, known_h)
@@ -341,7 +350,7 @@
     partial = jax.ShapeDtypeStruct((2, tm * KEPT, chans), jnp.float32)
     far, edges_end, send_up = pl.pallas_call(
         edge_kernel,
-        out_shape=[brain(pitch, chans), partial, brain(3, tm * KEPT, chans)],
+        out_shape=[brain(pitch, chans), partial, brain(5, tm * KEPT, chans)],
         in_specs=[vmem] * 3,
         out_specs=[vmem] * 3,
         scratch_shapes=[held(3, 3 * pitch, chans)],

time: 47.7 us -> 48.9 us (1.025)
  the two profiles are of different devices: /device:TPU:1 before, /device:TPU:384 now
where the time goes in v12:
time: 48.9 us; the launch traced here: 48.7 us
  blocking collectives  31.1 us (64%)
  starting transfers between devices  6.18 us (13%)
  Pallas kernels  5.61 us (11%)
  waiting for transfers between devices  3.77 us (8%)
  local copies, waits for them, and re-layouts  1.79 us (4%)
    all_to_all x1, blocking collectives, per_device(): lax.all_to_all(cut, ('tm', 'rows'), split_axis=0, concat_axis=0, tiled=Tr...  21.2 us
    all_to_all x1, blocking collectives, per_device(): lax.all_to_all(encoded, 'rows', split_axis=0, concat_axis=0, tiled=True,...  9.93 us
    ppermute x1, starting transfers between devices, per_device(): below = lax.ppermute(send_down, 'rows', [(r + SLABS, r) for r in reach])  4.26 us
    ppermute x1, waiting for transfers between devices, per_device(): above = lax.ppermute(send_up, 'rows', [(r, r + SLABS) for r in reach])  2.9 us
    pallas_call x1, Pallas kernels, per_device(): pl.pallas_call(inner_kernel, out_shape=[partial, known, known, brain(inne...  2.87 us
    ppermute x1, starting transfers between devices, per_device(): above = lax.ppermute(send_up, 'rows', [(r, r + SLABS) for r in reach])  1.92 us
    pallas_call x1, Pallas kernels, per_device(): pl.pallas_call(end_kernel, out_shape=brain(3, tm, width, chans), in_specs...  1.22 us
    unnamed x8, local copies, waits for them, and re-layouts  1.06 us
  transfers between devices with their start and end apart: 2, of which 2 were waited for; matrix products, arithmetic and copies ran while one was open for 0% of the time, Pallas kernels for 10%

profile of v12, /device:TPU:384, one launch (start us, length us, event | category | flops | bytes accessed | tf_op | source)
XLA Modules:
  0.0 48.7 jit_solution(708482803527622171)
XLA Ops:
  0.0 0.0 copy-start.1
  0.0 1.0 %copy-done.1 = bf16[2,2,512,128]{3,2,1,0:T(8,128)(2,1)S(1)} copy-done((bf16[2,2,512,128]{3,2,1,0:T(8,128)(2,1)S(1)}, bf16[2,2,512,128]{3,2,1,0:T(8,128)(2,1)}, u32[]{:S(2)}) %copy-start.1) | copy-done | bytes 524312
  1.0 0.2 windows.1
  1.3 0.1 and_convert_fusion.masks
  1.4 0.0 copy-start
  1.4 21.2 %all_to_all.10 = bf16[32,88,128]{2,1,0:T(8,128)(2,1)S(1)} all-to-all(bf16[32,88,128]{2,1,0:T(8,128)(2,1)S(1)} %windows.1), channel_id=1, replica_groups={{0,1,2,3,64,65,66,67,128,129,130,131,192,193,194,195,256,257,258,259,32..., dimensions={0} | all-to-all | bytes 1441792 | tf_op jit(solution)/shard_map/all_to_all | solution.py:337
  22.6 0.0 copy-start.2
  22.6 0.0 copy-start.3
  22.6 4.3 %collective-permute-start.1 = (bf16[8,132,128]{2,1,0:T(8,128)(2,1)S(1)}, bf16[8,132,128]{2,1,0:T(8,128)(2,1)S(1)}, u32[]{:S(2)}, u32[]{:S(2)}) collective-permute-start(bf16[8,132,128]{2,1,0:T(8,128)(2,1)S(1)} %down.1), channel_id=1, source_target_pairs={{4,0},{5,1},{6,2},{7,3},{8,4},{9,5},{10,6},{11,7},{12,8},{13,9},{1... | collective-permute-start | bytes 811016 | tf_op jit(solution)/shard_map/ppermute | solution.py:362
  26.9 0.0 copy-done
  26.9 0.6 %edge.1 = (bf16[192,128]{1,0:T(8,128)(2,1)S(1)}, f32[2,160,128]{2,1,0:T(8,128)S(1)}, bf16[5,160,128]{2,1,0:T(8,128)(2,1)S(1)}) custom-call(f32[3,24,128]{2,1,0:T(8,128)S(1)} %and_convert_fusion.masks, bf16[8,4,88,128]{3,2,1,0:T(8,128)(2,1)S(1)} %bitcast.4, bf16[3,3,3,128,128]{4,3,2,1,0:T(8,128)(2,1)S(1)} %copy-done), custom_call_target="tpu_custom_call" | custom-call | flops 400000000 | bytes 1000000 | tf_op jit(solution)/shard_map/edge/pallas_call | solution.py:351
  27.5 1.9 %collective-permute-start = (bf16[5,160,128]{2,1,0:T(8,128)(2,1)S(1)}, bf16[5,160,128]{2,1,0:T(8,128)(2,1)S(1)}, u32[]{:S(2)}, u32[]{:S(2)}) collective-permute-start(bf16[5,160,128]{2,1,0:T(8,128)(2,1)S(1)} %get-tuple-element.24), channel_id=1, source_target_pairs={{0,4},{1,5},{2,6},{3,7},{4,8},{5,9},{6,10},{7,11},{8,12},{9,13},{1... | collective-permute-start | bytes 614408 | tf_op jit(solution)/shard_map/ppermute | solution.py:361
  29.5 0.0 copy-done.2
  29.5 0.0 copy-done.3
  29.5 2.9 %inner.1 = (f32[2,160,128]{2,1,0:T(8,128)S(1)}, f32[4,160,128]{2,1,0:T(8,128)S(1)}, f32[4,160,128]{2,1,0:T(8,128)S(1)}, bf16[2,8,16,128]{3,2,1,0:T(8,128)(2,1)S(...) custom-call(f32[3,24,128]{2,1,0:T(8,128)S(1)} %and_convert_fusion.masks, ...), custom_call_target="tpu_custom_call" | custom-call | flops 1000000000 | bytes 4000000 | tf_op jit(solution)/shard_map/inner/pallas_call | solution.py:366
  32.3 0.9 %collective-permute-done.1.below = bf16[8,132,128]{2,1,0:T(8,128)(2,1)S(1)} collective-permute-done((bf16[8,132,128]{2,1,0:T(8,128)(2,1)S(1)}, bf16[8,132,128]{2,1,0:T(8,128)(2,1)S(1)}, u32[]{:S(2)}, u32[]{:S(2)}) %collective-permute-start.1) | collective-permute-done | bytes 270368 | tf_op jit(solution)/shard_map/ppermute | solution.py:362
  33.2 1.2 %end.1.o_end = bf16[3,8,16,128]{3,2,1,0:T(8,128)(2,1)S(1)} custom-call(f32[3,160,128]{2,1,0:T(8,128)S(1)} %get-tuple-element.20.shown, bf16[3,3,3,128,128]{4,3,2,1,0:T(8,128)(2,1)S(1)} %copy-done, f32[2,160,128]{2,1,0:T(8,128)S(1)} %get-tuple-element.28.edges, f32[4,160,128]{2,1,0:T(8,128)S(1)} %get-tuple-element.22.known_h, ...), custom_call_target="tpu_custom_call" | custom-call | flops 400000000 | bytes 1000000 | tf_op jit(solution)/shard_map/end/pallas_call | solution.py:389
  34.4 2.9 %collective-permute-done.above = bf16[5,160,128]{2,1,0:T(8,128)(2,1)S(1)} collective-permute-done((bf16[5,160,128]{2,1,0:T(8,128)(2,1)S(1)}, bf16[5,160,128]{2,1,0:T(8,128)(2,1)S(1)}, u32[]{:S(2)}, u32[]{:S(2)}) %collective-permute-start) | collective-permute-done | bytes 204832 | tf_op jit(solution)/shard_map/ppermute | solution.py:361
  37.4 0.6 %top.1 = bf16[4,8,2,16,128]{4,3,2,1,0:T(8,128)(2,1)S(1)} custom-call(f32[3,160,128]{2,1,0:T(8,128)S(1)} %get-tuple-element.20.shown, f32[2,160,128]{2,1,0:T(8,128)S(1)} %get-tuple-element.21.edges, f32[4,160,128]{2,1,0:T(8,128)S(1)} %get-tuple-element.22.known_h, f32[4,160,128]{2,1,0:T(8,128)S(1)} %get-tuple-element.23.known_o, ...), custom_call_target="tpu_custom_call" | custom-call | tf_op jit(solution)/shard_map/top/pallas_call | solution.py:399
  38.0 9.9 %all_to_all.11 = bf16[4,8,2,16,128]{4,3,2,1,0:T(8,128)(2,1)S(1)} all-to-all(bf16[4,8,2,16,128]{4,3,2,1,0:T(8,128)(2,1)S(1)} %top.1), channel_id=1, replica_groups={{0,1,2,3},{4,5,6,7},{8,9,10,11},{12,13,14,15},{16,17,18,19},{20,21,22,2..., dimensions={0} | all-to-all | bytes 524288 | tf_op jit(solution)/shard_map/all_to_all | solution.py:409
  47.9 0.7 %copy.5 = bf16[8,2,4,16,128]{4,3,2,1,0:T(8,128)(2,1)} copy(bf16[8,2,4,16,128]{4,3,1,0,2:T(8,128)(2,1)S(1)} %bitcast.6) | data formatting | bytes 524288 | tf_op jit(solution)/shard_map/transpose | solution.py:412
  (3 shorter events, 0.1 us)
Async XLA Ops:
  0.0 1.0 %copy-start.1 = (bf16[2,2,512,128]{3,2,1,0:T(8,128)(2,1)S(1)}, bf16[2,2,512,128]{3,2,1,0:T(8,128)(2,1)}, u32[]{:S(2)}) copy-start(bf16[2,2,512,128]{3,2,1,0:T(8,128)(2,1)} %frames.1) | copy-start | bytes 1572868
  1.4 25.5 %copy-start = (bf16[3,3,3,128,128]{4,3,2,1,0:T(8,128)(2,1)S(1)}, bf16[3,3,3,128,128]{4,3,2,1,0:T(8,128)(2,1)}, u32[]{:S(2)}) copy-start(bf16[3,3,3,128,128]{4,3,2,1,0:T(8,128)(2,1)} %weight.5) | copy-start | bytes 2654212
  22.6 6.9 %copy-start.2 = (bf16[3,3,128,128]{3,2,1,0:T(8,128)(2,1)S(1)}, bf16[3,3,128,128]{3,2,1,0:T(8,128)(2,1)}, u32[]{:S(2)}) copy-start(bf16[3,3,128,128]{3,2,1,0:T(8,128)(2,1)} %w_first.1) | copy-start | bytes 884740
  22.6 6.9 %copy-start.3 = (bf16[3,3,128,128]{3,2,1,0:T(8,128)(2,1)S(1)}, bf16[3,3,128,128]{3,2,1,0:T(8,128)(2,1)}, u32[]{:S(2)}) copy-start(bf16[3,3,128,128]{3,2,1,0:T(8,128)(2,1)} %w_second.1) | copy-start | bytes 884740
  22.6 10.6 %collective-permute-start.1 = (bf16[8,132,128]{2,1,0:T(8,128)(2,1)S(1)}, bf16[8,132,128]{2,1,0:T(8,128)(2,1)S(1)}, u32[]{:S(2)}, u32[]{:S(2)}) collective-permute-start(bf16[8,132,128]{2,1,0:T(8,128)(2,1)S(1)} %down.1), channel_id=1, source_target_pairs={{4,0},{5,1},{6,2},{7,3},{8,4},{9,5},{10,6},{11,7},{12,8},{13,9},{1... | collective-permute-start | bytes 811016 | tf_op jit(solution)/shard_map/ppermute | solution.py:362
  27.5 9.8 %collective-permute-start = (bf16[5,160,128]{2,1,0:T(8,128)(2,1)S(1)}, bf16[5,160,128]{2,1,0:T(8,128)(2,1)S(1)}, u32[]{:S(2)}, u32[]{:S(2)}) collective-permute-start(bf16[5,160,128]{2,1,0:T(8,128)(2,1)S(1)} %get-tuple-element.24), channel_id=1, source_target_pairs={{0,4},{1,5},{2,6},{3,7},{4,8},{5,9},{6,10},{7,11},{8,12},{9,13},{1... | collective-permute-start | bytes 614408 | tf_op jit(solution)/shard_map/ppermute | solution.py:361

commit v13 on v10

--- a/solution.py
+++ b/solution.py
@@ -164,18 +164,28 @@
     return split_rows(top, pitch) + split_rows(end, pitch)
 
 
+def pair_rows(pair, weight):
+    deep, chans = weight.shape[1], weight.shape[0] // 3
+    sums = jnp.dot(
+        jnp.concatenate(pair, axis=1),
+        jnp.concatenate([weight[chans:], weight[: 2 * chans]], axis=1),
+        preferred_element_type=jnp.float32,
+    )
+    return column_taps(sums[:, :deep]), column_taps(sums[:, deep:])
+
+
 def top_rows(rows, weight, known):
-    none, chans = jnp.zeros_like(rows[0]), rows[0].shape[1]
-    first = dot_taps([rows], weight[...])
-    near = split_rows(dot_taps([rows[1:], [rows[2], none]], weight[: 2 * chans]), none.shape[0])
-    return [first, near[0] + known[0], near[1] + known[1]]
+    pitch, chans = rows[0].shape
+    lower, upper = pair_rows(rows[1:], weight)
+    through = split_rows(dot_taps([[rows[0]], [rows[2]]], weight[:chans]), pitch)
+    return [lower + through[0], upper + known[0], through[1] + known[1]]
 
 
 def end_rows(rows, weight, known):
-    none, chans = jnp.zeros_like(rows[0]), rows[0].shape[1]
-    last = dot_taps([rows], weight[...])
-    far = split_rows(dot_taps([[none, rows[0]], rows[:2]], weight[chans:]), none.shape[0])
-    return [far[0] + known[2], far[1] + known[3], last]
+    pitch, chans = rows[0].shape
+    lower, upper = pair_rows(rows[:2], weight)
+    through = split_rows(dot_taps([[rows[0]], [rows[2]]], weight[2 * chans :]), pitch)
+    return [through[0] + known[2], lower + known[3], upper + through[1]]
 
 
 def inner_kernel(

time: 47.4 us -> 47.4 us (level)
  no operation moved by 1% of the time
where the time goes in v13:
time: 47.4 us; the launch traced here: 47.1 us
  blocking collectives  31.2 us (66%)
  starting transfers between devices  6.05 us (13%)
  Pallas kernels  4.77 us (10%)
  waiting for transfers between devices  3.15 us (7%)
  local copies, waits for them, and re-layouts  1.78 us (4%)
    all_to_all x1, blocking collectives, per_device(): lax.all_to_all(cut, ('tm', 'rows'), split_axis=0, concat_axis=0, tiled=Tr...  21.1 us
    all_to_all x1, blocking collectives, per_device(): lax.all_to_all(encoded, 'rows', split_axis=0, concat_axis=0, tiled=True,...  10 us
    ppermute x1, starting transfers between devices, per_device(): below = lax.ppermute(send_down, 'rows', [(r + SLABS, r) for r in reach])  4.13 us
    ppermute x1, waiting for transfers between devices, per_device(): above = lax.ppermute(send_up, 'rows', [(r, r + SLABS) for r in reach])  3.15 us
    pallas_call x1, Pallas kernels, per_device(): pl.pallas_call(inner_kernel, out_shape=[partial, partial, brain(inner - 2...  2.35 us
    ppermute x1, starting transfers between devices, per_device(): above = lax.ppermute(send_up, 'rows', [(r, r + SLABS) for r in reach])  1.92 us
    unnamed x8, local copies, waits for them, and re-layouts  1.05 us
    pallas_call x1, Pallas kernels, per_device(): pl.pallas_call(edge_kernel, out_shape=[brain(2, pitch, chans), jax.ShapeD...  1.03 us
  transfers between devices with their start and end apart: 2, of which 1 were waited for; matrix products, arithmetic and copies ran while one was open for 0% of the time, Pallas kernels for 6%

profile of v13, /device:TPU:384, one launch (start us, length us, event | category | flops | bytes accessed | tf_op | source)
XLA Modules:
  0.0 47.1 jit_solution(17851202934383546723)
XLA Ops:
  0.0 0.0 copy-start.1
  0.0 1.0 %copy-done.1 = bf16[2,2,512,128]{3,2,1,0:T(8,128)(2,1)S(1)} copy-done((bf16[2,2,512,128]{3,2,1,0:T(8,128)(2,1)S(1)}, bf16[2,2,512,128]{3,2,1,0:T(8,128)(2,1)}, u32[]{:S(2)}) %copy-start.1) | copy-done | bytes 524312
  1.1 0.2 windows.1
  1.3 0.0 copy-start
  1.3 0.1 and_convert_fusion.masks
  1.4 21.1 %all_to_all.10 = bf16[32,88,128]{2,1,0:T(8,128)(2,1)S(1)} all-to-all(bf16[32,88,128]{2,1,0:T(8,128)(2,1)S(1)} %windows.1), channel_id=1, replica_groups={{0,1,2,3,64,65,66,67,128,129,130,131,192,193,194,195,256,257,258,259,32..., dimensions={0} | all-to-all | bytes 1441792 | tf_op jit(solution)/shard_map/all_to_all | solution.py:308
  22.5 0.0 copy-done
  22.5 0.0 copy-start.2
  22.5 0.0 copy-start.3
  22.5 1.0 %edge.1 = (bf16[2,192,128]{2,1,0:T(8,128)(2,1)S(1)}, f32[4,160,128]{2,1,0:T(8,128)S(1)}, bf16[3,160,128]{2,1,0:T(8,128)(2,1)S(1)}, bf16[3,160,128]{2,1,0:T(8,128)(2,1)S(1)}) custom-call(f32[3,24,128]{2,1,0:T(8,128)S(1)} %and_convert_fusion.masks, bf16[8,4,88,128]{3,2,1,0:T(8,128)(2,1)S(1)} %bitcast.3, bf16[3,3,3,128,128]{4,3,2,1,0:T(8,128)(2,1)S(1)} %copy-done), custom_call_target="tpu_custom_call" | custom-call | tf_op jit(solution)/shard_map/edge/pallas_call | solution.py:312
  23.5 4.1 %collective-permute-start.1 = (bf16[3,160,128]{2,1,0:T(8,128)(2,1)S(1)}, bf16[3,160,128]{2,1,0:T(8,128)(2,1)S(1)}, u32[]{:S(2)}, u32[]{:S(2)}) collective-permute-start(bf16[3,160,128]{2,1,0:T(8,128)(2,1)S(1)} %get-tuple-element.28), channel_id=1, source_target_pairs={{4,0},{5,1},{6,2},{7,3},{8,4},{9,5},{10,6},{11,7},{12,8},{13,9},{1... | collective-permute-start | bytes 368648 | tf_op jit(solution)/shard_map/ppermute | solution.py:329
  27.7 1.9 %collective-permute-start = (bf16[3,160,128]{2,1,0:T(8,128)(2,1)S(1)}, bf16[3,160,128]{2,1,0:T(8,128)(2,1)S(1)}, u32[]{:S(2)}, u32[]{:S(2)}) collective-permute-start(bf16[3,160,128]{2,1,0:T(8,128)(2,1)S(1)} %get-tuple-element.24), channel_id=1, source_target_pairs={{0,4},{1,5},{2,6},{3,7},{4,8},{5,9},{6,10},{7,11},{8,12},{9,13},{1... | collective-permute-start | bytes 368648 | tf_op jit(solution)/shard_map/ppermute | solution.py:328
  29.6 0.0 copy-done.2
  29.6 0.0 copy-done.3
  29.6 2.4 %inner.1 = (f32[4,160,128]{2,1,0:T(8,128)S(1)}, f32[4,160,128]{2,1,0:T(8,128)S(1)}, bf16[2,8,16,128]{3,2,1,0:T(8,128)(2,1)S(1)}, f32[3,160,128]{2,1,0:T(8,128)S(...) custom-call(f32[3,24,128]{2,1,0:T(8,128)S(1)} %and_convert_fusion.masks, ...), custom_call_target="tpu_custom_call" | custom-call | flops 1000000000 | bytes 4000000 | tf_op jit(solution)/shard_map/inner/pallas_call | solution.py:333
  32.0 0.0 collective-permute-done.1.below
  32.0 0.6 %end.1.o_end = bf16[3,8,16,128]{3,2,1,0:T(8,128)(2,1)S(1)} custom-call(f32[3,160,128]{2,1,0:T(8,128)S(1)} %get-tuple-element.20.shown, f32[4,160,128]{2,1,0:T(8,128)S(1)} %get-tuple-element.21.edges, f32[4,160,128]{2,1,0:T(8,128)S(1)} %get-tuple-element.22.known_h, f32[4,160,128]{2,1,0:T(8,128)S(1)} %get-tuple-element.23.known_o, ...), custom_call_target="tpu_custom_call" | custom-call | flops 400000000 | bytes 1000000 | tf_op jit(solution)/shard_map/end/pallas_call | solution.py:355
  32.6 3.1 %collective-permute-done.above = bf16[3,160,128]{2,1,0:T(8,128)(2,1)S(1)} collective-permute-done((bf16[3,160,128]{2,1,0:T(8,128)(2,1)S(1)}, bf16[3,160,128]{2,1,0:T(8,128)(2,1)S(1)}, u32[]{:S(2)}, u32[]{:S(2)}) %collective-permute-start) | collective-permute-done | bytes 122912 | tf_op jit(solution)/shard_map/ppermute | solution.py:328
  35.8 0.6 %top.1 = bf16[4,8,2,16,128]{4,3,2,1,0:T(8,128)(2,1)S(1)} custom-call(f32[3,160,128]{2,1,0:T(8,128)S(1)} %get-tuple-element.20.shown, f32[4,160,128]{2,1,0:T(8,128)S(1)} %get-tuple-element.21.edges, f32[4,160,128]{2,1,0:T(8,128)S(1)} %get-tuple-element.22.known_h, f32[4,160,128]{2,1,0:T(8,128)S(1)} %get-tuple-element.23.known_o, ...), custom_call_target="tpu_custom_call" | custom-call | tf_op jit(solution)/shard_map/top/pallas_call | solution.py:364
  36.4 10.0 %all_to_all.11 = bf16[4,8,2,16,128]{4,3,2,1,0:T(8,128)(2,1)S(1)} all-to-all(bf16[4,8,2,16,128]{4,3,2,1,0:T(8,128)(2,1)S(1)} %top.1), channel_id=1, replica_groups={{0,1,2,3},{4,5,6,7},{8,9,10,11},{12,13,14,15},{16,17,18,19},{20,21,22,2..., dimensions={0} | all-to-all | bytes 524288 | tf_op jit(solution)/shard_map/all_to_all | solution.py:374
  46.4 0.7 %copy.5 = bf16[8,2,4,16,128]{4,3,2,1,0:T(8,128)(2,1)} copy(bf16[8,2,4,16,128]{4,3,1,0,2:T(8,128)(2,1)S(1)} %bitcast.5) | data formatting | bytes 524288 | tf_op jit(solution)/shard_map/transpose | solution.py:377
  (2 shorter events, 0.0 us)
Async XLA Ops:
  0.0 1.0 %copy-start.1 = (bf16[2,2,512,128]{3,2,1,0:T(8,128)(2,1)S(1)}, bf16[2,2,512,128]{3,2,1,0:T(8,128)(2,1)}, u32[]{:S(2)}) copy-start(bf16[2,2,512,128]{3,2,1,0:T(8,128)(2,1)} %frames.1) | copy-start | bytes 1572868
  1.3 21.2 %copy-start = (bf16[3,3,3,128,128]{4,3,2,1,0:T(8,128)(2,1)S(1)}, bf16[3,3,3,128,128]{4,3,2,1,0:T(8,128)(2,1)}, u32[]{:S(2)}) copy-start(bf16[3,3,3,128,128]{4,3,2,1,0:T(8,128)(2,1)} %weight.3) | copy-start | bytes 2654212
  22.5 7.1 %copy-start.2 = (bf16[3,3,128,128]{3,2,1,0:T(8,128)(2,1)S(1)}, bf16[3,3,128,128]{3,2,1,0:T(8,128)(2,1)}, u32[]{:S(2)}) copy-start(bf16[3,3,128,128]{3,2,1,0:T(8,128)(2,1)} %w_first.1) | copy-start | bytes 884740
  22.5 7.1 %copy-start.3 = (bf16[3,3,128,128]{3,2,1,0:T(8,128)(2,1)S(1)}, bf16[3,3,128,128]{3,2,1,0:T(8,128)(2,1)}, u32[]{:S(2)}) copy-start(bf16[3,3,128,128]{3,2,1,0:T(8,128)(2,1)} %w_second.1) | copy-start | bytes 884740
  23.5 8.4 %collective-permute-start.1 = (bf16[3,160,128]{2,1,0:T(8,128)(2,1)S(1)}, bf16[3,160,128]{2,1,0:T(8,128)(2,1)S(1)}, u32[]{:S(2)}, u32[]{:S(2)}) collective-permute-start(bf16[3,160,128]{2,1,0:T(8,128)(2,1)S(1)} %get-tuple-element.28), channel_id=1, source_target_pairs={{4,0},{5,1},{6,2},{7,3},{8,4},{9,5},{10,6},{11,7},{12,8},{13,9},{1... | collective-permute-start | bytes 368648 | tf_op jit(solution)/shard_map/ppermute | solution.py:329
  27.7 8.1 %collective-permute-start = (bf16[3,160,128]{2,1,0:T(8,128)(2,1)S(1)}, bf16[3,160,128]{2,1,0:T(8,128)(2,1)S(1)}, u32[]{:S(2)}, u32[]{:S(2)}) collective-permute-start(bf16[3,160,128]{2,1,0:T(8,128)(2,1)S(1)} %get-tuple-element.24), channel_id=1, source_target_pairs={{0,4},{1,5},{2,6},{3,7},{4,8},{5,9},{6,10},{7,11},{8,12},{9,13},{1... | collective-permute-start | bytes 368648 | tf_op jit(solution)/shard_map/ppermute | solution.py:328

commit v14 on v13

--- a/solution.py
+++ b/solution.py
@@ -107,39 +107,31 @@
     return jnp.concatenate(kept, axis=0)
 
 
-def edge_kernel(masks, own, weight, t_edge, edges, send_down, send_up, xs):
-    frames, span, chans = own.shape[0], SPAN, own.shape[3]
-    rows_each = PLANE_ROWS // own.shape[1]
-    rows = own.shape[1] * rows_each
-    pitch = frames * span
-
+def side_kernel(at, masks, own, weight, near, edges, send, xs):
+    frames, chans = own.shape[0], own.shape[3]
+    pitch = frames * SPAN
+    deep = 3 * chans
     for i in range(3):
-        frames_to(xs, i * pitch, own, i, rows_each)
-        frames_to(xs, (3 + i) * pitch, own, rows - 3 + i, rows_each)
-
-    def taps_of(i):
-        return jnp.concatenate([xs[a, i * pitch : (i + 1) * pitch] for a in range(3)], axis=1)
-
-    deep = 3 * chans
-    x = [taps_of(i) for i in range(6)]
+        frames_to(xs, i * pitch, own, at + i, PLANE_ROWS // own.shape[1])
+    x = [
+        jnp.concatenate([xs[a, i * pitch : (i + 1) * pitch] for a in range(3)], axis=1)
+        for i in range(3)
+    ]
+    pair, (inner, outer), tap = (x[:2], (x[2], x[0]), 2) if at == 0 else (x[1:], (x[0], x[2]), 0)
     sums = jnp.dot(
-        jnp.concatenate([jnp.concatenate(pair, axis=1) for pair in (x[0:2], x[4:6])], axis=0),
+        jnp.concatenate(pair, axis=1),
         jnp.concatenate([temporal_taps(weight, taps) for taps in ((1, 2), (0, 1))], axis=1),
         preferred_element_type=jnp.float32,
     )
     lower, upper = column_taps(sums[:, :deep]), column_taps(sums[:, deep:])
-    first, last = lower[:pitch], upper[pitch:]
-    second, before = split_rows(dot_taps([[x[2]], [x[0]]], temporal_taps(weight, (2,))), pitch)
-    third, after = split_rows(dot_taps([[x[3]], [x[5]]], temporal_taps(weight, (0,))), pitch)
-    near = inside(upper[:pitch] + second, masks[0])
-    far = inside(lower[pitch:] + third, masks[0])
-    t_edge[0], t_edge[1] = near.astype(jnp.bfloat16), far.astype(jnp.bfloat16)
-    first, last, before, after = [pack(value) for value in (first, last, before, after)]
-    edges[0], edges[1], edges[2], edges[3] = first, last, before, after
-    for i, value in enumerate((pack(far), last, after)):
-        send_up[i] = value.astype(jnp.bfloat16)
-    for i, value in enumerate((pack(near), first, before)):
-        send_down[i] = value.astype(jnp.bfloat16)
+    part, whole = (lower, upper) if at == 0 else (upper, lower)
+    more, beside = split_rows(dot_taps([[inner], [outer]], temporal_taps(weight, (tap,))), pitch)
+    whole = inside(whole + more, masks[0])
+    near[...] = whole.astype(jnp.bfloat16)
+    part, beside = pack(part), pack(beside)
+    edges[0], edges[1] = part, beside
+    for i, value in enumerate((pack(whole), part, beside)):
+        send[i] = value.astype(jnp.bfloat16)
 
 
 def crop(value, frames, span):
@@ -189,7 +181,7 @@
 
 
 def inner_kernel(
-    masks, own, weight, t_edge, w_first, w_second, known_h, known_o, o_mid, shown, w1, w2,
+    masks, own, weight, near, far, w_first, w_second, known_h, known_o, o_mid, shown, w1, w2,
     xs, tall, hs, wt,
 ):
     frames, span = own.shape[0], SPAN
@@ -206,9 +198,9 @@
     )
     sums = column_taps(jnp.dot(lhs, wt[...], preferred_element_type=jnp.float32))
 
-    tall[:pitch] = t_edge[0]
+    tall[:pitch] = near[...]
     tall[pitch : (rows - 3) * pitch] = inside(sums, masks[0]).astype(jnp.bfloat16)
-    tall[(rows - 3) * pitch :] = t_edge[1]
+    tall[(rows - 3) * pitch :] = far[...]
     inner = rows - 4
     sums = column_taps(
         jnp.dot(row_taps(tall, 0, inner, pitch), w1[...], preferred_element_type=jnp.float32)
@@ -237,8 +229,8 @@
 
 def end_kernel(shown, edges, known_h, known_o, below, w1, w2, o_end):
     rows = [
-        (below[2] + edges[1]) * shown[0],
-        (below[1] + edges[3]) * shown[2],
+        (below[2] + edges[0]) * shown[0],
+        (below[1] + edges[1]) * shown[2],
         below[0] * shown[2],
     ]
     rows = [row.astype(jnp.bfloat16) for row in rows]
@@ -253,7 +245,7 @@
 def top_kernel(shown, edges, known_h, known_o, above, w1, w2, o_mid, o_end, out):
     rows = [
         above[0] * shown[1],
-        (above[1] + edges[2]) * shown[1],
+        (above[1] + edges[1]) * shown[1],
         (above[2] + edges[0]) * shown[0],
     ]
     rows = [row.astype(jnp.bfloat16) for row in rows]
@@ -309,20 +301,24 @@
         cut, ("tm", "rows"), split_axis=0, concat_axis=0, tiled=True, axis_index_groups=members
     ).reshape(tm, SLABS, frame_count * row_count * size, chans)
 
-    t_edge, edges, send_down, send_up = pl.pallas_call(
-        edge_kernel,
-        out_shape=[
-            brain(2, pitch, chans),
-            jax.ShapeDtypeStruct((4, tm * KEPT, chans), jnp.float32),
-            brain(3, tm * KEPT, chans),
-            brain(3, tm * KEPT, chans),
-        ],
-        in_specs=[vmem] * 3,
-        out_specs=[vmem] * 4,
-        scratch_shapes=[held(3, 6 * pitch, chans)],
-        compiler_params=params,
-        name="edge",
-    )(masks, own, temporal_weight)
+    def side(at, name):
+        return pl.pallas_call(
+            lambda *refs: side_kernel(at, *refs),
+            out_shape=[
+                brain(pitch, chans),
+                jax.ShapeDtypeStruct((2, tm * KEPT, chans), jnp.float32),
+                brain(3, tm * KEPT, chans),
+            ],
+            in_specs=[vmem] * 3,
+            out_specs=[vmem] * 3,
+            scratch_shapes=[held(3, 3 * pitch, chans)],
+            compiler_params=params,
+            cost_estimate=pl.CostEstimate(flops=4 * 10**8, bytes_accessed=10**6, transcendentals=0),
+            name=name,
+        )(masks, own, temporal_weight)
+
+    near, edges_top, send_down = side(0, "first")
+    far, edges_end, send_up = side(plane_rows - 3, "last")
 
     reach = range(slabs - SLABS)
     above = lax.ppermute(send_up, "rows", [(r, r + SLABS) for r in reach])
@@ -340,7 +336,7 @@
             brain(3 * chans, 3 * chans),
             brain(3 * chans, 3 * chans),
         ],
-        in_specs=[vmem] * 6,
+        in_specs=[vmem] * 7,
         out_specs=[vmem] * 6,
         scratch_shapes=[
             held(3, (inner + 2) * pitch, chans),
@@ -351,7 +347,7 @@
         compiler_params=params,
         cost_estimate=pl.CostEstimate(flops=10**9, bytes_accessed=4 * 10**6, transcendentals=10**5),
         name="inner",
-    )(masks, own, temporal_weight, t_edge, first_weight, second_weight)
+    )(masks, own, temporal_weight, near, far, first_weight, second_weight)
     o_end = pl.pallas_call(
         end_kernel,
         out_shape=brain(3, tm, width, chans),
@@ -360,7 +356,7 @@
         compiler_params=params,
         cost_estimate=pl.CostEstimate(flops=4 * 10**8, bytes_accessed=10**6, transcendentals=10**5),
         name="end",
-    )(shown, edges, known_h, known_o, below, w1, w2)
+    )(shown, edges_end, known_h, known_o, below, w1, w2)
     encoded = pl.pallas_call(
         top_kernel,
         out_shape=brain(SLABS, tm, row_count, width, chans),
@@ -368,7 +364,7 @@
         out_specs=vmem,
         compiler_params=params,
         name="top",
-    )(shown, edges, known_h, known_o, above, w1, w2, o_mid, o_end)
+    )(shown, edges_top, known_h, known_o, above, w1, w2, o_mid, o_end)
 
     groups = [[z * SLABS + j for j in range(SLABS)] for z in range(planes)]
     encoded = lax.all_to_all(

time: 47.4 us -> 47.8 us (level)
    pallas_call x1 -> x2, Pallas kernels: 1.03 us -> 1.23 us  [side(): pl.pallas_call(lambda *refs: side_kernel(at, *refs), out_shape=[brain(pit...]
  transfers between devices with their start and end apart: 2 -> 2, of which waited for: 1 -> 1; matrix products, arithmetic and copies ran while one was open for 0% -> 0% of each run, Pallas kernels for 6% -> 8%
where the time goes in v14:
time: 47.8 us; the launch traced here: 47.5 us
  blocking collectives  31.2 us (65%)
  starting transfers between devices  6.18 us (13%)
  Pallas kernels  4.99 us (10%)
  waiting for transfers between devices  3.13 us (7%)
  local copies, waits for them, and re-layouts  1.79 us (4%)
    all_to_all x1, blocking collectives, per_device(): lax.all_to_all(cut, ('tm', 'rows'), split_axis=0, concat_axis=0, tiled=Tr...  21.1 us
    all_to_all x1, blocking collectives, per_device(): lax.all_to_all(encoded, 'rows', split_axis=0, concat_axis=0, tiled=True,...  10.1 us
    ppermute x1, starting transfers between devices, per_device(): below = lax.ppermute(send_down, 'rows', [(r + SLABS, r) for r in reach])  4.26 us
    ppermute x1, waiting for transfers between devices, per_device(): above = lax.ppermute(send_up, 'rows', [(r, r + SLABS) for r in reach])  3.13 us
    pallas_call x1, Pallas kernels, per_device(): pl.pallas_call(inner_kernel, out_shape=[partial, partial, brain(inner - 2...  2.36 us
    ppermute x1, starting transfers between devices, per_device(): above = lax.ppermute(send_up, 'rows', [(r, r + SLABS) for r in reach])  1.92 us
    pallas_call x2, Pallas kernels, side(): pl.pallas_call(lambda *refs: side_kernel(at, *refs), out_shape=[brain(pit...  1.23 us
    unnamed x8, local copies, waits for them, and re-layouts  1.06 us
  transfers between devices with their start and end apart: 2, of which 1 were waited for; matrix products, arithmetic and copies ran while one was open for 0% of the time, Pallas kernels for 8%

profile of v14, /device:TPU:384, one launch (start us, length us, event | category | flops | bytes accessed | tf_op | source)
XLA Modules:
  0.0 47.5 jit_solution(546229617619505589)
XLA Ops:
  0.0 0.0 copy-start.1
  0.0 1.0 %copy-done.1 = bf16[2,2,512,128]{3,2,1,0:T(8,128)(2,1)S(1)} copy-done((bf16[2,2,512,128]{3,2,1,0:T(8,128)(2,1)S(1)}, bf16[2,2,512,128]{3,2,1,0:T(8,128)(2,1)}, u32[]{:S(2)}) %copy-start.1) | copy-done | bytes 524312
  1.1 0.2 windows.1
  1.3 0.0 copy-start
  1.3 0.1 and_convert_fusion.refs_0_.masks
  1.4 21.1 %all_to_all.10 = bf16[32,88,128]{2,1,0:T(8,128)(2,1)S(1)} all-to-all(bf16[32,88,128]{2,1,0:T(8,128)(2,1)S(1)} %windows.1), channel_id=1, replica_groups={{0,1,2,3,64,65,66,67,128,129,130,131,192,193,194,195,256,257,258,259,32..., dimensions={0} | all-to-all | bytes 1441792 | tf_op jit(solution)/shard_map/all_to_all | solution.py:300
  22.5 0.0 copy-done
  22.5 0.6 %first.1 = (bf16[192,128]{1,0:T(8,128)(2,1)S(1)}, f32[2,160,128]{2,1,0:T(8,128)S(1)}, bf16[3,160,128]{2,1,0:T(8,128)(2,1)S(1)}) custom-call(f32[3,24,128]{2,1,0:T(8,128)S(1)} %and_convert_fusion.refs_0_.masks, bf16[8,4,88,128]{3,2,1,0:T(8,128)(2,1)S(1)} %bitcast.3, bf16[3,3,3,128,128]{4,3,2,1,0:T(8,128)(2,1)S(1)} %copy-done), custom_call_target="tpu_custom_call" | custom-call | flops 400000000 | bytes 1000000 | tf_op jit(solution)/shard_map/first/pallas_call | solution.py:305
  23.1 0.0 copy-start.2
  23.1 0.0 copy-start.3
  23.1 4.3 %collective-permute-start.1 = (bf16[3,160,128]{2,1,0:T(8,128)(2,1)S(1)}, bf16[3,160,128]{2,1,0:T(8,128)(2,1)S(1)}, u32[]{:S(2)}, u32[]{:S(2)}) collective-permute-start(bf16[3,160,128]{2,1,0:T(8,128)(2,1)S(1)} %get-tuple-element.32), channel_id=1, source_target_pairs={{4,0},{5,1},{6,2},{7,3},{8,4},{9,5},{10,6},{11,7},{12,8},{13,9},{1... | collective-permute-start | bytes 368648 | tf_op jit(solution)/shard_map/ppermute | solution.py:325
  27.4 0.6 %last.1 = (bf16[192,128]{1,0:T(8,128)(2,1)S(1)}, f32[2,160,128]{2,1,0:T(8,128)S(1)}, bf16[3,160,128]{2,1,0:T(8,128)(2,1)S(1)}) custom-call(f32[3,24,128]{2,1,0:T(8,128)S(1)} %and_convert_fusion.refs_0_.masks, bf16[8,4,88,128]{3,2,1,0:T(8,128)(2,1)S(1)} %bitcast.4, bf16[3,3,3,128,128]{4,3,2,1,0:T(8,128)(2,1)S(1)} %copy-done), custom_call_target="tpu_custom_call" | custom-call | flops 400000000 | bytes 1000000 | tf_op jit(solution)/shard_map/last/pallas_call | solution.py:305
  28.0 1.9 %collective-permute-start = (bf16[3,160,128]{2,1,0:T(8,128)(2,1)S(1)}, bf16[3,160,128]{2,1,0:T(8,128)(2,1)S(1)}, u32[]{:S(2)}, u32[]{:S(2)}) collective-permute-start(bf16[3,160,128]{2,1,0:T(8,128)(2,1)S(1)} %get-tuple-element.27), channel_id=1, source_target_pairs={{0,4},{1,5},{2,6},{3,7},{4,8},{5,9},{6,10},{7,11},{8,12},{9,13},{1... | collective-permute-start | bytes 368648 | tf_op jit(solution)/shard_map/ppermute | solution.py:324
  30.0 0.0 copy-done.2
  30.0 0.0 copy-done.3
  30.0 2.4 %inner.1 = (f32[4,160,128]{2,1,0:T(8,128)S(1)}, f32[4,160,128]{2,1,0:T(8,128)S(1)}, bf16[2,8,16,128]{3,2,1,0:T(8,128)(2,1)S(1)}, f32[3,160,128]{2,1,0:T(8,128)S(...) custom-call(f32[3,24,128]{2,1,0:T(8,128)S(1)} %and_convert_fusion.refs_0_.masks, ...), custom_call_target="tpu_custom_call" | custom-call | flops 1000000000 | bytes 4000000 | tf_op jit(solution)/shard_map/inner/pallas_call | solution.py:329
  32.4 0.0 collective-permute-done.1.below
  32.4 0.6 %end.1.o_end = bf16[3,8,16,128]{3,2,1,0:T(8,128)(2,1)S(1)} custom-call(f32[3,160,128]{2,1,0:T(8,128)S(1)} %get-tuple-element.23.shown, f32[2,160,128]{2,1,0:T(8,128)S(1)} %get-tuple-element.31.edges, f32[4,160,128]{2,1,0:T(8,128)S(1)} %get-tuple-element.25.known_h, f32[4,160,128]{2,1,0:T(8,128)S(1)} %get-tuple-element.26.known_o, ...), custom_call_target="tpu_custom_call" | custom-call | flops 400000000 | bytes 1000000 | tf_op jit(solution)/shard_map/end/pallas_call | solution.py:351
  33.0 3.1 %collective-permute-done.above = bf16[3,160,128]{2,1,0:T(8,128)(2,1)S(1)} collective-permute-done((bf16[3,160,128]{2,1,0:T(8,128)(2,1)S(1)}, bf16[3,160,128]{2,1,0:T(8,128)(2,1)S(1)}, u32[]{:S(2)}, u32[]{:S(2)}) %collective-permute-start) | collective-permute-done | bytes 122912 | tf_op jit(solution)/shard_map/ppermute | solution.py:324
  36.1 0.6 %top.1 = bf16[4,8,2,16,128]{4,3,2,1,0:T(8,128)(2,1)S(1)} custom-call(f32[3,160,128]{2,1,0:T(8,128)S(1)} %get-tuple-element.23.shown, f32[2,160,128]{2,1,0:T(8,128)S(1)} %get-tuple-element.24.edges, f32[4,160,128]{2,1,0:T(8,128)S(1)} %get-tuple-element.25.known_h, f32[4,160,128]{2,1,0:T(8,128)S(1)} %get-tuple-element.26.known_o, ...), custom_call_target="tpu_custom_call" | custom-call | tf_op jit(solution)/shard_map/top/pallas_call | solution.py:360
  36.7 10.1 %all_to_all.11 = bf16[4,8,2,16,128]{4,3,2,1,0:T(8,128)(2,1)S(1)} all-to-all(bf16[4,8,2,16,128]{4,3,2,1,0:T(8,128)(2,1)S(1)} %top.1), channel_id=1, replica_groups={{0,1,2,3},{4,5,6,7},{8,9,10,11},{12,13,14,15},{16,17,18,19},{20,21,22,2..., dimensions={0} | all-to-all | bytes 524288 | tf_op jit(solution)/shard_map/all_to_all | solution.py:370
  46.8 0.7 %copy.5 = bf16[8,2,4,16,128]{4,3,2,1,0:T(8,128)(2,1)} copy(bf16[8,2,4,16,128]{4,3,1,0,2:T(8,128)(2,1)S(1)} %bitcast.6) | data formatting | bytes 524288 | tf_op jit(solution)/shard_map/transpose | solution.py:373
  (2 shorter events, 0.0 us)
Async XLA Ops:
  0.0 1.0 %copy-start.1 = (bf16[2,2,512,128]{3,2,1,0:T(8,128)(2,1)S(1)}, bf16[2,2,512,128]{3,2,1,0:T(8,128)(2,1)}, u32[]{:S(2)}) copy-start(bf16[2,2,512,128]{3,2,1,0:T(8,128)(2,1)} %frames.1) | copy-start | bytes 1572868
  1.3 21.2 %copy-start = (bf16[3,3,3,128,128]{4,3,2,1,0:T(8,128)(2,1)S(1)}, bf16[3,3,3,128,128]{4,3,2,1,0:T(8,128)(2,1)}, u32[]{:S(2)}) copy-start(bf16[3,3,3,128,128]{4,3,2,1,0:T(8,128)(2,1)} %weight.1) | copy-start | bytes 2654212
  23.1 6.8 %copy-start.2 = (bf16[3,3,128,128]{3,2,1,0:T(8,128)(2,1)S(1)}, bf16[3,3,128,128]{3,2,1,0:T(8,128)(2,1)}, u32[]{:S(2)}) copy-start(bf16[3,3,128,128]{3,2,1,0:T(8,128)(2,1)} %w_first.1) | copy-start | bytes 884740
  23.1 6.8 %copy-start.3 = (bf16[3,3,128,128]{3,2,1,0:T(8,128)(2,1)S(1)}, bf16[3,3,128,128]{3,2,1,0:T(8,128)(2,1)}, u32[]{:S(2)}) copy-start(bf16[3,3,128,128]{3,2,1,0:T(8,128)(2,1)} %w_second.1) | copy-start | bytes 884740
  23.1 9.2 %collective-permute-start.1 = (bf16[3,160,128]{2,1,0:T(8,128)(2,1)S(1)}, bf16[3,160,128]{2,1,0:T(8,128)(2,1)S(1)}, u32[]{:S(2)}, u32[]{:S(2)}) collective-permute-start(bf16[3,160,128]{2,1,0:T(8,128)(2,1)S(1)} %get-tuple-element.32), channel_id=1, source_target_pairs={{4,0},{5,1},{6,2},{7,3},{8,4},{9,5},{10,6},{11,7},{12,8},{13,9},{1... | collective-permute-start | bytes 368648 | tf_op jit(solution)/shard_map/ppermute | solution.py:325
  28.0 8.1 %collective-permute-start = (bf16[3,160,128]{2,1,0:T(8,128)(2,1)S(1)}, bf16[3,160,128]{2,1,0:T(8,128)(2,1)S(1)}, u32[]{:S(2)}, u32[]{:S(2)}) collective-permute-start(bf16[3,160,128]{2,1,0:T(8,128)(2,1)S(1)} %get-tuple-element.27), channel_id=1, source_target_pairs={{0,4},{1,5},{2,6},{3,7},{4,8},{5,9},{6,10},{7,11},{8,12},{9,13},{1... | collective-permute-start | bytes 368648 | tf_op jit(solution)/shard_map/ppermute | solution.py:324

commit v15 on v11

--- a/solution.py
+++ b/solution.py
@@ -182,18 +182,28 @@
     return split_rows(top, pitch) + split_rows(end, pitch)
 
 
+def pair_rows(pair, weight):
+    deep, chans = weight.shape[1], weight.shape[0] // 3
+    sums = jnp.dot(
+        jnp.concatenate(pair, axis=1),
+        jnp.concatenate([weight[chans:], weight[: 2 * chans]], axis=1),
+        preferred_element_type=jnp.float32,
+    )
+    return column_taps(sums[:, :deep]), column_taps(sums[:, deep:])
+
+
 def top_rows(rows, weight, known):
-    none, chans = jnp.zeros_like(rows[0]), rows[0].shape[1]
-    first = dot_taps([rows], weight[...])
-    near = split_rows(dot_taps([rows[1:], [rows[2], none]], weight[: 2 * chans]), none.shape[0])
-    return [first, near[0] + known[0], near[1] + known[1]]
+    pitch, chans = rows[0].shape
+    lower, upper = pair_rows(rows[1:], weight)
+    through = split_rows(dot_taps([[rows[0]], [rows[2]]], weight[:chans]), pitch)
+    return [lower + through[0], upper + known[0], through[1] + known[1]]
 
 
 def end_rows(rows, weight, known):
-    none, chans = jnp.zeros_like(rows[0]), rows[0].shape[1]
-    last = dot_taps([rows], weight[...])
-    far = split_rows(dot_taps([[none, rows[0]], rows[:2]], weight[chans:]), none.shape[0])
-    return [far[0] + known[2], far[1] + known[3], last]
+    pitch, chans = rows[0].shape
+    lower, upper = pair_rows(rows[:2], weight)
+    through = split_rows(dot_taps([[rows[0]], [rows[2]]], weight[2 * chans :]), pitch)
+    return [through[0] + known[2], lower + known[3], upper + through[1]]
 
 
 def inner_kernel(

time: 47.7 us -> 47.6 us (level)
  no operation moved by 1% of the time
where the time goes in v15:
time: 47.6 us; the launch traced here: 47.4 us
  blocking collectives  33.6 us (71%)
  Pallas kernels  5.52 us (12%)
  starting transfers between devices  5.42 us (11%)
  local copies, waits for them, and re-layouts  1.79 us (4%)
  waiting for transfers between devices  0.81 us (2%)
    all_to_all x1, blocking collectives, per_device(): lax.all_to_all(cut, ('tm', 'rows'), split_axis=0, concat_axis=0, tiled=Tr...  23.4 us
    all_to_all x1, blocking collectives, per_device(): lax.all_to_all(encoded, 'rows', split_axis=0, concat_axis=0, tiled=True,...  10.2 us
    ppermute x1, starting transfers between devices, per_device(): above = lax.ppermute(send_up, 'rows', [(r, r + SLABS) for r in reach])  3.99 us
    pallas_call x1, Pallas kernels, per_device(): pl.pallas_call(inner_kernel, out_shape=[partial, known, known, brain(inne...  2.87 us
    ppermute x1, starting transfers between devices, per_device(): below = lax.ppermute(send_down, 'rows', [(r + SLABS, r) for r in reach])  1.42 us
    pallas_call x1, Pallas kernels, per_device(): pl.pallas_call(end_kernel, out_shape=brain(3, tm, width, chans), in_specs...  1.19 us
    unnamed x8, local copies, waits for them, and re-layouts  1.06 us
  transfers between devices with their start and end apart: 2, of which 1 were waited for; matrix products, arithmetic and copies ran while one was open for 0% of the time, Pallas kernels for 10%

profile of v15, /device:TPU:1, one launch (start us, length us, event | category | flops | bytes accessed | tf_op | source)
XLA Modules:
  0.0 47.4 jit_solution(10054530276626256408)
XLA Ops:
  0.0 0.0 copy-start.1
  0.0 1.0 %copy-done.1 = bf16[2,2,512,128]{3,2,1,0:T(8,128)(2,1)S(1)} copy-done((bf16[2,2,512,128]{3,2,1,0:T(8,128)(2,1)S(1)}, bf16[2,2,512,128]{3,2,1,0:T(8,128)(2,1)}, u32[]{:S(2)}) %copy-start.1) | copy-done | bytes 524312
  1.0 0.2 windows.1
  1.3 0.1 and_convert_fusion.masks
  1.4 0.0 copy-start
  1.4 23.4 %all_to_all.10 = bf16[32,88,128]{2,1,0:T(8,128)(2,1)S(1)} all-to-all(bf16[32,88,128]{2,1,0:T(8,128)(2,1)S(1)} %windows.1), channel_id=1, replica_groups={{0,1,2,3,64,65,66,67,128,129,130,131,192,193,194,195,256,257,258,259,32..., dimensions={0} | all-to-all | bytes 1441792 | tf_op jit(solution)/shard_map/all_to_all | solution.py:338
  24.8 0.0 copy-start.2
  24.8 0.0 copy-start.3
  24.8 1.4 %collective-permute-start.1 = (bf16[8,132,128]{2,1,0:T(8,128)(2,1)S(1)}, bf16[8,132,128]{2,1,0:T(8,128)(2,1)S(1)}, u32[]{:S(2)}, u32[]{:S(2)}) collective-permute-start(bf16[8,132,128]{2,1,0:T(8,128)(2,1)S(1)} %down.1), channel_id=1, source_target_pairs={{4,0},{5,1},{6,2},{7,3},{8,4},{9,5},{10,6},{11,7},{12,8},{13,9},{1... | collective-permute-start | bytes 811016 | tf_op jit(solution)/shard_map/ppermute | solution.py:363
  26.3 0.0 copy-done
  26.3 0.6 %edge.1 = (bf16[192,128]{1,0:T(8,128)(2,1)S(1)}, f32[2,160,128]{2,1,0:T(8,128)S(1)}, bf16[3,160,128]{2,1,0:T(8,128)(2,1)S(1)}) custom-call(f32[3,24,128]{2,1,0:T(8,128)S(1)} %and_convert_fusion.masks, bf16[8,4,88,128]{3,2,1,0:T(8,128)(2,1)S(1)} %bitcast.4, bf16[3,3,3,128,128]{4,3,2,1,0:T(8,128)(2,1)S(1)} %copy-done), custom_call_target="tpu_custom_call" | custom-call | flops 400000000 | bytes 1000000 | tf_op jit(solution)/shard_map/edge/pallas_call | solution.py:352
  26.9 4.0 %collective-permute-start = (bf16[3,160,128]{2,1,0:T(8,128)(2,1)S(1)}, bf16[3,160,128]{2,1,0:T(8,128)(2,1)S(1)}, u32[]{:S(2)}, u32[]{:S(2)}) collective-permute-start(bf16[3,160,128]{2,1,0:T(8,128)(2,1)S(1)} %get-tuple-element.24), channel_id=1, source_target_pairs={{0,4},{1,5},{2,6},{3,7},{4,8},{5,9},{6,10},{7,11},{8,12},{9,13},{1... | collective-permute-start | bytes 368648 | tf_op jit(solution)/shard_map/ppermute | solution.py:362
  30.9 0.0 copy-done.2
  30.9 0.0 copy-done.3
  30.9 2.9 %inner.1 = (f32[2,160,128]{2,1,0:T(8,128)S(1)}, f32[4,160,128]{2,1,0:T(8,128)S(1)}, f32[4,160,128]{2,1,0:T(8,128)S(1)}, bf16[2,8,16,128]{3,2,1,0:T(8,128)(2,1)S(...) custom-call(f32[3,24,128]{2,1,0:T(8,128)S(1)} %and_convert_fusion.masks, ...), custom_call_target="tpu_custom_call" | custom-call | flops 1000000000 | bytes 4000000 | tf_op jit(solution)/shard_map/inner/pallas_call | solution.py:367
  33.8 0.8 %collective-permute-done.1.below = bf16[8,132,128]{2,1,0:T(8,128)(2,1)S(1)} collective-permute-done((bf16[8,132,128]{2,1,0:T(8,128)(2,1)S(1)}, bf16[8,132,128]{2,1,0:T(8,128)(2,1)S(1)}, u32[]{:S(2)}, u32[]{:S(2)}) %collective-permute-start.1) | collective-permute-done | bytes 270368 | tf_op jit(solution)/shard_map/ppermute | solution.py:363
  34.6 1.2 %end.1.o_end = bf16[3,8,16,128]{3,2,1,0:T(8,128)(2,1)S(1)} custom-call(f32[3,160,128]{2,1,0:T(8,128)S(1)} %get-tuple-element.20.shown, bf16[3,3,3,128,128]{4,3,2,1,0:T(8,128)(2,1)S(1)} %copy-done, f32[2,160,128]{2,1,0:T(8,128)S(1)} %get-tuple-element.28.edges, f32[4,160,128]{2,1,0:T(8,128)S(1)} %get-tuple-element.22.known_h, ...), custom_call_target="tpu_custom_call" | custom-call | flops 400000000 | bytes 1000000 | tf_op jit(solution)/shard_map/end/pallas_call | solution.py:390
  35.8 0.0 collective-permute-done.above
  35.8 0.6 %top.1 = bf16[4,8,2,16,128]{4,3,2,1,0:T(8,128)(2,1)S(1)} custom-call(f32[3,160,128]{2,1,0:T(8,128)S(1)} %get-tuple-element.20.shown, f32[2,160,128]{2,1,0:T(8,128)S(1)} %get-tuple-element.21.edges, f32[4,160,128]{2,1,0:T(8,128)S(1)} %get-tuple-element.22.known_h, f32[4,160,128]{2,1,0:T(8,128)S(1)} %get-tuple-element.23.known_o, ...), custom_call_target="tpu_custom_call" | custom-call | tf_op jit(solution)/shard_map/top/pallas_call | solution.py:400
  36.4 10.2 %all_to_all.11 = bf16[4,8,2,16,128]{4,3,2,1,0:T(8,128)(2,1)S(1)} all-to-all(bf16[4,8,2,16,128]{4,3,2,1,0:T(8,128)(2,1)S(1)} %top.1), channel_id=1, replica_groups={{0,1,2,3},{4,5,6,7},{8,9,10,11},{12,13,14,15},{16,17,18,19},{20,21,22,2..., dimensions={0} | all-to-all | bytes 524288 | tf_op jit(solution)/shard_map/all_to_all | solution.py:410
  46.6 0.7 %copy.5 = bf16[8,2,4,16,128]{4,3,2,1,0:T(8,128)(2,1)} copy(bf16[8,2,4,16,128]{4,3,1,0,2:T(8,128)(2,1)S(1)} %bitcast.6) | data formatting | bytes 524288 | tf_op jit(solution)/shard_map/transpose | solution.py:413
  (3 shorter events, 0.1 us)
Async XLA Ops:
  0.0 1.0 %copy-start.1 = (bf16[2,2,512,128]{3,2,1,0:T(8,128)(2,1)S(1)}, bf16[2,2,512,128]{3,2,1,0:T(8,128)(2,1)}, u32[]{:S(2)}) copy-start(bf16[2,2,512,128]{3,2,1,0:T(8,128)(2,1)} %frames.1) | copy-start | bytes 1572868
  1.4 24.9 %copy-start = (bf16[3,3,3,128,128]{4,3,2,1,0:T(8,128)(2,1)S(1)}, bf16[3,3,3,128,128]{4,3,2,1,0:T(8,128)(2,1)}, u32[]{:S(2)}) copy-start(bf16[3,3,3,128,128]{4,3,2,1,0:T(8,128)(2,1)} %weight.5) | copy-start | bytes 2654212
  24.8 6.1 %copy-start.2 = (bf16[3,3,128,128]{3,2,1,0:T(8,128)(2,1)S(1)}, bf16[3,3,128,128]{3,2,1,0:T(8,128)(2,1)}, u32[]{:S(2)}) copy-start(bf16[3,3,128,128]{3,2,1,0:T(8,128)(2,1)} %w_first.1) | copy-start | bytes 884740
  24.8 6.1 %copy-start.3 = (bf16[3,3,128,128]{3,2,1,0:T(8,128)(2,1)S(1)}, bf16[3,3,128,128]{3,2,1,0:T(8,128)(2,1)}, u32[]{:S(2)}) copy-start(bf16[3,3,128,128]{3,2,1,0:T(8,128)(2,1)} %w_second.1) | copy-start | bytes 884740
  24.8 9.8 %collective-permute-start.1 = (bf16[8,132,128]{2,1,0:T(8,128)(2,1)S(1)}, bf16[8,132,128]{2,1,0:T(8,128)(2,1)S(1)}, u32[]{:S(2)}, u32[]{:S(2)}) collective-permute-start(bf16[8,132,128]{2,1,0:T(8,128)(2,1)S(1)} %down.1), channel_id=1, source_target_pairs={{4,0},{5,1},{6,2},{7,3},{8,4},{9,5},{10,6},{11,7},{12,8},{13,9},{1... | collective-permute-start | bytes 811016 | tf_op jit(solution)/shard_map/ppermute | solution.py:363
  26.9 8.9 %collective-permute-start = (bf16[3,160,128]{2,1,0:T(8,128)(2,1)S(1)}, bf16[3,160,128]{2,1,0:T(8,128)(2,1)S(1)}, u32[]{:S(2)}, u32[]{:S(2)}) collective-permute-start(bf16[3,160,128]{2,1,0:T(8,128)(2,1)S(1)} %get-tuple-element.24), channel_id=1, source_target_pairs={{0,4},{1,5},{2,6},{3,7},{4,8},{5,9},{6,10},{7,11},{8,12},{9,13},{1... | collective-permute-start | bytes 368648 | tf_op jit(solution)/shard_map/ppermute | solution.py:362
